TPU v7x, 32 devices: a whole 2x2x4 slice. The times are simulated.
32 devices in a mesh: section: 2 (over core), dp: 16 (over z, y, x).
Axes of the slice: x: 2, y: 2, z: 4, core: 2. Of those that a mesh axis runs over, the one named last changes fastest.
Arguments:
- clip_input: bfloat16 [32, 16, 14, 14, 832], P('dp', 'section'), may hold values from -30 to 30
- out_grad: bfloat16 [32, 8, 7, 7, 832], P('dp', 'section'), may hold values from -6 to 6
- clip_lengths: int32 [32, 2], P('dp'), may hold values from 2 to 8, as said below
- w_one: bfloat16 [2, 832, 256], P('section'), may hold values from -0.21875 to 0.21875
- w_mid_in: bfloat16 [2, 832, 160], P('section'), may hold values from -0.21875 to 0.21875
- w_mid: bfloat16 [2, 4320, 320], P('section'), may hold values from -0.09375 to 0.09375
- w_small_in: bfloat16 [2, 832, 32], P('section'), may hold values from -0.21875 to 0.21875
- w_small: bfloat16 [2, 864, 128], P('section'), may hold values from -0.21875 to 0.21875
- w_pool: bfloat16 [2, 832, 128], P('section'), may hold values from -0.21875 to 0.21875
- bn_offset: float32 [2, 1024], P('section'), may hold values from -3 to 3
Outputs:
- block_output: bfloat16 [32, 8, 7, 7, 832], P('dp', 'section')
- input_grad: bfloat16 [32, 16, 14, 14, 832], P('dp', 'section')
- w_one_grad: float32 [2, 832, 256], P('section')
- w_mid_in_grad: float32 [2, 832, 160], P('section')
- w_mid_grad: float32 [2, 4320, 320], P('section')
- w_small_in_grad: float32 [2, 832, 32], P('section')
- w_small_grad: float32 [2, 864, 128], P('section')
- w_pool_grad: float32 [2, 832, 128], P('section')
- bn_offset_grad: float32 [2, 1024], P('section')
Inputs may be any that keep to these rules, and one draw needn't show every extreme that they name: `clip_lengths`: every entry is even; the clips of a slot take at most 16 frames together, the rest of the slot is padding; in some slot the last clip has 8 frames.
All inputs are finite; a program needn't handle non-finite values.
Results may differ from a plain program's by a relative error of at most 0.019.
Values may be sent and summed in bfloat16 or wider, within the bound.
A program may use at most 512 MiB of HBM per device.

v0:
```python
import jax
import jax.numpy as jnp
from jax import lax
from jax.sharding import PartitionSpec as P

D = 832
C0 = 256
C1A = 160
C1B = 320
C2A = 32
C2B = 128
MICRO = 2
SLOT_MB = 1


EPS = 0.001
TAP_LIST = [
    (shift_t, shift_y, shift_x)
    for shift_t in (-1, 0, 1)
    for shift_y in (-1, 0, 1)
    for shift_x in (-1, 0, 1)
]


def shifted_2(x, axis, by):
    size = lax.axis_size(axis)
    pairs = [(i, i + by) for i in range(size) if 0 <= i + by < size]
    return lax.ppermute(x, axis, pairs)


def shift_frames(table, shift_t):
    padded = jnp.pad(table, ((0, 0), (1, 1)))
    return lax.slice_in_dim(padded, 1 + shift_t, 1 + shift_t + table.shape[1], axis=1)


def frame_masks(lengths, frame_total, stride):
    starts = jnp.cumsum(lengths, axis=1, dtype=jnp.int32) - lengths
    places = (jnp.arange(frame_total, dtype=jnp.int32) * stride)[None, None, :]
    inside = (places >= starts[:, :, None]) & (places < (starts + lengths)[:, :, None])
    validity = jnp.any(inside, axis=1).astype(jnp.float32)
    numbers = (jnp.arange(lengths.shape[1], dtype=jnp.int32) + 1)[None, :, None]
    labels = jnp.sum(inside.astype(jnp.int32) * numbers, axis=1, dtype=jnp.int32)
    masks_list = []
    for shift_t in (-1, 0, 1):
        matched = (labels == shift_frames(labels, shift_t)).astype(jnp.float32)
        masks_list.append(validity * shift_frames(validity, shift_t) * matched)
    return (validity, jnp.stack(masks_list))


def shift_grid(volume, shift_t, shift_y, shift_x):
    padded = jnp.pad(volume, ((0, 0), (1, 1), (1, 1), (1, 1), (0, 0)))
    frame_count, rows_y, rows_x = (volume.shape[1], volume.shape[2], volume.shape[3])
    return padded[
        :,
        1 + shift_t : 1 + shift_t + frame_count,
        1 + shift_y : 1 + shift_y + rows_y,
        1 + shift_x : 1 + shift_x + rows_x,
        :,
    ]


def box_sum(volume, tap_masks):
    temporal = jnp.zeros_like(volume)
    for shift_t in (-1, 0, 1):
        temporal = (
            temporal
            + shift_grid(volume, shift_t, 0, 0) * tap_masks[shift_t + 1][:, :, None, None, None]
        )
    rows_sum = shift_grid(temporal, 0, -1, 0) + temporal + shift_grid(temporal, 0, 1, 0)
    return shift_grid(rows_sum, 0, 0, -1) + rows_sum + shift_grid(rows_sum, 0, 0, 1)


def pool_counts(tap_masks, frame_side):
    spread = jnp.sum(tap_masks, axis=0)
    places = jnp.arange(frame_side, dtype=jnp.int32)
    edges = 3.0 - (places == 0).astype(jnp.float32) - (places == frame_side - 1).astype(jnp.float32)
    counts = spread[:, :, None, None, None] * edges[:, None, None] * edges[None, :, None]
    return jnp.maximum(counts, 1.0)


def pool_input(source, tap_masks, frame_side):
    summed = box_sum(source.astype(jnp.float32), tap_masks)
    return (summed / pool_counts(tap_masks, frame_side)).astype(jnp.bfloat16)


def pool_pairs(volume):
    slot_count, frame_count, rows_y, rows_x, channel_count = volume.shape
    blocks = volume.reshape(
        slot_count, frame_count // 2, 2, rows_y // 2, 2, rows_x // 2, 2, channel_count
    )
    return jnp.mean(blocks, axis=(2, 4, 6))


def spread_pairs(grads):
    slot_count, frame_count, rows_y, rows_x, channel_count = grads.shape
    expanded = jnp.broadcast_to(
        grads[:, :, None, :, None, :, None, :] / 8.0,
        (slot_count, frame_count, 2, rows_y, 2, rows_x, 2, channel_count),
    )
    return expanded.reshape(slot_count, frame_count * 2, rows_y * 2, rows_x * 2, channel_count)


def gather_taps(volume, tap_masks):
    padded = jnp.pad(volume, ((0, 0), (1, 1), (1, 1), (1, 1), (0, 0)))
    frame_count, rows_y, rows_x = (volume.shape[1], volume.shape[2], volume.shape[3])
    pieces = []
    for shift_t, shift_y, shift_x in TAP_LIST:
        window = padded[
            :,
            1 + shift_t : 1 + shift_t + frame_count,
            1 + shift_y : 1 + shift_y + rows_y,
            1 + shift_x : 1 + shift_x + rows_x,
            :,
        ]
        pieces.append(window * tap_masks[shift_t + 1][:, :, None, None, None].astype(volume.dtype))
    return jnp.concatenate(pieces, axis=-1)


def scatter_taps(columns, tap_masks, channel_count):
    summed = jnp.zeros(columns.shape[:-1] + (channel_count,), jnp.float32)
    for position, (shift_t, shift_y, shift_x) in enumerate(TAP_LIST):
        shifted = columns[..., position * channel_count : (position + 1) * channel_count]
        shifted = shifted * tap_masks[shift_t + 1][:, :, None, None, None]
        summed = summed + shift_grid(shifted, -shift_t, -shift_y, -shift_x)
    return summed


def moments(values, valid_rows):
    masked = values * valid_rows
    return (jnp.sum(masked, axis=0), jnp.sum(masked * values, axis=0), jnp.sum(valid_rows))


def normalize(values, stats):
    totals, squares, voxel_count = stats
    center = totals / voxel_count
    factor = lax.rsqrt(squares / voxel_count - center * center + EPS)
    return ((values - center) * factor, factor)


def widen(rows, rows_total):
    return jnp.pad(rows, ((0, rows_total - rows.shape[0]), (0, 0)))


def make_branch(number, active, core, rows_total):

    def real_branch(operand):
        row_items, minor = core(number, operand)
        return (tuple((widen(row_item, rows_total) for row_item in row_items)), minor)

    def empty_branch(operand):
        return jax.tree.map(jnp.zeros_like, real_branch(operand))

    return real_branch if active else empty_branch


def sectioned(core, operand, active, rows_total):
    return lax.cond(
        lax.axis_index("section") == 0,
        make_branch(0, active[0], core, rows_total),
        make_branch(1, active[1], core, rows_total),
        operand,
    )


def reduce_norms(partials):
    return lax.psum(partials, "dp")


def reduce_grads(partials):
    return lax.psum(partials, "dp")


def micro_slice(array, micro_index):
    return lax.slice_in_dim(array, micro_index * SLOT_MB, (micro_index + 1) * SLOT_MB, axis=0)


def dot_rows(values, weight):
    return jnp.dot(values, weight, preferred_element_type=jnp.float32)


def dot_back(grads, weight):
    return jnp.einsum("vo,io->vi", grads, weight, preferred_element_type=jnp.float32)


def dot_weight(values, grads):
    return jnp.einsum("vi,vo->io", values, grads, preferred_element_type=jnp.float32)


def on_device(
    clip_input,
    out_grad,
    clip_lengths,
    w_one,
    w_mid_in,
    w_mid,
    w_small_in,
    w_small,
    w_pool,
    bn_offset,
):
    full_input, full_grad = (
        lax.all_gather(clip_input, "section", axis=1, tiled=True),
        lax.all_gather(out_grad, "section", axis=1, tiled=True),
    )
    frame_total = full_input.shape[1]
    frame_side = full_input.shape[2]
    rows_total = SLOT_MB * frame_total * frame_side * frame_side
    input_proj = jnp.concatenate([w_one[0], w_mid_in[0], w_small_in[0]], axis=1)
    mid_weight = w_mid[0]
    small_weight = w_small[0]
    pool_weight = w_pool[0]
    offsets = bn_offset[0]
    mid_from = C0
    small_from = C0 + C1A
    pool_from = C0 + C1A + C2A
    off_mid = C0 + C1A
    off_small_in = off_mid + C1B
    off_small = off_small_in + C2A
    off_pool = off_small + C2B
    beta_first = jnp.concatenate(
        [offsets[:off_mid], offsets[off_small_in:off_small], offsets[off_pool:]]
    )
    beta_second = jnp.concatenate([offsets[off_mid:off_small_in], offsets[off_small:off_pool]])

    def final_of(first_part, second_part):
        return jnp.concatenate(
            [first_part[..., :C0], second_part, first_part[..., pool_from:]], axis=-1
        )

    def inner_of(first_part):
        return first_part[..., mid_from:pool_from]

    beta_final = final_of(beta_first, beta_second)
    beta_inner = inner_of(beta_first)

    def prepare(number, operand):
        if number == 0:
            source, lengths, frames_here, side_here, stride = (
                operand[0],
                operand[2],
                frame_total,
                frame_side,
                1,
            )
        else:
            source, lengths, frames_here, side_here, stride = (
                operand[1],
                operand[3],
                frame_total // 2,
                frame_side // 2,
                2,
            )
        validity, tap_masks = frame_masks(lengths, frames_here, stride)
        valid_rows = jnp.broadcast_to(
            validity[:, :, None, None], validity.shape + (side_here, side_here)
        ).reshape(-1, 1)
        return (source, tap_masks, valid_rows, side_here)

    def conv_inputs(acts_first, grid_shape):
        mid_in = (
            acts_first[:, mid_from:small_from].astype(jnp.bfloat16).reshape(grid_shape + (C1A,))
        )
        small_in = (
            acts_first[:, small_from:pool_from].astype(jnp.bfloat16).reshape(grid_shape + (C2A,))
        )
        return (mid_in, small_in)

    def core_first(number, operand):
        source, tap_masks, valid_rows, side_here = prepare(number, operand)
        flat = source.reshape(-1, D)
        pooled = pool_input(source, tap_masks, side_here).reshape(-1, D)
        z_first = jnp.concatenate(
            [dot_rows(flat, input_proj), dot_rows(pooled, pool_weight)], axis=1
        )
        return ((z_first,), moments(z_first, valid_rows))

    def core_second(number, operand):
        source, tap_masks, valid_rows, side_here = prepare(number, operand)
        rows_here = valid_rows.shape[0]
        u_first, scale_first = normalize(operand[4][:rows_here], operand[5])
        acts_first = jax.nn.softplus(u_first + beta_first) * valid_rows
        mid_in, small_in = conv_inputs(acts_first, source.shape[:4])
        z_second = jnp.concatenate(
            [
                dot_rows(gather_taps(mid_in, tap_masks).reshape(rows_here, -1), mid_weight),
                dot_rows(gather_taps(small_in, tap_masks).reshape(rows_here, -1), small_weight),
            ],
            axis=1,
        )
        return ((z_second,), moments(z_second, valid_rows))

    def states(number, operand):
        source, tap_masks, valid_rows, side_here = prepare(number, operand)
        rows_here = valid_rows.shape[0]
        u_first, scale_first = normalize(operand[4][:rows_here], operand[6])
        u_second, scale_second = normalize(operand[5][:rows_here], operand[7])
        return (
            source,
            tap_masks,
            valid_rows,
            side_here,
            u_first,
            scale_first,
            u_second,
            scale_second,
        )

    def core_output(number, operand):
        source, tap_masks, valid_rows, side_here, u_first, scale_first, u_second, scale_second = (
            states(number, operand)
        )
        acts_first = jax.nn.softplus(u_first + beta_first) * valid_rows
        acts_second = jax.nn.softplus(u_second + beta_second) * valid_rows
        joined = final_of(acts_first, acts_second).reshape(source.shape[:4] + (D,))
        emitted = pool_pairs(joined) if number == 0 else joined
        return ((), (emitted.astype(jnp.bfloat16),))

    def core_upstream(number, operand):
        source, tap_masks, valid_rows, side_here, u_first, scale_first, u_second, scale_second = (
            states(number, operand)
        )
        if number == 0:
            incoming = spread_pairs(operand[8].astype(jnp.float32)).reshape(-1, D)
        else:
            incoming = operand[9].astype(jnp.float32).reshape(-1, D)
        u_final = final_of(u_first, u_second)
        upstream = incoming * jax.nn.sigmoid(u_final + beta_final) * valid_rows
        return ((upstream,), (jnp.sum(upstream, axis=0), jnp.sum(upstream * u_final, axis=0)))

    def core_middle(number, operand):
        source, tap_masks, valid_rows, side_here, u_first, scale_first, u_second, scale_second = (
            states(number, operand)
        )
        rows_here = valid_rows.shape[0]
        grid_shape = source.shape[:4]
        upstream = operand[10][:rows_here]
        total_up, total_cross = operand[11]
        voxel_count = operand[6][2]
        u_final = final_of(u_first, u_second)
        scale_final = final_of(scale_first, scale_second)
        dz_final = (
            scale_final
            * (upstream - total_up / voxel_count - u_final * (total_cross / voxel_count))
            * valid_rows
        ).astype(jnp.bfloat16)
        dz_zero = dz_final[:, :C0]
        dz_mid = dz_final[:, C0 : C0 + C1B]
        dz_small = dz_final[:, C0 + C1B : C0 + C1B + C2B]
        dz_pool = dz_final[:, C0 + C1B + C2B :]
        acts_first = jax.nn.softplus(u_first + beta_first) * valid_rows
        mid_in, small_in = conv_inputs(acts_first, grid_shape)
        grad_mid = dot_weight(gather_taps(mid_in, tap_masks).reshape(rows_here, -1), dz_mid)
        back_mid = scatter_taps(
            dot_back(dz_mid, mid_weight).reshape(grid_shape + (mid_weight.shape[0],)),
            tap_masks,
            C1A,
        ).reshape(rows_here, C1A)
        grad_small = dot_weight(gather_taps(small_in, tap_masks).reshape(rows_here, -1), dz_small)
        back_small = scatter_taps(
            dot_back(dz_small, small_weight).reshape(grid_shape + (small_weight.shape[0],)),
            tap_masks,
            C2A,
        ).reshape(rows_here, C2A)
        flat = source.reshape(-1, D)
        grad_one = dot_weight(flat, dz_zero)
        pooled = pool_input(source, tap_masks, side_here).reshape(-1, D)
        grad_pool = dot_weight(pooled, dz_pool)
        u_inner = inner_of(u_first)
        upstream_inner = (
            jnp.concatenate([back_mid, back_small], axis=1)
            * jax.nn.sigmoid(u_inner + beta_inner)
            * valid_rows
        )
        return (
            (dz_zero, dz_pool, upstream_inner),
            (
                (grad_one, grad_mid, grad_small, grad_pool),
                (jnp.sum(upstream_inner, axis=0), jnp.sum(upstream_inner * u_inner, axis=0)),
            ),
        )

    def core_input(number, operand):
        source, tap_masks, valid_rows, side_here, u_first, scale_first, u_second, scale_second = (
            states(number, operand)
        )
        rows_here = valid_rows.shape[0]
        grid_shape = source.shape[:4]
        voxel_count = operand[6][2]
        dz_zero = operand[12][:rows_here]
        dz_pool = operand[13][:rows_here]
        upstream_inner = operand[14][:rows_here]
        total_up, total_cross = operand[15]
        u_inner = inner_of(u_first)
        dz_inner = (
            inner_of(scale_first)
            * (upstream_inner - total_up / voxel_count - u_inner * (total_cross / voxel_count))
            * valid_rows
        ).astype(jnp.bfloat16)
        flat = source.reshape(-1, D)
        grad_mid_in = dot_weight(flat, dz_inner[:, :C1A])
        grad_small_in = dot_weight(flat, dz_inner[:, C1A:])
        back_rows = dot_back(jnp.concatenate([dz_zero, dz_inner], axis=1), input_proj)
        pool_back = dot_back(dz_pool, pool_weight).reshape(grid_shape + (D,)) / pool_counts(
            tap_masks, side_here
        )
        back_rows = back_rows + box_sum(pool_back, tap_masks).reshape(-1, D)
        return ((back_rows.astype(jnp.bfloat16),), (grad_mid_in, grad_small_in))

    def operands_for(tick_index, received):
        first_index = min(tick_index, MICRO - 1)
        second_index = max(tick_index - 1, 0)
        return (
            micro_slice(full_input, first_index),
            received,
            micro_slice(clip_lengths, first_index),
            micro_slice(clip_lengths, second_index),
        )

    zero_grid = jnp.zeros_like(micro_slice(full_grad, 0))
    received = zero_grid
    kept_inputs, kept_first, kept_second, outputs_list = ([], [], [], [])
    for tick_index in range(MICRO + 1):
        active = (tick_index < MICRO, tick_index >= 1)
        base_ops = operands_for(tick_index, received)
        first_rows, partials = sectioned(core_first, base_ops, active, rows_total)
        stats_first = reduce_norms(partials)
        second_rows, partials = sectioned(
            core_second, base_ops + (first_rows[0], stats_first), active, rows_total
        )
        stats_second = reduce_norms(partials)
        results = sectioned(
            core_output,
            base_ops + (first_rows[0], second_rows[0], stats_first, stats_second),
            active,
            rows_total,
        )
        emitted = results[1][0]
        kept_inputs.append(received)
        kept_first.append(stats_first)
        kept_second.append(stats_second)
        if tick_index >= 1:
            outputs_list.append(emitted)
        if tick_index < MICRO:
            received = shifted_2(emitted, "section", 1)
    grad_one = jnp.zeros(w_one.shape[1:], jnp.float32)
    grad_mid_in = jnp.zeros(w_mid_in.shape[1:], jnp.float32)
    grad_mid = jnp.zeros(w_mid.shape[1:], jnp.float32)
    grad_small_in = jnp.zeros(w_small_in.shape[1:], jnp.float32)
    grad_small = jnp.zeros(w_small.shape[1:], jnp.float32)
    grad_pool = jnp.zeros(w_pool.shape[1:], jnp.float32)
    offset_grad = jnp.zeros(offsets.shape, jnp.float32)
    grad_received = zero_grid
    input_list = [None] * MICRO
    rows_second = rows_total // 8
    for back_step in range(MICRO + 1):
        tick_index = MICRO - back_step
        active = (tick_index < MICRO, tick_index >= 1)
        base_ops = operands_for(tick_index, kept_inputs[tick_index])
        first_rows, partials = sectioned(core_first, base_ops, active, rows_total)
        stats_first = reduce_norms(partials)
        second_rows, partials = sectioned(
            core_second, base_ops + (first_rows[0], stats_first), active, rows_total
        )
        stats_second = reduce_norms(partials)
        grad_local = micro_slice(full_grad, max(tick_index - 1, 0))
        operand_all = base_ops + (
            first_rows[0],
            second_rows[0],
            stats_first,
            stats_second,
            grad_received,
            grad_local,
        )
        upstream_rows, partials = sectioned(core_upstream, operand_all, active, rows_total)
        final_sums = reduce_grads(partials)
        operand_all = operand_all + (upstream_rows[0], final_sums)
        middle_rows, middle_minor = sectioned(core_middle, operand_all, active, rows_total)
        inner_sums = reduce_grads(middle_minor[1])
        grad_one = grad_one + middle_minor[0][0]
        grad_mid = grad_mid + middle_minor[0][1]
        grad_small = grad_small + middle_minor[0][2]
        grad_pool = grad_pool + middle_minor[0][3]
        operand_all = operand_all + (middle_rows[0], middle_rows[1], middle_rows[2], inner_sums)
        input_rows, input_minor = sectioned(core_input, operand_all, active, rows_total)
        grad_mid_in = grad_mid_in + input_minor[0]
        grad_small_in = grad_small_in + input_minor[1]
        final_total = final_sums[0]
        inner_total = inner_sums[0]
        offset_grad = offset_grad + jnp.concatenate(
            [
                final_total[:C0],
                inner_total[:C1A],
                final_total[C0 : C0 + C1B],
                inner_total[C1A:],
                final_total[C0 + C1B : C0 + C1B + C2B],
                final_total[C0 + C1B + C2B :],
            ]
        )
        if tick_index < MICRO:
            input_list[tick_index] = (
                input_rows[0]
                .reshape(full_input.shape[1:])
                .reshape((SLOT_MB,) + full_input.shape[1:])
            )
        if back_step < MICRO:
            handoff_grad = input_rows[0][:rows_second].reshape(zero_grid.shape)
            grad_received = shifted_2(handoff_grad, "section", -1)
    grad_one, grad_mid_in, grad_mid, grad_small_in, grad_small, grad_pool = lax.psum(
        (grad_one, grad_mid_in, grad_mid, grad_small_in, grad_small, grad_pool), "dp"
    )
    on_first = lax.axis_index("section") == 0
    output_full = jnp.concatenate(outputs_list, axis=0)
    quarter_frames = output_full.shape[1] // 2
    output_moved = shifted_2(output_full[:, :quarter_frames], "section", -1)
    block_output = jnp.where(on_first, output_moved, output_full[:, quarter_frames:])
    input_full = jnp.concatenate(input_list, axis=0)
    half_frames = frame_total // 2
    input_moved = shifted_2(input_full[:, half_frames:], "section", 1)
    input_grad = jnp.where(on_first, input_full[:, :half_frames], input_moved)
    return (
        block_output,
        input_grad,
        grad_one[None],
        grad_mid_in[None],
        grad_mid[None],
        grad_small_in[None],
        grad_small[None],
        grad_pool[None],
        offset_grad[None],
    )


def solution(mesh):
    placed = (
        P("dp", "section", None, None, None),
        P("dp", "section", None, None, None),
        P("dp", None),
        P("section", None, None),
        P("section", None, None),
        P("section", None, None),
        P("section", None, None),
        P("section", None, None),
        P("section", None, None),
        P("section", None),
    )
    return jax.shard_map(
        on_device,
        mesh=mesh,
        in_specs=placed,
        out_specs=(
            P("dp", "section", None, None, None),
            P("dp", "section", None, None, None),
            P("section", None, None),
            P("section", None, None),
            P("section", None, None),
            P("section", None, None),
            P("section", None, None),
            P("section", None, None),
            P("section", None),
        ),
        check_vma=False,
    )
```

profile of v0, /device:TPU:0, one launch (start us, length us, event | category | flops | bytes accessed | tf_op | source)
XLA Modules:
  0.0 4690.2 jit_solution(6298964113078753391)
XLA Ops:
  50.5 69.8 %conditional.26 = (f32[3136,576]{0,1:T(8,128)}, f32[576]{0:T(1024)S(1)}, f32[576]{0:T(1024)S(1)}, f32[]{:T(128)}) conditional(s32[]{:T(128)} %convert_element_type.2639, () %tuple.195, (bf16[1,16,14,14,832]{4,3,2,1,0:T(8,128)(2,1)}, bf16[832,448]{1,0:T(8,128)(2,1)}, s32[1,2]{1,0:T(1,128)S(1)}, bf16[832,128]{1,0:T(8,128)(2,1)}) %tuple.1412), branch_computations={%region_0.0_spmd, %region_1.8_spmd} | conditional | flops 3046093824 | bytes 133556576 | solution.py:157
  120.3 44.1 all-reduce.337
  164.4 366.1 %conditional.27 = (f32[3136,448]{0,1:T(8,128)}, f32[448]{0:T(512)S(1)}, f32[448]{0:T(512)S(1)}, f32[]{:T(128)}) conditional(s32[]{:T(128)} %convert_element_type.2639, () %tuple.197, (f32[]{:T(128)}, f32[576]{0:T(1024)}, f32[3136,576]{0,1:T(8,128)}, f32[576]{0:T(1024)}, f32[576]{0:T(1024)S(1)}, /*index=5*/s32[1,2]{1,0:T(1,128)}, ...), branch_computations={%region_11.12_spmd, %region_12.0_spmd} | conditional | flops 9440318464 | bytes 261257632 | solution.py:157
  343.5 55.1 %concatenate.370 = bf16[3136,4320]{1,0:T(8,128)(2,1)} concatenate(bf16[3136,160]{1,0:T(8,128)(2,1)} %concatenate.341, bf16[3136,160]{1,0:T(8,128)(2,1)} %concatenate.343, bf16[3136,160]{1,0:T(8,128)(2,1)} %concatenate.345, bf16[3136,160]{1,0:T(8,128)(2,1)} %concatenate.347, bf16[3136,160]{1,0:T(8,128)(2,1)} %concatenate.348, bf16[3136,160]{1,0:T(8,128)(2,1)} %concatenate.349, ...), dimensions={1} | concatenate | bytes 54190080 | tf_op jit(solution)/shard_map/cond/branch_1_fun/concatenate | solution.py:116
  568.7 79.7 %conditional.28 = (bf16[1,8,7,7,832]{4,3,2,1,0:T(8,128)(2,1)}) conditional(s32[]{:T(128)} %convert_element_type.2639, () %tuple.194, (f32[]{:T(128)}, f32[576]{0:T(1024)}, f32[3136,576]{0,1:T(8,128)}, f32[576]{0:T(1024)}, f32[576]{0:T(1024)S(1)}, /*index=5*/s32[1,2]{1,0:T(1,128)}, f32[]{:T(128)}, f32[448]{0:T(512)}, f32[3136,448]{0,1:T(8,128)}, ...), branch_computations={%region_22.23_spmd, %region_23.27_spmd} | conditional | flops 40271492 | bytes 135832160 | solution.py:157
  654.9 80.0 %conditional.29 = (f32[3136,576]{1,0:T(8,128)}, f32[576]{0:T(1024)S(1)}, f32[576]{0:T(1024)S(1)}, f32[]{:T(128)}) conditional(s32[]{:T(128)} %convert_element_type.2639, (bf16[1,8,7,7,832]{4,1,3,2,0:T(8,128)(2,1)}, bf16[832,448]{1,0:T(8,128)(2,1)}, s32[1,2]{1,0:T(1,128)S(1)}, bf16[832,128]{1,0:T(8,128)(2,1)}) %tuple.1463, ...), branch_computations={%region_27.34_spmd, %region_34.41_spmd} | conditional | flops 3046093824 | bytes 148007072 | solution.py:157
  735.5 40.2 all-reduce.335
  775.7 368.1 %conditional.30 = (f32[3136,448]{1,0:T(8,128)}, f32[448]{0:T(512)}, f32[448]{0:T(512)}, f32[]{:T(128)}) conditional(s32[]{:T(128)} %convert_element_type.2639, (f32[3136,576]{1,0:T(8,128)}, f32[]{:T(128)}, f32[576]{0:T(1024)S(1)}, f32[576]{0:T(1024)S(1)}, f32[576]{0:T(1024)S(1)}, /*index=5*/s32[1,2]{1,0:T(1,128)}, ...), branch_computations={%region_44.51_spmd, %region_51.58_spmd} | conditional | flops 9440318464 | bytes 258045888 | solution.py:157
  948.9 55.0 %concatenate.596 = bf16[3136,4320]{1,0:T(8,128)(2,1)} concatenate(bf16[3136,160]{1,0:T(8,128)(2,1)} %concatenate.514, bf16[3136,160]{1,0:T(8,128)(2,1)} %concatenate.515, bf16[3136,160]{1,0:T(8,128)(2,1)} %concatenate.516, bf16[3136,160]{1,0:T(8,128)(2,1)} %concatenate.572, bf16[3136,160]{1,0:T(8,128)(2,1)} %concatenate.573, bf16[3136,160]{1,0:T(8,128)(2,1)} %concatenate.575, ...), dimensions={1} | concatenate | bytes 54190080 | tf_op jit(solution)/shard_map/cond/branch_1_fun/concatenate | solution.py:116
  1181.6 60.8 %conditional.31 = (bf16[1,8,7,7,832]{4,1,3,2,0:T(8,128)(2,1)S(1)}) conditional(s32[]{:T(128)} %convert_element_type.2639, (f32[3136,576]{1,0:T(8,128)}, f32[]{:T(128)}, f32[576]{0:T(1024)S(1)}, f32[576]{0:T(1024)S(1)}, f32[576]{0:T(1024)S(1)}, /*index=5*/s32[1,2]{1,0:T(1,128)}, f32[3136,448]{1,0:T(8,128)}, f32[]{:T(128)}, f32[448]{0:T(512)}, ...), branch_computations={%region_61.64_spmd, %region_64.68_spmd} | conditional | flops 40271492 | bytes 92214792
  1253.1 40.2 all-reduce.333
  1342.4 39.6 all-reduce.331
  1447.5 73.8 %conditional.35 = (f32[3136,576]{0,1:T(8,128)}, f32[576]{0:T(1024)}, f32[576]{0:T(1024)}, f32[]{:T(128)}) conditional(s32[]{:T(128)} %convert_element_type.2639, () %tuple.213, (bf16[1,16,14,14,832]{4,3,2,1,0:T(8,128)(2,1)}, bf16[832,448]{1,0:T(8,128)(2,1)}, s32[1,2]{1,0:T(1,128)}, bf16[832,128]{1,0:T(8,128)(2,1)}) %tuple.1457), branch_computations={%region_94.95_spmd, %region_95.102_spmd} | conditional | flops 3046093824 | bytes 133557152 | solution.py:157
  1521.4 321.3 %collective-permute-done.3 = bf16[1,8,7,7,832]{4,1,3,2,0:T(8,128)(2,1)} collective-permute-done((bf16[1,8,7,7,832]{4,1,3,2,0:T(8,128)(2,1)}, bf16[1,8,7,7,832]{4,1,3,2,0:T(8,128)(2,1)}, u32[]{:S(2)}, u32[]{:S(2)}) %collective-permute-start.3) | collective-permute-done | bytes 652320 | tf_op jit(solution)/shard_map/ppermute | solution.py:28
  1842.7 103.8 %conditional.42 = (f32[3136,832]{1,0:T(8,128)}, f32[832]{0:T(1024)}, f32[832]{0:T(1024)}) conditional(s32[]{:T(128)} %convert_element_type.2639, (bf16[2,8,7,7,832]{4,3,2,1,0:T(8,128)(2,1)}, f32[3136,576]{1,0:T(8,128)}, f32[]{:T(128)}, f32[576]{0:T(1024)S(1)}, f32[576]{0:T(1024)S(1)}, /*index=5*/f32[3136,448]{1,0:T(8,128)}, f32[]{:T(128)}, ...), branch_computations={%region_160.165_spmd, %region_165.170_spmd} | conditional | flops 56652292 | bytes 171239232 | solution.py:157
  1946.5 73.8 %all-reduce.329 = (f32[]{:T(128)}, f32[576]{0:T(1024)S(1)}, f32[576]{0:T(1024)}, f32[832]{0:T(1024)}, f32[832]{0:T(1024)}) all-reduce(f32[]{:T(128)} %get-tuple-element.999, f32[576]{0:T(1024)} %get-tuple-element.1000, f32[576]{0:T(1024)} %get-tuple-element.1001, ...), channel_id=1, replica_groups=mesh['section'=2,'dp'=16] {'dp'}, use_global_device_ids=true, to_apply=%region_102.103 | all-reduce | flops 2817 | bytes 22536 | tf_op jit(solution)/shard_map/psum | solution.py:166
  2021.0 367.6 %conditional.36 = (f32[3136,448]{0,1:T(8,128)}, f32[448]{0:T(512)}, f32[448]{0:T(512)}, f32[]{:T(128)}) conditional(s32[]{:T(128)} %convert_element_type.2639, () %tuple.215, (f32[]{:T(128)}, f32[576]{0:T(1024)}, f32[3136,576]{0,1:T(8,128)}, f32[576]{0:T(1024)S(1)}, f32[576]{0:T(1024)S(1)}, /*index=5*/s32[1,2]{1,0:T(1,128)}, ...), branch_computations={%region_105.106_spmd, %region_106.113_spmd} | conditional | flops 9440318464 | bytes 261266688 | solution.py:157
  2201.1 55.1 %concatenate.839 = bf16[3136,4320]{1,0:T(8,128)(2,1)} concatenate(bf16[3136,160]{1,0:T(8,128)(2,1)} %concatenate.745, bf16[3136,160]{1,0:T(8,128)(2,1)} %concatenate.746, bf16[3136,160]{1,0:T(8,128)(2,1)} %concatenate.747, bf16[3136,160]{1,0:T(8,128)(2,1)} %concatenate.748, bf16[3136,160]{1,0:T(8,128)(2,1)} %concatenate.749, bf16[3136,160]{1,0:T(8,128)(2,1)} %concatenate.750, ...), dimensions={1} | concatenate | bytes 54190080 | tf_op jit(solution)/shard_map/cond/branch_1_fun/concatenate | solution.py:116
  2388.6 722.2 %conditional.43 = (bf16[3136,256]{1,0:T(8,128)(2,1)}, bf16[3136,128]{1,0:T(8,128)(2,1)}, f32[3136,192]{1,0:T(8,128)S(1)}, f32[832,256]{1,0:T(8,128)}, f32[4320,3...) conditional(s32[]{:T(128)} %convert_element_type.2639, ...), branch_computations={%region_172.178_spmd, %region_178.184_spmd} | conditional | flops 20894103552 | bytes 889462848 | solution.py:157
  2702.5 55.1 %concatenate.1287 = bf16[3136,4320]{1,0:T(8,128)(2,1)} concatenate(bf16[3136,160]{1,0:T(8,128)(2,1)} %concatenate.1261, bf16[3136,160]{1,0:T(8,128)(2,1)} %concatenate.1262, bf16[3136,160]{1,0:T(8,128)(2,1)} %concatenate.1263, bf16[3136,160]{1,0:T(8,128)(2,1)} %concatenate.1264, bf16[3136,160]{1,0:T(8,128)(2,1)} %concatenate.1265, bf16[3136,160]{1,0:T(8,128)(2,1)} %concatenate.1266, ...), dimensions={1} | concatenate | bytes 54190080 | tf_op jit(solution)/shard_map/cond/branch_1_fun/concatenate | solution.py:116
  2799.6 47.0 %reshape.9126 = f32[1,16,14,14,4320]{4,3,2,1,0:T(8,128)} reshape(f32[3136,4320]{1,0:T(8,128)} %fusion.828) | data formatting | bytes 108380160 | tf_op jit(solution)/shard_map/cond/branch_1_fun/reshape | solution.py:354
  2846.7 46.3 slice_multiply_fusion.134
  3110.8 38.3 all-reduce.328
  3149.2 140.3 %conditional.44 = (bf16[3136,832]{1,0:T(8,128)(2,1)}, f32[832,160]{0,1:T(8,128)}, f32[832,32]{0,1:T(8,128)S(1)}) conditional(s32[]{:T(128)} %convert_element_type.2639, (bf16[3136,256]{1,0:T(8,128)(2,1)}, f32[]{:T(128)}, f32[576]{0:T(1024)S(1)}, f32[576]{0:T(1024)S(1)}, f32[3136,192]{1,0:T(8,128)S(1)}, /*index=5*/f32[192]{0:T(256)}, ...), branch_computations={%region_186.190_spmd, %region_190.194_spmd} | conditional | flops 4049414144 | bytes 250739328 | solution.py:157
  3297.7 112.8 %conditional.45 = (f32[3136,832]{1,0:T(8,128)}, f32[832]{0:T(1024)S(1)}, f32[832]{0:T(1024)S(1)}) conditional(s32[]{:T(128)} %convert_element_type.2639, () %tuple.217, (bf16[1,8,7,7,832]{4,1,3,2,0:T(8,128)(2,1)}, f32[]{:T(128)}, f32[576]{0:T(1024)S(1)}, f32[3136,576]{0,1:T(8,128)}, f32[576]{0:T(1024)S(1)}, /*index=5*/f32[]{:T(128)}, ...), branch_computations={%region_194.195_spmd, %region_195.200_spmd} | conditional | flops 56652292 | bytes 196929056 | solution.py:157
  3410.6 73.6 %all-reduce.327 = (f32[]{:T(128)}, f32[576]{0:T(1024)}, f32[576]{0:T(1024)}, f32[832]{0:T(1024)S(1)}, f32[832]{0:T(1024)S(1)}) all-reduce(f32[]{:T(128)} %get-tuple-element.992, f32[576]{0:T(1024)S(1)} %get-tuple-element.993, f32[576]{0:T(1024)S(1)} %get-tuple-element.994, ...), channel_id=1, replica_groups=mesh['section'=2,'dp'=16] {'dp'}, use_global_device_ids=true, to_apply=%region_76.77 | all-reduce | flops 2817 | bytes 22536 | tf_op jit(solution)/shard_map/psum | solution.py:166
  3484.8 717.1 %conditional.46 = (bf16[3136,256]{1,0:T(8,128)(2,1)}, bf16[3136,128]{1,0:T(8,128)(2,1)}, f32[3136,192]{1,0:T(8,128)}, f32[832,256]{1,0:T(8,128)}, f32[4320,320]{...) conditional(s32[]{:T(128)} %convert_element_type.2639, ...), branch_computations={%region_202.203_spmd, %region_203.209_spmd} | conditional | flops 20894103552 | bytes 923827776 | solution.py:157
  3792.9 55.1 %concatenate.1351 = bf16[3136,4320]{1,0:T(8,128)(2,1)} concatenate(bf16[3136,160]{1,0:T(8,128)(2,1)} %concatenate.1325, bf16[3136,160]{1,0:T(8,128)(2,1)} %concatenate.1326, bf16[3136,160]{1,0:T(8,128)(2,1)} %concatenate.1327, bf16[3136,160]{1,0:T(8,128)(2,1)} %concatenate.1328, bf16[3136,160]{1,0:T(8,128)(2,1)} %concatenate.1329, bf16[3136,160]{1,0:T(8,128)(2,1)} %concatenate.1330, ...), dimensions={1} | concatenate | bytes 54190080 | tf_op jit(solution)/shard_map/cond/branch_1_fun/concatenate | solution.py:116
  3890.3 47.1 %reshape.9140 = f32[1,16,14,14,4320]{4,3,2,1,0:T(8,128)} reshape(f32[3136,4320]{1,0:T(8,128)} %fusion.1025) | data formatting | bytes 108380160 | tf_op jit(solution)/shard_map/cond/branch_1_fun/reshape | solution.py:354
  3937.4 46.0 slice_multiply_fusion.188
  4244.1 157.8 %conditional.47 = (f32[832,160]{0,1:T(8,128)S(1)}, f32[832,32]{0,1:T(8,128)S(1)}, bf16[1,16,14,14,832]{4,3,2,1,0:T(8,128)(2,1)}) conditional(s32[]{:T(128)} %convert_element_type.2639, () %tuple.212, (f32[]{:T(128)}, f32[576]{0:T(1024)S(1)}, f32[576]{0:T(1024)S(1)}, f32[192]{0:T(256)S(1)}, f32[3136,192]{1,0:T(8,128)}, ...), branch_computations={%region_211.212_spmd, %region_212.216_spmd} | conditional | flops 4049414144 | bytes 265992800 | solution.py:157
  4475.5 196.3 %all-reduce.341.cloned.1.call-done = (f32[1,832,256]{2,1,0:T(8,128)}, f32[1,832,160]{1,2,0:T(8,128)}, f32[1,4320,320]{1,2,0:T(8,128)}, f32[1,832,32]{1,2,0:T(8,1...) async-done(((f32[1,832,256]{2,1,0:T(8,128)}, f32[1,832,160]{1,2,0:T(8,128)}, f32[1,4320,320]{1,2,0:T(8,128)}, f32[1,832,32]{1,2,0:T(8,128)}, f32[1,864,128]{2,1,0:T(8,128)}, ...) | async-done | bytes 7888912 | tf_op jit(solution)/shard_map/psum | solution.py:508
  (1152 shorter events, 3354.7 us)
Async XLA Ops:
  7.2 33.9 all-gather.3.cloned.1.call-start
  13.4 1323.0 %all-gather.5.cloned.1.call-start = ((), (), s32[]{:S(2)}) async-start(), calls=%async_computation.1 | async-start | bytes 2408448 | tf_op jit(solution)/shard_map/all_gather | solution.py:203
  21.0 2367.6 %copy-start = (bf16[1,4320,320]{2,1,0:T(8,128)(2,1)}, bf16[1,4320,320]{2,1,0:T(8,128)(2,1)S(1)}, u32[]{:S(2)}) copy-start(bf16[1,4320,320]{2,1,0:T(8,128)(2,1)S(1)} %copy.147) | copy-start | bytes 8294404
  50.5 113.9 %copy-start.14 = (bf16[1,864,128]{2,1,0:T(8,128)(2,1)S(1)}, bf16[1,864,128]{2,1,0:T(8,128)(2,1)}, u32[]{:S(2)}) copy-start(bf16[1,864,128]{2,1,0:T(8,128)(2,1)} %param.61) | copy-start | bytes 663556
  164.4 404.3 %copy-start.112 = (f32[448]{0:T(512)S(1)}, f32[448]{0:T(512)}, u32[]{:S(2)}) copy-start(f32[448]{0:T(512)} %pad_maximum_fusion.27) | copy-start | bytes 5380
  650.5 4.4 collective-permute-start
  654.8 4017.0 %all-reduce.341.cloned.1.call-start = ((), (), s32[]{:S(2)}) async-start(), calls=%async_computation.2 | async-start | bytes 15958016 | tf_op jit(solution)/shard_map/psum | solution.py:508
  775.7 405.9 %copy-start.85 = (f32[576]{0:T(1024)}, f32[576]{0:T(1024)S(1)}, u32[]{:S(2)}) copy-start(f32[576]{0:T(1024)S(1)} %get-tuple-element.1645) | copy-start | bytes 6916
  775.7 405.9 %copy-start.87 = (f32[576]{0:T(1024)}, f32[576]{0:T(1024)S(1)}, u32[]{:S(2)}) copy-start(f32[576]{0:T(1024)S(1)} %get-tuple-element.1646) | copy-start | bytes 6916
  775.7 405.9 %copy-start.113 = (f32[448]{0:T(512)S(1)}, f32[448]{0:T(512)}, u32[]{:S(2)}) copy-start(f32[448]{0:T(512)} %pad_maximum_fusion.27) | copy-start | bytes 5380
  1243.2 5.1 collective-permute-start.1
  1248.3 594.4 %copy-start.89 = (f32[832]{0:T(1024)}, f32[832]{0:T(1024)S(1)}, u32[]{:S(2)}) copy-start(f32[832]{0:T(1024)S(1)} %pad_maximum_fusion.26) | copy-start | bytes 9988
  1446.2 396.5 %collective-permute-start.3 = (bf16[1,8,7,7,832]{4,1,3,2,0:T(8,128)(2,1)}, bf16[1,8,7,7,832]{4,1,3,2,0:T(8,128)(2,1)}, u32[]{:S(2)}, u32[]{:S(2)}) collective-permute-start(bf16[1,8,7,7,832]{4,1,3,2,0:T(8,128)(2,1)} %copy.162), channel_id=1, source_target_pairs={{16,0},{17,1},{18,2},{19,3},{20,4},{21,5},{22,6},{23,7},{24,8},{25... | collective-permute-start | bytes 1956872 | tf_op jit(solution)/shard_map/ppermute | solution.py:28
  1447.5 395.2 %copy-start.86 = (f32[576]{0:T(1024)S(1)}, f32[576]{0:T(1024)}, u32[]{:S(2)}) copy-start(f32[576]{0:T(1024)} %copy-done.85) | copy-start | bytes 6916
  1447.5 395.2 %copy-start.88 = (f32[576]{0:T(1024)S(1)}, f32[576]{0:T(1024)}, u32[]{:S(2)}) copy-start(f32[576]{0:T(1024)} %copy-done.87) | copy-start | bytes 6916
  2799.6 47.0 %copy-start.134 = (f32[16]{0:T(128)S(1)}, f32[16]{0:T(128)}, u32[]{:S(2)}) copy-start(f32[16]{0:T(128)} %get-tuple-element.2695) | copy-start | bytes 196 | tf_op jit(solution)/shard_map/cond
  2799.6 47.0 %copy-start.177 = (f32[16]{0:T(128)S(1)}, f32[16]{0:T(128)}, u32[]{:S(2)}) copy-start(f32[16]{0:T(128)} %get-tuple-element.1716) | copy-start | bytes 196 | tf_op jit(solution)/shard_map/cond
  2846.7 46.3 copy-start.158
  3292.0 4.4 collective-permute-start.4
  3297.7 186.5 %copy-start.1 = (bf16[1,4320,320]{2,1,0:T(8,128)(2,1)S(1)}, bf16[1,4320,320]{2,1,0:T(8,128)(2,1)}, u32[]{:S(2)}) copy-start(bf16[1,4320,320]{2,1,0:T(8,128)(2,1)} %copy-done) | copy-start | bytes 8294404
  3484.2 717.7 %copy-start.145 = (f32[576]{0:T(1024)S(1)}, f32[576]{0:T(1024)}, u32[]{:S(2)}) copy-start(f32[576]{0:T(1024)} %get-tuple-element.1617) | copy-start | bytes 6916
  3484.2 717.7 %copy-start.146 = (f32[576]{0:T(1024)S(1)}, f32[576]{0:T(1024)}, u32[]{:S(2)}) copy-start(f32[576]{0:T(1024)} %get-tuple-element.1618) | copy-start | bytes 6916
  3485.9 78.5 %copy-start.174 = (f32[16]{0:T(128)}, f32[16]{0:T(128)S(1)}, u32[]{:S(2)}) copy-start(f32[16]{0:T(128)S(1)} %get-tuple-element.1730) | copy-start | bytes 196 | tf_op jit(solution)/shard_map/cond
  3486.3 147.0 %copy-start.92 = (f32[3136]{0:T(1024)}, f32[3136]{0:T(1024)S(1)}, u32[]{:S(2)}) copy-start(f32[3136]{0:T(1024)S(1)} %broadcast_in_dim.254) | copy-start | bytes 37636 | tf_op jit(solution)/shard_map/cond
  3890.3 47.1 %copy-start.133 = (f32[16]{0:T(128)S(1)}, f32[16]{0:T(128)}, u32[]{:S(2)}) copy-start(f32[16]{0:T(128)} %get-tuple-element.2853) | copy-start | bytes 196 | tf_op jit(solution)/shard_map/cond
  3890.3 47.1 %copy-start.175 = (f32[16]{0:T(128)S(1)}, f32[16]{0:T(128)}, u32[]{:S(2)}) copy-start(f32[16]{0:T(128)} %copy-done.174) | copy-start | bytes 196 | tf_op jit(solution)/shard_map/cond
  3937.4 46.1 copy-start.156
  4201.9 42.2 copy-start.20
  4201.9 42.2 copy-start.105
  4201.9 42.2 copy-start.107
  4453.2 11.6 collective-permute-start.5
  4459.3 4.1 collective-permute-start.2
  (149 other events, 1054.4 us)
Sparse Core Ops, SparseCore 0:
  13.5 27.4 all-gather.2
  654.9 7.6 all-gather.4
  4421.9 249.8 all-reduce.340
where the time goes:
time: 4760 us; the launch traced here: 4690 us
  local copies, waits for them, and re-layouts  1970 us (41%)
  other arithmetic  1310 us (28%)
  blocking collectives  539 us (11%)
  waiting for transfers between devices  537 us (11%)
  matrix products  274 us (6%)
    concatenate x270, local copies, waits for them, and re-layouts, gather_taps(): return jnp.concatenate(pieces, axis=-1)  1170 us
    psum x10, blocking collectives, reduce_norms(): return lax.psum(partials, 'dp')  462 us
    mul x30, other arithmetic, gather_taps(): window * tap_masks[shift_t + 1][:, :, None, None, None].astype(volume.dtype)  351 us
    ppermute x6, waiting for transfers between devices, shifted_2(): return lax.ppermute(x, axis, pairs)  325 us
    mul x8, other arithmetic, scatter_taps(): shifted = shifted * tap_masks[shift_t + 1][:, :, None, None, None]  210 us
    psum x1, waiting for transfers between devices, on_device(): lax.psum((grad_one, grad_mid_in, grad_mid, grad_small_in, grad_small, gra...  196 us
    another operation x43, local copies, waits for them, and re-layouts  137 us
    dot_general x12, matrix products, dot_rows(): return jnp.dot(values, weight, preferred_element_type=jnp.float32)  100 us
  transfers between devices with their start and end apart: 9, of which 5 were waited for; matrix products, arithmetic and copies ran while one was open for 14% of the time, Pallas kernels for 0%

commit v1 on v0

v1 whole, which is shorter than its diff:
```python
import functools

import jax
import jax.numpy as jnp
from jax import lax
from jax.experimental import pallas as pl
from jax.experimental.pallas import tpu as pltpu
from jax.sharding import PartitionSpec as P

D = 832
DP = 896
C0 = 256
C1A = 160
C1B = 320
C2A = 32
C2B = 128
C3 = 128
EPS = 0.001
MESH = pl.DeviceIdType.MESH
F32 = jnp.float32
BF16 = jnp.bfloat16
VMEM_LIMIT = 60 * 2**20


def dot(a, b):
    return jnp.dot(a, b, preferred_element_type=F32)


def dot_nt(a, b):
    return lax.dot_general(a, b, (((1,), (1,)), ((), ())), preferred_element_type=F32)


def dot_tn(a, b):
    return lax.dot_general(a, b, (((0,), (0,)), ((), ())), preferred_element_type=F32)


def roll_rows(x, by):
    return pltpu.roll(x, by % x.shape[0], 0)


def roll_lanes(x, by):
    return pltpu.roll(x, by % x.shape[1], 1)


def lane_below(x, count):
    lanes = lax.broadcasted_iota(jnp.int32, x.shape, 1)
    return jnp.where(lanes < count, x, 0.0)


class Grid:
    def __init__(self, frames, side, pitch, stride, len_ref):
        self.frames, self.side, self.pitch, self.stride = frames, side, pitch, stride
        self.rows = side * pitch
        self.len_ref = len_ref
        self.sec = lax.axis_index("section")

    def label(self, frame):
        place = frame * self.stride
        label = jnp.int32(0)
        start = jnp.int32(0)
        for c in range(self.len_ref.shape[1]):
            end = start + self.len_ref[0, c]
            label = jnp.where((place >= start) & (place < end), jnp.int32(c + 1), label)
            start = end
        return label

    def place(self, j):
        return lax.rem(j + self.sec * (self.frames // 2), self.frames)

    def valid(self, j):
        return jnp.where(self.label(self.place(j)) > 0, 1.0, 0.0).astype(F32)

    def taps(self, j):
        f = self.place(j)
        here = self.label(f)
        out = []
        for dt in (-1, 0, 1):
            there = f + dt
            inside = (there >= 0) & (there < self.frames)
            same = inside & (here > 0) & (self.label(there) == here)
            out.append(jnp.where(same, 1.0, 0.0).astype(F32))
        return out

    def wrap(self, j):
        return lax.rem(j + self.frames, self.frames)

    def inv_spread(self, taps):
        return 1.0 / jnp.maximum(taps[0] + taps[1] + taps[2], 1.0)

    def places_yx(self):
        r = lax.broadcasted_iota(jnp.int32, (self.rows, 128), 0)
        y = r // self.pitch
        return y, r - y * self.pitch

    def colmask(self):
        y, x = self.places_yx()
        return jnp.where(x < self.side, 1.0, 0.0).astype(F32)

    def inv_edges(self):
        y, x = self.places_yx()
        last = self.side - 1
        ey = jnp.where((y == 0) | (y == last), 2.0, 3.0)
        ex = jnp.where((x == 0) | (x == last), 2.0, 3.0)
        return jnp.where(x < self.side, 1.0 / (ey * ex), 0.0).astype(F32)

    def box(self, load, j, taps):
        t = None
        for dt in (-1, 0, 1):
            term = load(self.wrap(j + dt)) * taps[dt + 1]
            t = term if t is None else t + term
        lanes = t.shape[-1]
        v = t.reshape(self.side, self.pitch, lanes)
        zero = jnp.zeros((1, self.pitch, lanes), F32)
        v = v + jnp.concatenate([v[1:], zero], 0) + jnp.concatenate([zero, v[:-1]], 0)
        v = v.reshape(self.rows, lanes)
        return v + roll_rows(v, 1) + roll_rows(v, -1)


def fold8(v):
    return jnp.sum(v.reshape(-1, 8, v.shape[-1]), axis=0)


def add_stats(acc, lanes, v, w=None):
    acc[0, :, lanes] += fold8(v)
    acc[1, :, lanes] += fold8(v * (v if w is None else w))


def affine(st, lanes, beta):
    total, square, count = st[0:1, lanes], st[1:2, lanes], st[2:3, lanes]
    mean = total / count
    scale = lax.rsqrt(square / count - mean * mean + EPS)
    return scale, mean


def soft(t):
    e = jnp.exp(-jnp.abs(t))
    r = 1.0 / (1.0 + e)
    return jnp.maximum(t, 0.0) + jnp.log(1.0 + e), jnp.where(t >= 0, r, e * r)


def sigm(t):
    e = jnp.exp(-jnp.abs(t))
    r = 1.0 / (1.0 + e)
    return jnp.where(t >= 0, r, e * r)


def greet():
    n = lax.axis_size("dp")
    me = lax.axis_index("dp")
    barrier = pltpu.get_barrier_semaphore()

    def go(k, _):
        pl.semaphore_signal(
            barrier, inc=1, device_id={"dp": lax.rem(me + k, n)}, device_id_type=MESH
        )
        return 0

    lax.fori_loop(1, n, go, 0)


def greeted():
    pl.semaphore_wait(pltpu.get_barrier_semaphore(), lax.axis_size("dp") - 1)


def exchange(loc, buf, ssem, rsem, out):
    n = lax.axis_size("dp")
    me = lax.axis_index("dp")

    def copy(k):
        return pltpu.make_async_remote_copy(
            src_ref=loc,
            dst_ref=buf.at[me],
            send_sem=ssem.at[k],
            recv_sem=rsem.at[me],
            device_id={"dp": lax.rem(me + k, n)},
            device_id_type=MESH,
        )

    def start(k, _):
        copy(k).start()
        return 0

    lax.fori_loop(1, n, start, 0)
    buf[me] = loc[...]

    def wait(k, _):
        copy(k).wait_send()
        j = lax.rem(me + k, n)
        pltpu.make_async_remote_copy(
            src_ref=loc,
            dst_ref=buf.at[j],
            send_sem=ssem.at[k],
            recv_sem=rsem.at[j],
            device_id={"dp": j},
            device_id_type=MESH,
        ).wait_recv()
        return 0

    lax.fori_loop(1, n, wait, 0)
    out[...] = jnp.sum(buf[...], axis=0)


def exchange_scratch(n, lanes):
    return [
        pltpu.VMEM((8, lanes), F32),
        pltpu.VMEM((n, 8, lanes), F32),
        pltpu.SemaphoreType.DMA((n,)),
        pltpu.SemaphoreType.DMA((n,)),
    ]


def pack_stats(loc, acc, count=None):
    lanes = loc.shape[1]
    loc[0:1, :] = jnp.sum(acc[0, :, 0:lanes], axis=0, keepdims=True)
    loc[1:2, :] = jnp.sum(acc[1, :, 0:lanes], axis=0, keepdims=True)
    if count is not None:
        loc[2:3, :] = jnp.full((1, loc.shape[1]), 1.0, F32) * count


def count_voxels(g):
    total = jnp.float32(0.0)
    for j in range(g.frames):
        total = total + g.valid(j)
    return total * float(g.side * g.side)


def loop(n, body):
    def step(i, _):
        body(i)
        return 0

    lax.fori_loop(0, n, step, 0)


def first_kernel(len_ref, xo, xr, wp, xp, z1, zin, st, yp, acc, loc, buf, ssem, rsem):
    greet()
    half, side = xo.shape[0], xo.shape[1]
    g = Grid(2 * half, side, 16, 1, len_ref)
    nf = 2
    acc[...] = jnp.zeros_like(acc)
    loc[...] = jnp.zeros_like(loc)
    for part, src in enumerate((xo, xr)):

        def body(i, src=src, part=part):
            f0 = part * half + i * nf
            for q in range(nf):
                vm = g.valid(f0 + q).astype(BF16)
                xp[f0 + q, :, 0:side, :] = src[i * nf + q] * vm
                xp[f0 + q, :, side:16, :] = jnp.zeros((side, 16 - side, D), BF16)
            lhs = xp[pl.ds(f0, nf)].reshape(nf * g.rows, D)
            y = dot(lhs, wp[...])
            z1[pl.ds(f0, nf), :, 0:C0] = y[:, 0:C0].reshape(nf, g.rows, C0)
            yp[pl.ds(f0, nf)] = y[:, 256:384].reshape(nf, g.rows, 128)
            zin[pl.ds(f0, nf)] = y[:, 384:640].reshape(nf, g.rows, 256)
            add_stats(acc, pl.ds(0, 256), y[:, 0:256])
            add_stats(acc, pl.ds(384, 256), y[:, 384:640])

        loop(half // nf, body)
    pool_forward(g, yp, z1, acc)
    pack_stats(loc, acc, count_voxels(g))
    greeted()
    exchange(loc, buf, ssem, rsem, st)


def pool_forward(g, yp, z1, acc):
    edges = g.inv_edges()

    def body(f):
        taps = g.taps(f)
        z = g.box(lambda j: yp[j], f, taps) * (edges * g.inv_spread(taps))
        z1[f, :, 256:384] = z
        add_stats(acc, pl.ds(256, 128), z)

    loop(g.frames, body)


def inner_tiles(g, zf, st, beta, f, mask):
    tiles = []
    for t in range(2):
        lanes = pl.ds(384 + 128 * t, 128)
        scale, mean = affine(st, lanes, None)
        b = beta[0:1, pl.ds(896 + 128 * t, 128)]
        act, _ = soft(zf[:, 128 * t : 128 * (t + 1)] * scale + (b - mean * scale))
        tiles.append(act * mask)
    return tiles


def neighbours32(v):
    return roll_rows(v, 1) + roll_lanes(v, 32) + roll_lanes(roll_rows(v, -1), 64)


def tap_tiles(a, b, mask):
    tail = lane_below(b, 32)
    small = lane_below(roll_lanes(b, -32), 32)
    ones = jnp.where(lax.broadcasted_iota(jnp.int32, b.shape, 1) == 96, mask, 0.0)
    return (
        [roll_rows(a, 1), a, roll_rows(a, -1), neighbours32(tail) + ones],
        neighbours32(small) + ones,
    )


def typical(beta):
    sp, sg = soft(jnp.broadcast_to(beta, (8, beta.shape[-1])))
    return sp + 0.5 * sg * (1.0 - sg)


def outer(c, s):
    k = lax.broadcasted_iota(jnp.int32, c.shape, 0)
    c = jnp.where(k < 2, c, 0.0).astype(BF16)
    s = jnp.broadcast_to(s, (8, s.shape[-1]))
    high = s.astype(BF16).astype(F32)
    k = lax.broadcasted_iota(jnp.int32, s.shape, 0)
    s = jnp.where(k == 0, high, jnp.where(k == 1, s - high, 0.0)).astype(BF16)
    return dot_tn(c, s)


def tap_points(beta):
    a = typical(beta[0:1, 896:1024])
    b = typical(beta[0:1, 1024:1152])

    def three(v):
        return v + roll_lanes(v, 32) + roll_lanes(v, 64)

    tail = three(lane_below(b, 32))
    small = three(lane_below(roll_lanes(b, -32), 32))
    return jnp.concatenate([a, a, a, tail], 1), small


def centre_mid(grad, beta):
    c, _ = tap_points(beta)
    row = jnp.broadcast_to(grad[992:993, :], (8, 1024))
    main = row[:, 256:512]
    tail = lane_below(roll_lanes(row[:, 768:896], 64), 64)
    s = jnp.concatenate([main, main, main, tail + roll_lanes(tail, 64), tail], 1)
    return outer(c, s)


def centre_small(grad, beta):
    _, c = tap_points(beta)
    row = jnp.broadcast_to(grad[224:225, 128:256], (8, 128))
    return outer(c, jnp.concatenate([row, row, row], 1))


def untap(parts, small):
    def back32(v):
        left = lane_below(roll_rows(v, -1), 32)
        centre = lane_below(roll_lanes(v, -32), 32)
        right = lane_below(roll_lanes(roll_rows(v, 1), -64), 32)
        return left + centre + right

    a = roll_rows(parts[0], -1) + parts[1] + roll_rows(parts[2], 1)
    return a, back32(parts[3]) + roll_lanes(back32(small), 32)


def conv_gather(taps, load_mid, load_small, g, f):
    main = small = tail = None
    for dt in (-1, 0, 1):
        p = load_mid(g.wrap(f + dt))
        s = load_small(g.wrap(f + dt))
        m = taps[dt + 1]
        k = dt + 1
        piece = p[:, 768:896] if k < 2 else p[:, 896:1024]
        if k == 1:
            piece = roll_lanes(piece, 64)
        terms = (p[:, 256 * k : 256 * k + 256] * m, s[:, 128 * k : 128 * k + 128] * m, piece * m)
        if main is None:
            main, small, tail = terms
        else:
            main, small, tail = main + terms[0], small + terms[1], tail + terms[2]
    return main, small, lane_below(tail, 64)


def conv_kernel(
    len_ref, zin, st1, beta, wf, ws, cat, scat, z2, st2, pbuf, sbuf, acc, loc, buf, ssem, rsem
):
    greet()
    frames = zin.shape[0]
    side = cat.shape[1] - 2
    g = Grid(frames, side, 16, 1, len_ref)
    acc[...] = jnp.zeros_like(acc)
    loc[...] = jnp.zeros_like(loc)
    colmask = g.colmask()

    def build(f):
        a, b = inner_tiles(g, zin[f], st1, beta, f, colmask * g.valid(f))
        parts, small = tap_tiles(a, b, colmask * g.valid(f))
        zero = jnp.zeros((1, 16, 512), BF16)
        cat[f, 0:1] = zero
        cat[f, side + 1 : side + 2] = zero
        scat[f, 0:1] = zero[:, :, 0:128]
        scat[f, side + 1 : side + 2] = zero[:, :, 0:128]
        for i, part in enumerate(parts):
            cat[f, 1 : side + 1, :, 128 * i : 128 * i + 128] = part.astype(BF16).reshape(
                side, 16, 128
            )
        scat[f, 1 : side + 1] = small.astype(BF16).reshape(side, 16, 128)

    loop(frames, build)
    nf = 4

    def products(i):
        f0 = i * nf
        lhs = jnp.concatenate(
            [
                cat[pl.ds(f0, nf), dy : dy + side].reshape(nf * g.rows, 512)
                for dy in range(3)
            ],
            axis=1,
        )
        pbuf[pl.ds(f0, nf)] = dot(lhs, wf[...]).reshape(nf, g.rows, 1024)
        lhs = jnp.concatenate(
            [
                scat[pl.ds(f0, nf), dy : dy + side].reshape(nf * g.rows, 128)
                for dy in range(3)
            ],
            axis=1,
        )
        sbuf[pl.ds(f0, nf)] = dot(lhs, ws[...]).reshape(nf, g.rows, 384)

    loop(frames // nf, products)
    gather_conv(g, colmask, pbuf, sbuf, z2, acc)
    pack_stats(loc, acc)
    greeted()
    exchange(loc, buf, ssem, rsem, st2)


def gather_conv(g, colmask, pbuf, sbuf, z2, acc):
    def body(f):
        main, small, tail = conv_gather(
            g.taps(f), lambda j: pbuf[j], lambda j: sbuf[j], g, f
        )
        wide = jnp.concatenate([colmask, colmask], 1)
        main, small, tail = main * wide, small * colmask, tail * colmask
        z2[f, :, 0:256] = main
        z2[f, :, 256:384] = small
        z2[f, :, 384:512] = tail
        add_stats(acc, pl.ds(0, 256), main)
        add_stats(acc, pl.ds(256, 128), small)
        add_stats(acc, pl.ds(384, 128), tail)

    loop(g.frames, body)


def final_tile(t, z1, z2):
    if t < 3:
        return z1, 128 * t, False
    return z2, 128 * (t - 3), True


def tile_norm(t, st1, st2, beta):
    if t < 3:
        scale, mean = affine(st1, pl.ds(128 * t, 128), None)
    else:
        lanes = pl.ds(128 * (t - 3), 128)
        total, square, count = st2[0:1, lanes], st2[1:2, lanes], st1[2:3, 0:128]
        mean = total / count
        scale = lax.rsqrt(square / count - mean * mean + EPS)
    return scale, mean, beta[0:1, pl.ds(128 * t, 128)]


def output_kernel(len_ref, z1, z2, st1, st2, beta, sig, hand, asum, bsum, scr):
    frames = z1.shape[0]
    side = z1.shape[1] // 16
    half = side // 2
    g = Grid(frames, side, 16, 1, len_ref)
    colmask = g.colmask()

    def body(k):
        mask = colmask * g.valid(2 * k)
        for t in range(7):
            ref, lane, _ = final_tile(t, z1, z2)
            scale, mean, b = tile_norm(t, st1, st2, beta)
            pooled = None
            for q in range(2):
                u = (ref[2 * k + q, :, lane : lane + 128] - mean) * scale
                sp, sg = soft(u + b)
                sp, sg = sp * mask, sg * mask
                if t == 6:
                    lanes = lax.broadcasted_iota(jnp.int32, sp.shape, 1)
                    sp = jnp.where(lanes == 127, mask, lane_below(sp, 64))
                    sg = lane_below(sg, 64)
                sig[2 * k + q, :, 128 * t : 128 * t + 128] = sg.astype(BF16)
                three = [sp, sg, sg * u]
                three = [
                    jnp.sum(v.reshape(half, 2, 16, 128), axis=1) for v in three
                ]
                pooled = three if pooled is None else [x + y for x, y in zip(pooled, three)]
            for v, dst in zip(pooled, (hand, asum, bsum)):
                scr[...] = v
                dst[k, :, :, 128 * t : 128 * t + 128] = (
                    scr[:, pl.ds(0, 8, stride=2), :] + scr[:, pl.ds(1, 8, stride=2), :]
                ) * 0.125

    loop(frames // 2, body)


def second_kernel(
    len_ref, hand, asum, bsum, grad, wp, wf, ws, beta, beta1,
    out, hg, dwp, dwf, dws, sums5, sums6, sums7,
    hbuf, z1, zin, z2, yp, cat, scat, pbuf, sbuf, dbuf, dzf, dzc, dzs, dz1, din,
    acc, st3, st4, acc7, accm, accs, accp,
    loc3, buf3, ss3, rs3, loc4, buf4, ss4, rs4, loc5, buf5, ss5, rs5,
    loc6, buf6, ss6, rs6, loc7, buf7, ss7, rs7,
):
    greet()
    frames, side = hand.shape[0], hand.shape[1]
    g = Grid(frames, side, 8, 2, len_ref)
    rows = g.rows
    colmask = g.colmask()
    for ref in (acc, acc7, loc3, loc4, loc5, loc6, loc7):
        ref[...] = jnp.zeros_like(ref)

    hbuf[...] = hand[...].reshape(frames * rows, DP).astype(BF16)
    y = dot(hbuf[...], wp[...])
    z1[:, :, 0:C0] = y[:, 0:C0].reshape(frames, rows, C0)
    yp[...] = y[:, 256:384].reshape(frames, rows, 128)
    zin[...] = y[:, 384:640].reshape(frames, rows, 256)

    def first_sums(f):
        vm = colmask * g.valid(f)
        wide = jnp.concatenate([vm, vm], 1)
        one, inner = z1[f, :, 0:256], zin[f]
        add_stats(acc, pl.ds(0, 256), one * wide)
        add_stats(acc, pl.ds(384, 256), inner * wide)

    loop(frames, first_sums)
    pool_forward(g, yp, z1, acc)
    pack_stats(loc3, acc, count_voxels(g))
    greeted()
    exchange(loc3, buf3, ss3, rs3, st3)

    def shifted(v, dy):
        v = v.reshape(2, side, 8, v.shape[-1])
        zero = jnp.zeros((2, 1, 8, v.shape[-1]), F32)
        if dy < 0:
            v = jnp.concatenate([zero, v[:, :-1]], 1)
        elif dy > 0:
            v = jnp.concatenate([v[:, 1:], zero], 1)
        return v.reshape(2 * rows, v.shape[-1])

    def build(i):
        pairs = []
        for q in range(2):
            f = 2 * i + q
            a, b = inner_tiles(g, zin[f], st3, beta, f, colmask * g.valid(f))
            parts, small = tap_tiles(a, b, colmask * g.valid(f))
            pairs.append(parts + [small])
        here = pl.ds(pl.multiple_of(i * 2 * rows, 16), 2 * rows)
        for t in range(5):
            both = jnp.concatenate([pairs[0][t], pairs[1][t]], 0)
            for dy in (-1, 0, 1):
                v = shifted(both, dy).astype(BF16)
                if t < 4:
                    lane = (dy + 1) * 512 + 128 * t
                    cat[here, lane : lane + 128] = v
                else:
                    scat[here, (dy + 1) * 128 : (dy + 1) * 128 + 128] = v

    loop(frames // 2, build)
    pbuf[...] = dot(cat[...], wf[...]).reshape(frames, rows, 1024)
    sbuf[...] = dot(scat[...], ws[...]).reshape(frames, rows, 384)
    acc[...] = jnp.zeros_like(acc)
    gather_conv(g, colmask, pbuf, sbuf, z2, acc)
    pack_stats(loc4, acc)
    exchange(loc4, buf4, ss4, rs4, st4)

    acc7[...] = jnp.zeros_like(acc7)

    def emit(i):
        here = pl.ds(pl.multiple_of(i * 2 * rows, 16), 2 * rows)
        for t in range(7):
            lanes = pl.ds(128 * t, 128)
            ref, lane, _ = final_tile(t, z1, z2)
            scale, mean, b = tile_norm(t, st3, st4, beta)
            gr = grad[here, lanes].astype(F32)
            outs = []
            for q in range(2):
                f = 2 * i + q
                mask = colmask * g.valid(f)
                u = (ref[f, :, lane : lane + 128] - mean) * scale
                sp, sg = soft(u + b)
                outs.append(sp * mask)
                d = gr[q * rows : (q + 1) * rows] * sg * mask
                dbuf[f, :, lanes] = d
                add_stats(acc7, lanes, d, u)
            out[here, lanes] = jnp.concatenate(outs, 0).astype(BF16)

    loop(frames // 2, emit)
    pack_stats(loc5, acc7)
    exchange(loc5, buf5, ss5, rs5, sums5)

    count = st3[2:3, 0:128]

    def dz_of(f, t, mask):
        ref, lane, _ = final_tile(t, z1, z2)
        lanes = pl.ds(128 * t, 128)
        scale, mean, _ = tile_norm(t, st3, st4, beta)
        u = (ref[f, :, lane : lane + 128] - mean) * scale
        m1, m2 = sums5[0:1, lanes] / count, sums5[1:2, lanes] / count
        return (dbuf[f, :, lanes] - m1 - u * m2) * (scale * mask)

    def dz_final(f):
        mask = colmask * g.valid(f)
        for t in range(2):
            dz1[f, :, 128 * t : 128 * t + 128] = dz_of(f, t, mask)
        yp[f] = dz_of(f, 2, mask) * (g.inv_edges() * g.inv_spread(g.taps(f)))
        for t in range(3, 7):
            z = dz_of(f, t, mask)
            if t == 6:
                z = lane_below(z, 64)
            dzf[f, :, 128 * (t - 3) : 128 * (t - 3) + 128] = z

    loop(frames, dz_final)

    def spread(f):
        boxed = g.box(lambda j: yp[j], f, g.taps(f)) * colmask
        dz1[f, :, 256:384] = boxed
        for dt in (-1, 0, 1):
            k = dt + 1
            j = g.wrap(f - dt)
            m = g.taps(j)[k]
            dzc[f, :, 256 * k : 256 * k + 256] = dzf[j, :, 0:256] * m
            dzs[f, :, 128 * k : 128 * k + 128] = dzf[j, :, 256:384] * m
            tail = dzf[j, :, 384:512] * m
            if k == 0:
                low_tail = tail
            elif k == 1:
                dzc[f, :, 768:896] = low_tail + roll_lanes(tail, 64)
            else:
                dzc[f, :, 896:1024] = tail

    loop(frames, spread)
    dzc_b = dzc[...].reshape(frames * rows, 1024).astype(BF16)
    dzs_b = dzs[...].reshape(frames * rows, 384).astype(BF16)
    q = dot_nt(dzc_b, wf[...])
    for dy in range(3):
        pbuf[:, :, 0:512] = q[:, 512 * dy : 512 * dy + 512].reshape(frames, rows, 512)
        back_rows(g, pbuf, 512, dy - 1, din if dy == 1 else None, dbuf, dy == 0)
    q = dot_nt(dzs_b, ws[...])
    for dy in range(3):
        sbuf[:, :, 0:128] = q[:, 128 * dy : 128 * dy + 128].reshape(frames, rows, 128)
        back_rows(g, sbuf, 128, dy - 1, None, dzf, dy == 0)
    acc[...] = jnp.zeros_like(acc)

    def inner_back(f):
        back = [dbuf[f, :, 128 * t : 128 * t + 128] for t in range(4)]
        tiles = untap(back, dzf[f, :, 0:128])
        mask = colmask * g.valid(f)
        for t in range(2):
            inner_up(g, t, zin[f, :, 128 * t : 128 * t + 128], tiles[t] * mask, st3, beta, din, f, acc)

    loop(frames, inner_back)
    pack_stats(loc6, acc)
    exchange(loc6, buf6, ss6, rs6, sums6)
    accm[...] = dot_tn(cat[...], dzc_b)
    mid = centre_mid(accm, beta)
    for k in range(3):
        dwf[512 * k : 512 * k + 512] = (accm[512 * k : 512 * k + 512] - mid).astype(BF16)
    accs[...] = dot_tn(scat[...], dzs_b)
    small = centre_small(accs, beta)
    for k in range(3):
        dws[128 * k : 128 * k + 128] = (accs[128 * k : 128 * k + 128] - small).astype(BF16)

    def dz_inner(f):
        mask = colmask * g.valid(f)
        for t in range(2):
            dz1[f, :, 384 + 128 * t : 512 + 128 * t] = inner_dz(t, zin, din, st3, sums6, count, f, mask)

    loop(frames, dz_inner)
    dz1_b = dz1[...].reshape(frames * rows, 640).astype(BF16)
    hgv = dot_nt(dz1_b, wp[...]).astype(BF16).astype(F32)
    hg[...] = hgv.reshape(frames, side, 8, DP)
    acc7[...] = jnp.zeros_like(acc7)

    def upstream(f):
        for t in range(7):
            lanes = pl.ds(128 * t, 128)
            gr = hg[f, :, :, lanes].reshape(rows, 128)
            acc7[0, :, lanes] += fold8(gr * asum[f, :, :, lanes].reshape(rows, 128))
            acc7[1, :, lanes] += fold8(gr * bsum[f, :, :, lanes].reshape(rows, 128))

    loop(frames, upstream)
    pack_stats(loc7, acc7)
    exchange(loc7, buf7, ss7, rs7, sums7)
    accp[...] = dot_tn(hbuf[...], dz1_b)
    pool = dz1[:, :, 256:384].reshape(frames * rows, 128)
    rest = (pool - dz1_b[:, 256:384].astype(F32)).astype(BF16)
    accp[:, 256:384] += dot_tn(hbuf[...], rest)
    c = jnp.concatenate([typical(beta1[0:1, 0:832]), jnp.zeros((8, 64), F32)], 1)
    dwp[...] = (accp[...] - outer(c, accp[DP - 1 : DP, :])).astype(BF16)


def back_rows(g, src, lanes, dy, _, dst, first):
    def body(f):
        v = src[f, :, 0:lanes].reshape(g.side, g.pitch, lanes)
        zero = jnp.zeros((1, g.pitch, lanes), F32)
        if dy > 0:
            v = jnp.concatenate([zero, v[:-1]], 0)
        elif dy < 0:
            v = jnp.concatenate([v[1:], zero], 0)
        v = v.reshape(g.rows, lanes)
        dst[f, :, 0:lanes] = v if first else dst[f, :, 0:lanes] + v

    loop(g.frames, body)


def inner_up(g, t, z, back, st, beta, din, f, acc):
    lanes = pl.ds(384 + 128 * t, 128)
    scale, mean = affine(st, lanes, None)
    u = (z - mean) * scale
    d = back * sigm(u + beta[0:1, pl.ds(896 + 128 * t, 128)])
    din[f, :, 128 * t : 128 * t + 128] = d
    add_stats(acc, lanes, d, u)


def inner_dz(t, zin, din, st, sums, count, f, mask):
    lanes = pl.ds(384 + 128 * t, 128)
    scale, mean = affine(st, lanes, None)
    u = (zin[f, :, 128 * t : 128 * t + 128] - mean) * scale
    m1, m2 = sums[0:1, lanes] / count, sums[1:2, lanes] / count
    dz = (din[f, :, 128 * t : 128 * t + 128] - m1 - u * m2) * (scale * mask)
    return lane_below(dz, 64) if t == 1 else dz


def dz_kernel(len_ref, z1, z2, sig, hg, st1, st2, sums7, beta, dzc, dzs, dz1, scr, yp, dzf):
    frames = z1.shape[0]
    side = z1.shape[1] // 16
    half = side // 2
    g = Grid(frames, side, 16, 1, len_ref)
    colmask = g.colmask()
    edges = g.inv_edges()
    count = st1[2:3, 0:128]

    def body(k):
        mask = colmask * g.valid(2 * k)
        for t in range(7):
            lanes = pl.ds(128 * t, 128)
            ref, lane, _ = final_tile(t, z1, z2)
            scale, mean, _ = tile_norm(t, st1, st2, beta)
            m1, m2 = sums7[0:1, lanes] / count, sums7[1:2, lanes] / count
            gr = hg[k, :, :, lanes] * 0.125
            scr[:, pl.ds(0, 8, stride=2), :] = gr
            scr[:, pl.ds(1, 8, stride=2), :] = gr
            gr = scr[...]
            gr = jnp.broadcast_to(gr[:, None], (half, 2, 16, 128)).reshape(g.rows, 128)
            for q in range(2):
                f = 2 * k + q
                u = (ref[f, :, lane : lane + 128] - mean) * scale
                d = gr * sig[f, :, lanes].astype(F32)
                dz = (d - m1 - u * m2) * (scale * mask)
                if t < 2:
                    dz1[f, :, lanes] = dz.astype(BF16)
                elif t == 2:
                    yp[f] = dz * (edges * g.inv_spread(g.taps(f)))
                else:
                    if t == 6:
                        dz = lane_below(dz, 64)
                    dzf[f, :, 128 * (t - 3) : 128 * (t - 3) + 128] = dz.astype(BF16)

    loop(frames // 2, body)

    def spread(f):
        boxed = g.box(lambda j: yp[j], f, g.taps(f)) * colmask
        dz1[f, :, 256:384] = boxed.astype(BF16)
        zero = jnp.zeros((1, 16, 1024), BF16)
        dzc[f, 0:1] = zero
        dzc[f, side + 1 : side + 2] = zero
        dzs[f, 0:1] = zero[:, :, 0:384]
        dzs[f, side + 1 : side + 2] = zero[:, :, 0:384]

        def put(ref, lane, v):
            ref[f, 1 : side + 1, :, lane : lane + v.shape[-1]] = v.reshape(side, 16, v.shape[-1])

        for dt in (-1, 0, 1):
            k = dt + 1
            j = g.wrap(f - dt)
            m = g.taps(j)[k]
            mb = m.astype(BF16)
            put(dzc, 256 * k, dzf[j, :, 0:256] * mb)
            put(dzs, 128 * k, dzf[j, :, 256:384] * mb)
            tail = dzf[j, :, 384:512].astype(F32) * m
            if k == 0:
                low_tail = tail
            elif k == 1:
                put(dzc, 768, (low_tail + roll_lanes(tail, 64)).astype(BF16))
            else:
                put(dzc, 896, tail.astype(BF16))

    loop(frames, spread)


def conv_grad_kernel(cat, scat, dzc, dzs, beta, dwf, dws, acc, accs):
    frames = cat.shape[0]
    side = cat.shape[1] - 2
    rows = side * 16
    nf = 4
    acc[...] = jnp.zeros_like(acc)
    accs[...] = jnp.zeros_like(accs)

    def body(i):
        f0 = i * nf
        here = pl.ds(f0, nf)
        a = cat[here, 1 : side + 1].reshape(nf * rows, 512)
        s = scat[here, 1 : side + 1].reshape(nf * rows, 128)
        for dy in (-1, 0, 1):
            k = dy + 1
            b = dzc[here, 1 - dy : 1 - dy + side].reshape(nf * rows, 1024)
            acc[512 * k : 512 * k + 512] += dot_tn(a, b)
            b = dzs[here, 1 - dy : 1 - dy + side].reshape(nf * rows, 384)
            accs[128 * k : 128 * k + 128] += dot_tn(s, b)

    loop(frames // nf, body)
    mid = centre_mid(acc, beta)
    small = centre_small(accs, beta)
    for k in range(3):
        dwf[512 * k : 512 * k + 512] = (acc[512 * k : 512 * k + 512] - mid).astype(BF16)
        dws[128 * k : 128 * k + 128] = (accs[128 * k : 128 * k + 128] - small).astype(BF16)


def conv_back_kernel(
    len_ref, dzc, dzs, wf, ws, zin, st1, beta, dzi, sums8, din, acc, loc, buf, ssem, rsem
):
    greet()
    frames = zin.shape[0]
    side = dzc.shape[1] - 2
    g = Grid(frames, side, 16, 1, len_ref)
    rows = g.rows
    colmask = g.colmask()
    acc[...] = jnp.zeros_like(acc)
    loc[...] = jnp.zeros_like(loc)
    nf = 4

    def body(i):
        here = pl.ds(i * nf, nf)
        q = s = None
        for dy in (-1, 0, 1):
            k = dy + 1
            v = dzc[here, 1 - dy : 1 - dy + side].reshape(nf * rows, 1024)
            t = dot_nt(v, wf[512 * k : 512 * k + 512])
            q = t if q is None else q + t
            v = dzs[here, 1 - dy : 1 - dy + side].reshape(nf * rows, 384)
            t = dot_nt(v, ws[128 * k : 128 * k + 128])
            s = t if s is None else s + t
        for j in range(nf):
            f = i * nf + j
            qs = q[j * rows : (j + 1) * rows]
            tiles = untap([qs[:, 128 * t : 128 * t + 128] for t in range(4)], s[j * rows : (j + 1) * rows])
            mask = colmask * g.valid(f)
            for t in range(2):
                inner_up(g, t, zin[f, :, 128 * t : 128 * t + 128], tiles[t] * mask, st1, beta, din, f, acc)

    loop(frames // nf, body)
    pack_stats(loc, acc)
    greeted()
    exchange(loc, buf, ssem, rsem, sums8)
    count = st1[2:3, 0:128]

    def dz(f):
        mask = colmask * g.valid(f)
        for t in range(2):
            dzi[f, :, 128 * t : 128 * t + 128] = inner_dz(
                t, zin, din, st1, sums8, count, f, mask
            ).astype(BF16)

    loop(frames, dz)


def input_kernel(xp, dz1, dzi, wp, gin, dwp, acc):
    frames, side = xp.shape[0], xp.shape[1]
    rows = side * 16
    nf = 2
    acc[...] = jnp.zeros_like(acc)

    def body(i):
        here = pl.ds(i * nf, nf)
        d = jnp.concatenate([dz1[here], dzi[here]], -1).reshape(nf * rows, 640)
        back = dot_nt(d, wp[...]).astype(BF16).reshape(nf, side, 16, D)
        gin[here] = back[:, :, 0:side]
        acc[...] += dot_tn(xp[here].reshape(nf * rows, D), d)

    loop(frames // nf, body)
    dwp[...] = acc[...].astype(BF16)


def vmem(*shape, dtype=F32):
    return pltpu.VMEM(shape, dtype)


def call(kernel, outs, args, scratch, collective=None, smem_first=True):
    specs = [pl.BlockSpec(memory_space=pltpu.VMEM)] * len(args)
    if smem_first:
        specs[0] = pl.BlockSpec(memory_space=pltpu.SMEM)
    params = {"vmem_limit_bytes": VMEM_LIMIT}
    if collective is not None:
        params.update(collective_id=collective, has_side_effects=True)
    return pl.pallas_call(
        kernel,
        out_shape=[jax.ShapeDtypeStruct(shape, dtype) for shape, dtype in outs],
        in_specs=specs,
        out_specs=[pl.BlockSpec(memory_space=pltpu.VMEM)] * len(outs),
        scratch_shapes=scratch,
        compiler_params=pltpu.CompilerParams(**params),
    )(*args)


def to_final(v):
    one, mid, small, pool = v[..., :256], v[..., 256:576], v[..., 576:704], v[..., 704:]
    zero = jnp.zeros(v.shape[:-1] + (64,), v.dtype)
    return jnp.concatenate([one, pool, mid[..., :256], small, mid[..., 256:], zero], -1)


def from_final(v):
    return jnp.concatenate(
        [v[..., 0:256], v[..., 384:640], v[..., 768:832], v[..., 640:768], v[..., 256:384]], -1
    )


def arrange_first(w_one, w_mid_in, w_small_in, w_pool):
    zero = jnp.zeros((w_one.shape[0], 64), w_one.dtype)
    return jnp.concatenate([w_one, w_pool, w_mid_in, w_small_in, zero], 1)


def arrange_mid(w):
    w = w.reshape(3, 3, 3, C1A, C1B).transpose(1, 2, 3, 0, 4)
    rows = jnp.concatenate(
        [
            w[:, :, :128].reshape(3, 384, 3, C1B),
            w[:, :, 128:].reshape(3, 96, 3, C1B),
            jnp.zeros((3, 32, 3, C1B), w.dtype),
        ],
        1,
    )
    return jnp.concatenate(
        [
            rows[..., :256].reshape(1536, 768),
            rows[..., 256:].reshape(1536, 192),
            jnp.zeros((1536, 64), w.dtype),
        ],
        1,
    )


def restore_mid(g):
    g = g.reshape(3, 512, 1024)
    cols = jnp.concatenate(
        [g[..., :768].reshape(3, 512, 3, 256), g[..., 768:960].reshape(3, 512, 3, 64)], -1
    )
    w = jnp.concatenate(
        [cols[:, :384].reshape(3, 3, 128, 3, C1B), cols[:, 384:480].reshape(3, 3, 32, 3, C1B)], 2
    )
    return w.transpose(3, 0, 1, 2, 4).reshape(27 * C1A, C1B)


def arrange_small(w):
    w = w.reshape(3, 3, 96, C2B).transpose(1, 2, 0, 3)
    w = jnp.concatenate([w, jnp.zeros((3, 32, 3, C2B), w.dtype)], 1)
    return w.reshape(384, 384)


def restore_small(g):
    g = g.reshape(3, 128, 3, C2B)[:, :96]
    return g.transpose(2, 0, 1, 3).reshape(27 * C2A, C2B)


def arrange_beta(b):
    one, mid_in, mid = b[0:256], b[256:416], b[416:736]
    small_in, small, pool = b[736:768], b[768:896], b[896:1024]
    zero = jnp.zeros((64,), b.dtype)
    return jnp.concatenate(
        [one, pool, mid[:256], small, mid[256:], zero, mid_in, small_in, zero]
    )[None]


def restore_beta(final, inner):
    return jnp.concatenate(
        [
            final[0:256],
            inner[384:544],
            final[384:640],
            final[768:832],
            inner[544:576],
            final[640:768],
            final[256:384],
        ]
    )


def swap(x):
    return lax.ppermute(x, "section", [(0, 1), (1, 0)])


def on_device(
    clip_input, out_grad, clip_lengths, w_one, w_mid_in, w_mid, w_small_in, w_small, w_pool, bn_offset
):
    n = lax.axis_size("dp")
    sec = lax.axis_index("section")
    first = sec == 0

    def mine(v, axis=0):
        return lax.dynamic_index_in_dim(v, sec, axis, keepdims=False)

    def other(v, axis=0):
        return lax.dynamic_index_in_dim(v, 1 - sec, axis, keepdims=False)

    def both(v):
        got = swap(v[0])
        return jnp.where(first, v[0], got), jnp.where(first, got, v[0])

    x_got = swap(other(clip_input))
    x_own = mine(clip_input)
    half, side = x_own.shape[0], x_own.shape[1]
    frames = 2 * half
    rows = side * 16
    frames2, side2 = frames // 2, side // 2
    rows2 = side2 * 8
    lengths = lax.dynamic_slice_in_dim(clip_lengths, sec, 1, 0)

    wp1, wp2 = both(arrange_first(w_one[0], w_mid_in[0], w_small_in[0], w_pool[0])[None])
    wp2 = to_final(wp2.T).T
    beta1, beta2 = both(arrange_beta(bn_offset[0])[None])
    wf1, wf2 = both(arrange_mid(w_mid[0])[None])
    ws1, ws2 = both(arrange_small(w_small[0])[None])

    xp, z1, zin, st1 = call(
        first_kernel,
        [
            ((frames, side, 16, D), BF16),
            ((frames, rows, 384), F32),
            ((frames, rows, 256), F32),
            ((8, 640), F32),
        ],
        (lengths, x_own, x_got, wp1),
        [vmem(frames, rows, 128), vmem(2, 8, 640)] + exchange_scratch(n, 640),
        collective=1,
    )
    cat, scat, z2, st2 = call(
        conv_kernel,
        [
            ((frames, side + 2, 16, 512), BF16),
            ((frames, side + 2, 16, 128), BF16),
            ((frames, rows, 512), F32),
            ((8, 512), F32),
        ],
        (lengths, zin, st1, beta1, wf1, ws1),
        [vmem(frames, rows, 1024), vmem(frames, rows, 384), vmem(2, 8, 512)]
        + exchange_scratch(n, 512),
        collective=2,
    )
    sig, hand, asum, bsum = call(
        output_kernel,
        [((frames, rows, DP), BF16)] + [((frames2, side2, 8, DP), F32)] * 3,
        (lengths, z1, z2, st1, st2, beta1),
        [vmem(side2, 16, 128)],
    )
    grad_got = swap(other(out_grad))
    grad = jnp.concatenate([mine(out_grad), grad_got], 0)
    grad = jnp.pad(to_final(grad), ((0, 0), (0, 0), (0, 1), (0, 0))).reshape(frames2 * rows2, DP)
    total2 = frames2 * rows2
    out, hg, dwp2, dwf2, dws2, sums5, sums6, sums7 = call(
        second_kernel,
        [
            ((total2, DP), BF16),
            ((frames2, side2, 8, DP), F32),
            ((DP, 640), BF16),
            ((1536, 1024), BF16),
            ((384, 384), BF16),
            ((8, DP), F32),
            ((8, 640), F32),
            ((8, DP), F32),
        ],
        (lengths, hand, asum, bsum, grad, wp2, wf2, ws2, beta2, beta1),
        [
            vmem(total2, DP, dtype=BF16),
            vmem(frames2, rows2, 384),
            vmem(frames2, rows2, 256),
            vmem(frames2, rows2, 512),
            vmem(frames2, rows2, 128),
            vmem(total2, 1536, dtype=BF16),
            vmem(total2, 384, dtype=BF16),
            vmem(frames2, rows2, 1024),
            vmem(frames2, rows2, 384),
            vmem(frames2, rows2, DP),
            vmem(frames2, rows2, 512),
            vmem(frames2, rows2, 1024),
            vmem(frames2, rows2, 384),
            vmem(frames2, rows2, 640),
            vmem(frames2, rows2, 256),
            vmem(2, 8, 640),
            vmem(8, 640),
            vmem(8, 512),
            vmem(2, 8, DP),
            vmem(1536, 1024),
            vmem(384, 384),
            vmem(DP, 640),
        ]
        + exchange_scratch(n, 640)
        + exchange_scratch(n, 512)
        + exchange_scratch(n, DP)
        + exchange_scratch(n, 640)
        + exchange_scratch(n, DP),
        collective=3,
    )
    dzc, dzs, dz1 = call(
        dz_kernel,
        [
            ((frames, side + 2, 16, 1024), BF16),
            ((frames, side + 2, 16, 384), BF16),
            ((frames, rows, 384), BF16),
        ],
        (lengths, z1, z2, sig, hg, st1, st2, sums7, beta1),
        [vmem(side2, 16, 128), vmem(frames, rows, 128), vmem(frames, rows, 512, dtype=BF16)],
    )
    dwf1, dws1 = call(
        conv_grad_kernel,
        [((1536, 1024), BF16), ((384, 384), BF16)],
        (cat, scat, dzc, dzs, beta1),
        [vmem(1536, 1024), vmem(384, 384)],
        smem_first=False,
    )
    dzi, sums8 = call(
        conv_back_kernel,
        [((frames, rows, 256), BF16), ((8, 640), F32)],
        (lengths, dzc, dzs, wf1, ws1, zin, st1, beta1),
        [vmem(frames, rows, 256), vmem(2, 8, 640)] + exchange_scratch(n, 640),
        collective=4,
    )
    gin, dwp1 = call(
        input_kernel,
        [((frames, side, side, D), BF16), ((D, 640), BF16)],
        (xp, dz1, dzi, wp1),
        [vmem(D, 640)],
        smem_first=False,
    )

    dwp2 = from_final(dwp2.T).T
    beta_grad1 = restore_beta(sums7[0], sums8[0])
    beta_grad2 = restore_beta(sums5[0], sums6[0])

    def to_section(one, two):
        keep = jnp.where(first, one, two)
        send = jnp.where(first, two, one)
        return keep + swap(send)

    offset_grad = to_section(beta_grad1, beta_grad2)
    dwp = lax.psum(to_section(dwp1, dwp2), "dp").astype(F32)
    dwf = lax.psum(to_section(dwf1, dwf2), "dp").astype(F32)
    dws = lax.psum(to_section(dws1, dws2), "dp").astype(F32)

    out = from_final(out.reshape(frames2, side2, 8, DP)[:, :, :side2])
    out_got = swap(out[frames2 // 2 :])
    out_own = out[: frames2 // 2]
    block_output = jnp.stack([jnp.where(first, out_own, out_got), jnp.where(first, out_got, out_own)])
    gin_got = swap(gin[half:])
    gin_own = gin[:half]
    input_grad = jnp.stack([jnp.where(first, gin_own, gin_got), jnp.where(first, gin_got, gin_own)])
    return (
        block_output,
        input_grad,
        dwp[None, :, 0:256],
        dwp[None, :, 384:544],
        restore_mid(dwf)[None],
        dwp[None, :, 544:576],
        restore_small(dws)[None],
        dwp[None, :, 256:384],
        offset_grad[None],
    )


def solution(mesh):
    placed = (
        P("dp", "section", None, None, None),
        P("dp", "section", None, None, None),
        P("dp", None),
        P("section", None, None),
        P("section", None, None),
        P("section", None, None),
        P("section", None, None),
        P("section", None, None),
        P("section", None, None),
        P("section", None),
    )
    return jax.shard_map(
        on_device,
        mesh=mesh,
        in_specs=placed,
        out_specs=(
            P("dp", "section", None, None, None),
            P("dp", "section", None, None, None),
            P("section", None, None),
            P("section", None, None),
            P("section", None, None),
            P("section", None, None),
            P("section", None, None),
            P("section", None, None),
            P("section", None),
        ),
        check_vma=False,
    )
```

time: 4760 us -> 591 us (0.12); the launches traced: 4690 us -> 580 us
  local copies, waits for them, and re-layouts: 1970 us -> 107 us
  other arithmetic: 1310 us -> 42 us
  blocking collectives: 539 us -> 0 us
  waiting for transfers between devices: 537 us -> 154 us
  matrix products: 274 us -> 0 us
  Pallas kernels: 0 us -> 259 us
    concatenate x285 -> x11, local copies, waits for them, and re-layouts: 1200 us -> 8.51 us  [the longest x2 2.64 us: to_final(): jnp.concatenate([one, pool, mid[..., :256], small, mid[..., 256:], zero],...]
    mul x57 -> x0, other arithmetic: 645 us -> none  [the longest x30 351 us: gather_taps(): window * tap_masks[shift_t + 1][:, :, None, None, None].astype(volume.dtype)]
    psum x12 -> x0, blocking collectives: 539 us -> none  [the longest x10 462 us: reduce_norms(): return lax.psum(partials, 'dp')]
    reshape x42 -> x6, local copies, waits for them, and re-layouts: 397 us -> 18.4 us  [the longest x1 6.37 us: arrange_mid(): w[:, :, :128].reshape(3, 384, 3, C1B)]
    ppermute x6 -> x12, waiting for transfers between devices: 325 us -> 3.52 us  [swap(): return lax.ppermute(x, 'section', [(0, 1), (1, 0)])]
    add x31 -> x4, other arithmetic: 283 us -> 5.13 us  [to_section(): return keep + swap(send)]
    dot_general x32 -> x0, matrix products: 274 us -> none  [the longest x12 100 us: dot_rows(): return jnp.dot(values, weight, preferred_element_type=jnp.float32)]
    pallas_call x0 -> x8, Pallas kernels: none -> 259 us  [call(): pl.pallas_call(kernel, out_shape=[jax.ShapeDtypeStruct(shape, dtype) for...]
  transfers between devices with their start and end apart: 9 -> 13, of which waited for: 5 -> 3; matrix products, arithmetic and copies ran while one was open for 14% -> 17% of each run, Pallas kernels for 0% -> 15%
where the time goes in v1:
time: 591 us; the launch traced here: 580 us
  Pallas kernels  259 us (44%)
  waiting for transfers between devices  154 us (26%)
  local copies, waits for them, and re-layouts  107 us (18%)
  other arithmetic  42 us (7%)
  between operations  14.9 us (3%)
    pallas_call x8, Pallas kernels, call(): pl.pallas_call(kernel, out_shape=[jax.ShapeDtypeStruct(shape, dtype) for...  259 us
    psum x1, waiting for transfers between devices, on_device(): dwf = lax.psum(to_section(dwf1, dwf2), 'dp').astype(F32)  151 us
    unnamed x65, local copies, waits for them, and re-layouts  33.3 us
  transfers between devices with their start and end apart: 13, of which 3 were waited for; matrix products, arithmetic and copies ran while one was open for 17% of the time, Pallas kernels for 15%

profile of v1, /device:TPU:0, one launch (start us, length us, event | category | flops | bytes accessed | tf_op | source)
XLA Modules:
  0.0 580.2 jit_solution(15103408428611820361)
XLA Ops:
  7.3 5.7 dynamic-slice_bitcast_fusion
  13.9 2.5 concatenate.42
  16.4 5.5 copy.90
  24.8 3.1 copy.92
  27.9 6.4 %copy.91 = bf16[3,384,3,320]{1,0,3,2:T(4,128)(2,1)S(1)} copy(bf16[3,384,3,320]{3,1,0,2:T(8,128)(2,1)} %bitcast.122) | data formatting | bytes 4423680 | tf_op jit(solution)/shard_map/reshape | solution.py:927
  34.4 3.6 maximum_maximum_fusion
  40.3 2.2 copy.94
  44.7 2.9 copy.114
  47.7 2.5 maximum_maximum_fusion.1
  55.3 4.0 copy.131
  68.7 2.8 select_bitcast_fusion.2
  75.6 3.9 copy.89.xr
  79.5 27.5 %shard_map.169 = (bf16[16,14,16,832]{3,2,1,0:T(8,128)(2,1)}, f32[16,224,384]{2,1,0:T(8,128)}, f32[16,224,256]{2,1,0:T(8,128)}, f32[8,640]{1,0:T(8,128)}) custom-call(s32[1,2]{1,0:T(1,128)} %constant_dynamic-slice_fusion.1.len_ref, bf16[8,14,14,832]{3,2,1,0:T(8,128)(2,1)} %bitcast.117, bf16[8,14,14,832]{3,2,1,0:T(8,128)(2,1)} %copy.89.xr, ...), custom_call_target="tpu_custom_call" | custom-call | tf_op jit(solution)/shard_map/pallas_call | solution.py:896
  107.0 4.9 broadcast_select_fusion.1
  112.0 39.5 %shard_map.170 = (bf16[16,16,16,512]{3,2,1,0:T(8,128)(2,1)}, bf16[16,16,16,128]{3,2,1,0:T(8,128)(2,1)}, f32[16,224,512]{2,1,0:T(8,128)}, f32[8,512]{1,0:T(8,128)}) custom-call(s32[1,2]{1,0:T(1,128)} %constant_dynamic-slice_fusion.1.len_ref, f32[16,224,256]{2,1,0:T(8,128)} %get-tuple-element.39.zin, f32[8,640]{1,0:T(8,128)} %get-tuple-element.40.st1, ...), custom_call_target="tpu_custom_call" | custom-call | tf_op jit(solution)/shard_map/pallas_call | solution.py:896
  151.5 21.9 %shard_map.171 = (bf16[16,224,896]{2,1,0:T(8,128)(2,1)}, f32[8,7,8,896]{3,2,1,0:T(8,128)}, f32[8,7,8,896]{3,2,1,0:T(8,128)}, f32[8,7,8,896]{3,2,1,0:T(8,128)}) custom-call(s32[1,2]{1,0:T(1,128)} %constant_dynamic-slice_fusion.1.len_ref, f32[16,224,384]{2,1,0:T(8,128)} %get-tuple-element.38.z1, f32[16,224,512]{2,1,0:T(8,128)} %get-tuple-element.41.z2, ...), custom_call_target="tpu_custom_call" | custom-call | tf_op jit(solution)/shard_map/pallas_call | solution.py:896
  173.5 67.2 %shard_map.172 = (bf16[448,896]{1,0:T(8,128)(2,1)}, f32[8,7,8,896]{3,2,1,0:T(8,128)}, bf16[896,640]{1,0:T(8,128)(2,1)}, bf16[1536,1024]{1,0:T(8,128)(2,1)}, bf16...) custom-call(s32[1,2]{1,0:T(1,128)} %constant_dynamic-slice_fusion.1.len_ref, ...), custom_call_target="tpu_custom_call" | custom-call | tf_op jit(solution)/shard_map/pallas_call | solution.py:896
  240.7 21.2 %shard_map.173 = (bf16[16,16,16,1024]{3,2,1,0:T(8,128)(2,1)}, bf16[16,16,16,384]{3,2,1,0:T(8,128)(2,1)}, bf16[16,224,384]{2,1,0:T(8,128)(2,1)}) custom-call(s32[1,2]{1,0:T(1,128)} %constant_dynamic-slice_fusion.1.len_ref, f32[16,224,384]{2,1,0:T(8,128)} %get-tuple-element.38.z1, f32[16,224,512]{2,1,0:T(8,128)} %get-tuple-element.41.z2, ...), custom_call_target="tpu_custom_call" | custom-call | tf_op jit(solution)/shard_map/pallas_call | solution.py:896
  262.0 24.7 %shard_map.176 = (bf16[1536,1024]{1,0:T(8,128)(2,1)}, bf16[384,384]{1,0:T(8,128)(2,1)}) custom-call(bf16[16,16,16,512]{3,2,1,0:T(8,128)(2,1)} %get-tuple-element.58.cat, bf16[16,16,16,128]{3,2,1,0:T(8,128)(2,1)} %get-tuple-element.59.scat, bf16[16,16,16,1024]{3,2,1,0:T(8,128)(2,1)} %get-tuple-element.52.dzc, ...), custom_call_target="tpu_custom_call" | custom-call | tf_op jit(solution)/shard_map/pallas_call | solution.py:896
  289.0 37.5 %shard_map.174 = (bf16[16,224,256]{2,1,0:T(8,128)(2,1)}, f32[8,640]{1,0:T(8,128)}) custom-call(s32[1,2]{1,0:T(1,128)} %constant_dynamic-slice_fusion.1.len_ref, bf16[16,16,16,1024]{3,2,1,0:T(8,128)(2,1)} %get-tuple-element.52.dzc, bf16[16,16,16,384]{3,2,1,0:T(8,128)(2,1)} %get-tuple-element.53.dzs, bf16[1536,1024]{1,0:T(8,128)(2,1)} %get-tuple-element.109.wf, ...), custom_call_target="tpu_custom_call" | custom-call | tf_op jit(solution)/shard_map/pallas_call | solution.py:896
  326.5 19.5 %shard_map.175 = (bf16[16,14,14,832]{3,2,1,0:T(8,128)(2,1)}, bf16[832,640]{1,0:T(8,128)(2,1)}) custom-call(bf16[16,14,16,832]{3,2,1,0:T(8,128)(2,1)} %get-tuple-element.47.xp, bf16[16,224,384]{2,1,0:T(8,128)(2,1)} %get-tuple-element.51.dz1, bf16[16,224,256]{2,1,0:T(8,128)(2,1)} %get-tuple-element.54.dzi, bf16[832,640]{1,0:T(8,128)(2,1)} %get-tuple-element.113.wp), custom_call_target="tpu_custom_call" | custom-call | tf_op jit(solution)/shard_map/pallas_call | solution.py:896
  349.0 2.5 collective-permute-done.10
  353.6 3.3 select_add_fusion
  356.9 2.9 copy.105
  381.4 3.7 select_bitcast_fusion.1
  386.4 4.4 copy.110
  390.8 150.5 %all-reduce.5.cloned.1.call-done = (bf16[3,512,1024]{1,2,0:T(8,128)(2,1)}, bf16[832,640]{1,0:T(8,128)(2,1)}, bf16[3,128,3,128]{3,2,1,0:T(4,128)(2,1)}) async-done(((bf16[3,512,1024]{1,2,0:T(8,128)(2,1)}, bf16[832,640]{1,0:T(8,128)(2,1)}, bf16[3,128,3,128]{3,2,1,0:T(4,128)(2,1)}), (bf16[3,512,1024]{1,2,0:T(8,128)(2,1)}, bf16[832,640]{1,0:T(8,128)(2,1)}, ...) | async-done | bytes 4505616 | tf_op jit(solution)/shard_map/psum | solution.py:1146
  544.9 2.6 fusion
  550.0 7.2 %copy.106 = f32[3,384,3,320]{3,1,2,0:T(8,128)} copy(f32[3,384,3,320]{1,3,2,0:T(8,128)} %fusion) | data formatting | bytes 8847360 | tf_op jit(solution)/shard_map/slice | solution.py:949
  557.3 2.9 maximum_bitcast_fusion
  560.2 3.2 copy.108
  563.4 7.8 %copy.112 = f32[1,4320,320]{1,2,0:T(8,128)} copy(f32[1,4320,320]{2,1,0:T(8,128)} %bitcast.113) | data formatting | bytes 11059200
  (157 shorter events, 65.0 us)
Async XLA Ops:
  7.2 47.6 %copy-start = (s32[2,2]{1,0:T(2,128)S(1)}, s32[2,2]{1,0:T(2,128)}, u32[]{:S(2)}) copy-start(s32[2,2]{1,0:T(2,128)} %param.12) | copy-start | bytes 52
  7.2 534.1 %all-reduce.5.cloned.1.call-start = ((), (), s32[]{:S(2)}) async-start(), calls=%async_computation | async-start | bytes 9207808 | tf_op jit(solution)/shard_map/psum | solution.py:1146
  7.2 6.2 %copy-start.14 = (bf16[1,832,160]{1,2,0:T(8,128)(2,1)S(1)}, bf16[1,832,160]{1,2,0:T(8,128)(2,1)}, u32[]{:S(2)}) copy-start(bf16[1,832,160]{1,2,0:T(8,128)(2,1)} %param.14) | copy-start | bytes 798724
  7.3 6.4 %copy-start.18 = (bf16[1,832,32]{1,2,0:T(8,128)(2,1)S(1)}, bf16[1,832,32]{1,2,0:T(8,128)(2,1)}, u32[]{:S(2)}) copy-start(bf16[1,832,32]{1,2,0:T(8,128)(2,1)} %param.16) | copy-start | bytes 159748
  7.3 6.6 %copy-start.12 = (bf16[1,832,256]{2,1,0:T(8,128)(2,1)S(1)}, bf16[1,832,256]{2,1,0:T(8,128)(2,1)}, u32[]{:S(2)}) copy-start(bf16[1,832,256]{2,1,0:T(8,128)(2,1)} %param.13) | copy-start | bytes 1277956
  7.3 6.6 %copy-start.17 = (bf16[1,832,128]{2,1,0:T(8,128)(2,1)S(1)}, bf16[1,832,128]{2,1,0:T(8,128)(2,1)}, u32[]{:S(2)}) copy-start(bf16[1,832,128]{2,1,0:T(8,128)(2,1)} %param.18) | copy-start | bytes 638980
  13.0 62.6 %collective-permute-start = (bf16[8,14,14,832]{3,0,2,1:T(8,128)(2,1)}, bf16[8,14,14,832]{3,0,2,1:T(8,128)(2,1)}, u32[]{:S(2)}, u32[]{:S(2)}) collective-permute-start(bf16[8,14,14,832]{3,0,2,1:T(8,128)(2,1)} %get-tuple-element.110), channel_id=1, source_target_pairs={{0,16},{16,0},{1,17},{17,1},{2,18},{18,2},{3,19},{19,3},{4,20},{20... | collective-permute-start | bytes 7827464 | tf_op jit(solution)/shard_map/ppermute | solution.py:989
  16.3 52.3 %collective-permute-start.1 = (bf16[832,640]{1,0:T(8,128)(2,1)}, bf16[832,640]{1,0:T(8,128)(2,1)}, u32[]{:S(2)}, u32[]{:S(2)}) collective-permute-start(bf16[832,640]{1,0:T(8,128)(2,1)} %concatenate.42), channel_id=1, source_target_pairs={{0,16},{16,0},{1,17},{17,1},{2,18},{18,2},{3,19},{19,3},{4,20},{20... | collective-permute-start | bytes 3194888 | tf_op jit(solution)/shard_map/ppermute | solution.py:989
  44.7 3.0 copy-start.4
  47.7 3.0 copy-start.19
  47.7 3.2 slice-start
  47.7 3.4 copy-start.16
  50.2 56.8 %collective-permute-start.3 = (bf16[1536,1024]{1,0:T(8,128)(2,1)}, bf16[1536,1024]{1,0:T(8,128)(2,1)}, u32[]{:S(2)}, u32[]{:S(2)}) collective-permute-start(bf16[1536,1024]{1,0:T(8,128)(2,1)} %maximum_maximum_fusion.1), channel_id=1, source_target_pairs={{0,16},{16,0},{1,17},{17,1},{2,18},{18,2},{3,19},{19,3},{4,20},{20... | collective-permute-start | bytes 9437192 | tf_op jit(solution)/shard_map/ppermute | solution.py:989
  51.0 8.3 %collective-permute-start.2 = (f32[1,1152]{1,0:T(1,128)S(1)}, f32[1,1152]{1,0:T(1,128)S(1)}, u32[]{:S(2)}, u32[]{:S(2)}) collective-permute-start(f32[1,1152]{1,0:T(1,128)S(1)} %broadcast_in_dim.39), channel_id=1, source_target_pairs={{0,16},{16,0},{1,17},{17,1},{2,18},{18,2},{3,19},{19,3},{4,20},{20... | collective-permute-start | bytes 13832 | tf_op jit(solution)/shard_map/ppermute | solution.py:989
  52.3 7.7 %collective-permute-start.4 = (bf16[384,384]{1,0:T(8,128)(2,1)}, bf16[384,384]{1,0:T(8,128)(2,1)}, u32[]{:S(2)}, u32[]{:S(2)}) collective-permute-start(bf16[384,384]{1,0:T(8,128)(2,1)} %bitcast.109), channel_id=1, source_target_pairs={{0,16},{16,0},{1,17},{17,1},{2,18},{18,2},{3,19},{19,3},{4,20},{20... | collective-permute-start | bytes 884744 | tf_op jit(solution)/shard_map/ppermute | solution.py:989
  55.3 4.0 copy-start.13
  55.3 4.7 copy-start.7
  59.3 2.5 collective-permute-start.5
  262.0 24.7 %copy-start.2 = (bf16[1536,1024]{1,0:T(8,128)(2,1)S(1)}, bf16[1536,1024]{1,0:T(8,128)(2,1)}, u32[]{:S(2)}) copy-start(bf16[1536,1024]{1,0:T(8,128)(2,1)} %get-tuple-element.61) | copy-start | bytes 9437188
  288.7 64.8 %collective-permute-start.9 = (bf16[1536,1024]{1,0:T(8,128)(2,1)}, bf16[1536,1024]{1,0:T(8,128)(2,1)}, u32[]{:S(2)}, u32[]{:S(2)}) collective-permute-start(bf16[1536,1024]{1,0:T(8,128)(2,1)} %broadcast_select_fusion), channel_id=1, source_target_pairs={{0,16},{16,0},{1,17},{17,1},{2,18},{18,2},{3,19},{19,3},{4,20},{20... | collective-permute-start | bytes 9437192 | tf_op jit(solution)/shard_map/ppermute | solution.py:989
  326.5 19.5 %copy-start.10 = (bf16[896,640]{1,0:T(8,128)(2,1)S(1)}, bf16[896,640]{1,0:T(8,128)(2,1)}, u32[]{:S(2)}) copy-start(bf16[896,640]{1,0:T(8,128)(2,1)} %get-tuple-element.57) | copy-start | bytes 3440644
  346.1 1.2 copy-start.5
  346.1 2.3 copy-start.8
  346.1 2.3 copy-start.9
  348.4 4.0 collective-permute-start.8
  348.4 3.0 collective-permute-start.10
  362.9 18.5 %collective-permute-start.7 = (bf16[8,14,14,832]{3,0,2,1:T(8,128)(2,1)S(1)}, bf16[8,14,14,832]{3,0,2,1:T(8,128)(2,1)}, u32[]{:S(2)}, u32[]{:S(2)}) collective-permute-start(bf16[8,14,14,832]{3,0,2,1:T(8,128)(2,1)S(1)} %copy.102), channel_id=1, source_target_pairs={{0,16},{16,0},{1,17},{17,1},{2,18},{18,2},{3,19},{19,3},{4,20},{20... | collective-permute-start | bytes 7827464 | tf_op jit(solution)/shard_map/ppermute | solution.py:989
  369.1 9.7 %collective-permute-start.6 = (bf16[4,7,7,832]{3,0,2,1:T(4,128)(2,1)}, bf16[4,7,7,832]{3,0,2,1:T(4,128)(2,1)}, u32[]{:S(2)}, u32[]{:S(2)}) collective-permute-start(bf16[4,7,7,832]{3,0,2,1:T(4,128)(2,1)} %slice.374), channel_id=1, source_target_pairs={{0,16},{16,0},{1,17},{17,1},{2,18},{18,2},{3,19},{19,3},{4,20},{20... | collective-permute-start | bytes 978440 | tf_op jit(solution)/shard_map/ppermute | solution.py:989
  377.0 1.2 collective-permute-start.11
  541.3 2.6 copy-start.3
  563.4 8.7 %copy-start.15 = (bf16[3,128,3,128]{3,2,1,0:T(4,128)(2,1)S(1)}, bf16[3,128,3,128]{3,2,1,0:T(4,128)(2,1)}, u32[]{:S(2)}) copy-start(bf16[3,128,3,128]{3,2,1,0:T(4,128)(2,1)} %get-tuple-element.105) | copy-start | bytes 884740
  563.4 9.5 %copy-start.1 = (s32[2,2]{1,0:T(2,128)S(1)}, s32[2,2]{1,0:T(2,128)}, u32[]{:S(2)}) copy-start(s32[2,2]{1,0:T(2,128)} %param.12) | copy-start | bytes 52
  (2 other events, 2.0 us)
Sparse Core Ops, SparseCore 0:
  359.9 181.3 all-reduce.4

commit v2 on v1

v2 whole, which is shorter than its diff:
```python
import functools

import jax
import jax.numpy as jnp
from jax import lax
from jax.experimental import pallas as pl
from jax.experimental.pallas import tpu as pltpu
from jax.sharding import PartitionSpec as P

D = 832
DP = 896
C0 = 256
C1A = 160
C1B = 320
C2A = 32
C2B = 128
C3 = 128
EPS = 0.001
MESH = pl.DeviceIdType.MESH
F32 = jnp.float32
BF16 = jnp.bfloat16
VMEM_LIMIT = 60 * 2**20


def dot(a, b):
    return jnp.dot(a, b, preferred_element_type=F32)


def dot_nt(a, b):
    return lax.dot_general(a, b, (((1,), (1,)), ((), ())), preferred_element_type=F32)


def dot_tn(a, b):
    return lax.dot_general(a, b, (((0,), (0,)), ((), ())), preferred_element_type=F32)


def roll_rows(x, by):
    return pltpu.roll(x, by % x.shape[0], 0)


def roll_lanes(x, by):
    return pltpu.roll(x, by % x.shape[1], 1)


def lane_below(x, count):
    lanes = lax.broadcasted_iota(jnp.int32, x.shape, 1)
    return jnp.where(lanes < count, x, 0.0)


class Clips:
    def __init__(self, len_ref, frames, stride):
        sec = lax.axis_index("section")
        f = lax.broadcasted_iota(jnp.int32, (frames, 128), 0)

        def label(v):
            place = v * stride
            out = jnp.zeros_like(v)
            start = jnp.int32(0)
            for c in range(len_ref.shape[1]):
                end = start + len_ref[sec, c]
                out = jnp.where((place >= start) & (place < end), c + 1, out)
                start = end
            return out

        here = label(f)
        inside = here > 0

        def mask(m):
            return jnp.where(m, 1.0, 0.0).astype(F32)

        self.frames = frames
        self.valid = mask(inside)
        self.before = mask(inside & (f > 0) & (label(f - 1) == here))
        self.after = mask(inside & (f < frames - 1) & (label(f + 1) == here))
        self.inv = 1.0 / jnp.maximum(self.valid + self.before + self.after, 1.0)

    def times(self, v, pattern):
        return (v.reshape(-1, self.frames, 128) * pattern).reshape(v.shape)

    def fold(self, v):
        return jnp.sum(v.reshape(-1, self.frames, v.shape[-1]), axis=0)


def shift_places(v, frames, by):
    lanes = v.shape[-1]
    v3 = v.reshape(-1, frames, lanes)
    zero = jnp.zeros((1, frames, lanes), v.dtype)
    if by > 0:
        v3 = jnp.concatenate([v3[1:], zero], 0)
    else:
        v3 = jnp.concatenate([zero, v3[:-1]], 0)
    return v3.reshape(v.shape)


def add_stats(clips, acc, lanes, v, w=None):
    acc[0, :, lanes] += clips.fold(v)
    acc[1, :, lanes] += clips.fold(v * (v if w is None else w))


def affine(st, lanes):
    total, square, count = st[0:1, lanes], st[1:2, lanes], st[2:3, lanes]
    mean = total / count
    scale = lax.rsqrt(square / count - mean * mean + EPS)
    return scale, mean


def soft(t):
    e = jnp.exp(-jnp.abs(t))
    r = 1.0 / (1.0 + e)
    return jnp.maximum(t, 0.0) + jnp.log(1.0 + e), jnp.where(t >= 0, r, e * r)


def sigm(t):
    e = jnp.exp(-jnp.abs(t))
    r = 1.0 / (1.0 + e)
    return jnp.where(t >= 0, r, e * r)


def greet(partner=False):
    n = lax.axis_size("dp")
    me = lax.axis_index("dp")
    barrier = pltpu.get_barrier_semaphore()

    def go(k, _):
        pl.semaphore_signal(
            barrier, inc=1, device_id={"dp": lax.rem(me + k, n)}, device_id_type=MESH
        )
        return 0

    if partner:
        other = 1 - lax.axis_index("section")
        pl.semaphore_signal(barrier, inc=1, device_id={"section": other}, device_id_type=MESH)
    lax.fori_loop(1, n, go, 0)


def greeted(partner=False):
    pl.semaphore_wait(pltpu.get_barrier_semaphore(), lax.axis_size("dp") - 1 + int(partner))


def exchange_start(loc, buf, ssem, rsem):
    n = lax.axis_size("dp")
    me = lax.axis_index("dp")

    def start(k, _):
        pltpu.make_async_remote_copy(
            src_ref=loc,
            dst_ref=buf.at[me],
            send_sem=ssem.at[k],
            recv_sem=rsem.at[me],
            device_id={"dp": lax.rem(me + k, n)},
            device_id_type=MESH,
        ).start()
        return 0

    lax.fori_loop(1, n, start, 0)
    buf[me] = loc[...]


def exchange_finish(loc, buf, ssem, rsem, out):
    n = lax.axis_size("dp")
    me = lax.axis_index("dp")

    def wait(k, _):
        j = lax.rem(me + k, n)
        copy = pltpu.make_async_remote_copy(
            src_ref=loc,
            dst_ref=buf.at[j],
            send_sem=ssem.at[k],
            recv_sem=rsem.at[j],
            device_id={"dp": j},
            device_id_type=MESH,
        )
        copy.wait_send()
        copy.wait_recv()
        return 0

    lax.fori_loop(1, n, wait, 0)
    out[...] = jnp.sum(buf[...], axis=0)


def exchange(loc, buf, ssem, rsem, out):
    exchange_start(loc, buf, ssem, rsem)
    exchange_finish(loc, buf, ssem, rsem, out)


def swap_copy(src, dst, ssem, rsem):
    return pltpu.make_async_remote_copy(
        src_ref=src,
        dst_ref=dst,
        send_sem=ssem,
        recv_sem=rsem,
        device_id={"section": 1 - lax.axis_index("section")},
        device_id_type=MESH,
    )


def exchange_scratch(n, lanes):
    return [
        pltpu.VMEM((8, lanes), F32),
        pltpu.VMEM((n, 8, lanes), F32),
        pltpu.SemaphoreType.DMA((n,)),
        pltpu.SemaphoreType.DMA((n,)),
    ]


def pack_stats(clips, loc, acc, count=None):
    for t in range(loc.shape[1] // 128):
        lanes = pl.ds(128 * t, 128)
        loc[0:1, lanes] = jnp.sum(acc[0, :, lanes] * clips.valid, axis=0, keepdims=True)
        loc[1:2, lanes] = jnp.sum(acc[1, :, lanes] * clips.valid, axis=0, keepdims=True)
    if count is not None:
        total = jnp.sum(clips.valid, axis=0, keepdims=True) * float(count)
        for t in range(loc.shape[1] // 128):
            loc[2:3, 128 * t : 128 * t + 128] = total


def loop(n, body):
    def step(i, _):
        body(i)
        return 0

    lax.fori_loop(0, n, step, 0)


def inv_edges(side, frames, y):
    x = lax.broadcasted_iota(jnp.int32, (side, frames, 128), 0)
    ex = jnp.where((x == 0) | (x == side - 1), 0.5, 1.0 / 3.0).astype(F32)
    ey = jnp.where((y == 0) | (y == side - 1), 0.5, 1.0 / 3.0).astype(F32)
    return (ex * ey).reshape(side * frames, 128)


def box(clips, side, load, tx, store):
    frames = clips.frames
    tx[0] = jnp.zeros(tx.shape[1:], F32)
    tx[side + 1] = jnp.zeros(tx.shape[1:], F32)

    def across(y):
        v = load(y)
        t = clips.times(v, clips.valid)
        t = t + clips.times(roll_rows(v, 1), clips.before)
        t = t + clips.times(roll_rows(v, -1), clips.after)
        tx[y + 1] = t + shift_places(t, frames, 1) + shift_places(t, frames, -1)

    def down(y):
        store(y, tx[y] + tx[y + 1] + tx[y + 2])

    loop(side, across)
    loop(side, down)


def pool_forward(clips, side, load, tx, zp, acc):
    def store(y, v):
        z = clips.times(v * inv_edges(side, clips.frames, y), clips.inv)
        zp[y] = z
        add_stats(clips, acc, pl.ds(256, 128), z)

    box(clips, side, load, tx, store)


def upright(src, dst):
    rows = src.shape[1]
    width = src.shape[0]

    def body(i):
        at = pl.ds(pl.multiple_of(i * 128, 128), 128)
        dst[at, 0:width] = src[:, at].astype(F32).T.astype(BF16)

    loop(rows // 128, body)
    if rows % 128:
        at = slice(rows - rows % 128, rows)
        dst[at, 0:width] = src[:, at].astype(F32).T.astype(BF16)


def arrange_first(src, wp, b, flip):
    one, mid_in, small_in, pool = src
    wp[b, :, 0:256] = one[...]
    wp[b, :, 256:384] = pool[...]
    upright(mid_in, flip)
    wp[b, :, 384:544] = flip[0:D, 0:C1A]
    upright(small_in, flip)
    wp[b, :, 544:576] = flip[0:D, 0:C2A]
    wp[b, :, 576:640] = jnp.zeros((D, 64), BF16)


def arrange_beta(src, dst):
    v = jnp.concatenate([jnp.broadcast_to(src[...], (8, 1024)), jnp.zeros((8, 128), F32)], 1)
    lane = lax.broadcasted_iota(jnp.int32, v.shape, 1)
    out = jnp.zeros_like(v)
    for lo, hi, by in (
        (0, 256, 0),
        (256, 576, -160),
        (576, 832, -192),
        (896, 1056, 640),
        (1056, 1088, 320),
    ):
        out = jnp.where((lane >= lo) & (lane < hi), roll_lanes(v, by), out)
    dst[...] = out[0:1]


def arrange_conv(mid_flat, small, wf, ws, b, mid):
    upright(mid_flat, mid)
    for dy in range(3):
        wf[b, 512 * dy + 480 : 512 * dy + 512, :] = jnp.zeros((32, 1024), BF16)
        ws[b, 128 * dy + 96 : 128 * dy + 128, :] = jnp.zeros((32, 384), BF16)
        wf[b, 512 * dy : 512 * dy + 512, 960:1024] = jnp.zeros((512, 64), BF16)
        for dt in range(3):
            for dx in range(3):
                r = 96 * (3 * dt + dy) + 32 * dx
                to = 128 * dy + 32 * dt
                ws[b, to : to + 32, 128 * dx : 128 * dx + 128] = small[r : r + 32, :]
            for dx in range(3):
                r = 480 * (3 * dt + dy) + 160 * dx
                for rows, to in ((128, 128 * dt), (32, 384 + 32 * dt)):
                    to = to + 512 * dy
                    wf[b, to : to + rows, 256 * dx : 256 * dx + 256] = mid[r : r + rows, 0:256]
                    wf[b, to : to + rows, 768 + 64 * dx : 832 + 64 * dx] = mid[
                        r : r + rows, 256:320
                    ]
                    r = r + rows


def start_kernel(
    len_ref, x, og, w_one, w_mid_in, w_small_in, w_pool, w_mid, w_small, bn,
    xgot_out, zone_out, zin_out, zp_out, st, wp1, wp2, wf1, wf2, ws1, ws2, beta1, beta2, og_got,
    x_own, x_got, zone, zin, zp, yp, tx,
    own_one, own_mid_in, own_small_in, own_pool, own_mid, own_small,
    got_one, got_mid_in, got_small_in, got_pool, got_mid, got_small, beta, got_beta, flip,
    wp, wf, ws, hacc, acc, loc, buf, ssem, rsem, lsem, osem, psem, qsem,
):
    greet(partner=True)
    sec = lax.axis_index("section")
    side = zone.shape[0]
    clips = Clips(len_ref, 16, 1)
    raw = (w_one, w_mid_in, w_small_in, w_pool, w_mid, w_small)
    own = (own_one, own_mid_in, own_small_in, own_pool, own_mid, own_small)
    got = (got_one, got_mid_in, got_small_in, got_pool, got_mid, got_small)
    local = [pltpu.make_async_copy(x.at[sec], x_own, lsem.at[0])]
    local += [
        pltpu.make_async_copy(a.at[0], b, lsem.at[i + 1]) for i, (a, b) in enumerate(zip(raw, own))
    ]
    for c in local:
        c.start()
    hacc[...] = jnp.zeros_like(hacc)
    acc[...] = jnp.zeros_like(acc)
    loc[...] = jnp.zeros_like(loc)
    arrange_beta(bn, beta)
    greeted(partner=True)
    pairs = [(a.at[0], b) for a, b in zip(raw[:4], got[:4])]
    pairs += [(beta, got_beta), (x.at[1 - sec], x_got)]
    pairs += [(a.at[0], b) for a, b in zip(raw[4:], got[4:])]
    pairs += [(og.at[1 - sec], og_got)]
    remote = [swap_copy(a, b, psem.at[i], qsem.at[i]) for i, (a, b) in enumerate(pairs)]
    for c in remote:
        c.start()
    for c in local[1:]:
        c.wait()
    arrange_first(own[:4], wp, sec, flip)
    arrange_conv(own_mid, own_small, wf, ws, sec, flip)
    for c in remote[:5]:
        c.wait()
    arrange_first(got[:4], wp, 1 - sec, flip)
    beta1[...] = jnp.where(sec == 0, beta[...], got_beta[...])
    beta2[...] = jnp.where(sec == 0, got_beta[...], beta[...])
    ny = side // 2
    rows = ny * side * 8
    outs = []

    def put(src, dst):
        c = pltpu.make_async_copy(src, dst, osem.at[len(outs)])
        c.start()
        outs.append(c)

    for part, src in enumerate((x_own, x_got)):
        (local[0] if part == 0 else remote[5]).wait()
        half = sec if part == 0 else 1 - sec

        def body(i, src=src, half=half):
            here = pl.ds(i * ny, ny)
            y = dot(src[pl.ds(pl.multiple_of(i * rows, 16), rows)], wp[0])

            def place(lo, hi):
                return y[:, lo:hi].reshape(ny, side, 8, hi - lo)

            zone[here, :, half] = place(0, 256)
            yp[here, :, half] = place(256, 384)
            zin[here, :, half] = place(384, 640)
            for lo, hi in ((0, 256), (384, 640)):
                v = y[:, lo:hi].reshape(-1, 8, 256)
                hacc[0, half, :, lo:hi] += jnp.sum(v, axis=0)
                hacc[1, half, :, lo:hi] += jnp.sum(v * v, axis=0)

        loop(2, body)
    put(x_got, xgot_out)
    put(zin, zin_out)
    put(zone, zone_out)
    acc[...] = hacc[...].reshape(acc.shape)
    pool_forward(clips, side, lambda y: yp[y].reshape(side * 16, 128), tx, zp, acc)
    put(zp, zp_out)
    pack_stats(clips, loc, acc, side * side)
    exchange_start(loc, buf, ssem, rsem)
    for c in remote[6:]:
        c.wait()
    arrange_conv(got_mid, got_small, wf, ws, 1 - sec, flip)
    for a, b in ((wf, (wf1, wf2)), (ws, (ws1, ws2)), (wp, (wp1, wp2))):
        for i in range(2):
            put(a.at[i], b[i])
    exchange_finish(loc, buf, ssem, rsem, st)
    for c in outs:
        c.wait()


def inner_tiles(clips, z, st, beta):
    tiles = []
    for t in range(2):
        scale, mean = affine(st, pl.ds(384 + 128 * t, 128))
        b = beta[0:1, pl.ds(896 + 128 * t, 128)]
        act, _ = soft(z[:, 128 * t : 128 * (t + 1)] * scale + (b - mean * scale))
        tiles.append(clips.times(act, clips.valid))
    return tiles


def tap_tiles(clips, a, b):
    def before(v):
        return clips.times(roll_rows(v, 1), clips.before)

    def after(v):
        return clips.times(roll_rows(v, -1), clips.after)

    lane = lax.broadcasted_iota(jnp.int32, b.shape, 1)
    ones = clips.times(jnp.where(lane == 96, 1.0, 0.0).astype(F32), clips.valid)

    def three32(v):
        return before(v) + roll_lanes(v, 32) + roll_lanes(after(v), 64) + ones

    tail = lane_below(b, 32)
    small = lane_below(roll_lanes(b, -32), 32)
    return [before(a), a, after(a), three32(tail)], three32(small)


def untap(clips, parts, small):
    def before(v):
        return roll_rows(clips.times(v, clips.before), -1)

    def after(v):
        return roll_rows(clips.times(v, clips.after), 1)

    def back32(v):
        return (
            lane_below(before(v), 32)
            + lane_below(roll_lanes(v, -32), 32)
            + lane_below(roll_lanes(after(v), -64), 32)
        )

    a = before(parts[0]) + parts[1] + after(parts[2])
    return a, back32(parts[3]) + roll_lanes(back32(small), 32)


def typical(beta):
    sp, sg = soft(jnp.broadcast_to(beta, (8, beta.shape[-1])))
    return sp + 0.5 * sg * (1.0 - sg)


def outer(c, s):
    k = lax.broadcasted_iota(jnp.int32, c.shape, 0)
    c = jnp.where(k < 2, c, 0.0).astype(BF16)
    s = jnp.broadcast_to(s, (8, s.shape[-1]))
    high = s.astype(BF16).astype(F32)
    k = lax.broadcasted_iota(jnp.int32, s.shape, 0)
    s = jnp.where(k == 0, high, jnp.where(k == 1, s - high, 0.0)).astype(BF16)
    return dot_tn(c, s)


def tap_points(beta):
    a = typical(beta[0:1, 896:1024])
    b = typical(beta[0:1, 1024:1152])

    def three(v):
        return v + roll_lanes(v, 32) + roll_lanes(v, 64)

    tail = three(lane_below(b, 32))
    small = three(lane_below(roll_lanes(b, -32), 32))
    return jnp.concatenate([a, a, a, tail], 1), small


def centre_mid(grad, beta):
    c, _ = tap_points(beta)
    row = jnp.broadcast_to(grad[992:993, :], (8, 1024))
    main = row[:, 256:512]
    tail = lane_below(roll_lanes(row[:, 768:896], 64), 64)
    s = jnp.concatenate([main, main, main, tail + roll_lanes(tail, 64), tail], 1)
    return outer(c, s)


def centre_small(grad, beta):
    _, c = tap_points(beta)
    row = jnp.broadcast_to(grad[224:225, 128:256], (8, 128))
    return outer(c, jnp.concatenate([row, row, row], 1))


def conv_gather(frames, p, s):
    def three(at):
        return (
            shift_places(at(0), frames, -1) + at(1) + shift_places(at(2), frames, 1)
        )

    main = three(lambda k: p[:, 256 * k : 256 * k + 256])
    small = three(lambda k: s[:, 128 * k : 128 * k + 128])
    ends = p[:, 768:896]
    tail = three(lambda k: (ends, roll_lanes(ends, 64), p[:, 896:1024])[k])
    return main, small, lane_below(tail, 64)


def spread_x(frames, v, by):
    return v if by == 0 else shift_places(v, frames, -by)


def put_spread(frames, main, small, tail, put_mid, put_small):
    for k in range(3):
        put_mid(256 * k, spread_x(frames, main, k - 1))
        put_small(128 * k, spread_x(frames, small, k - 1))
    put_mid(768, spread_x(frames, tail, -1) + roll_lanes(tail, 64))
    put_mid(896, spread_x(frames, tail, 1))


def join_final(small, tail, pool):
    s, p = roll_lanes(small, 64), roll_lanes(pool, 64)
    low = lax.broadcasted_iota(jnp.int32, small.shape, 1) < 64
    return jnp.where(low, tail, s), jnp.where(low, s, p), jnp.where(low, p, 0.0)


def split_final(t4, t5, t6):
    a, b, c = roll_lanes(t4, 64), roll_lanes(t5, 64), roll_lanes(t6, 64)
    low = lax.broadcasted_iota(jnp.int32, t4.shape, 1) < 64
    return jnp.where(low, a, b), jnp.where(low, t4, 0.0), jnp.where(low, b, c)


def final_stats(st1, st2, stf):
    stf[:, 0:256] = st1[:, 0:256]
    stf[:, 256:512] = st2[:, 0:256]
    for t, v in enumerate(join_final(st2[:, 256:384], st2[:, 384:512], st1[:, 256:384])):
        stf[:, 512 + 128 * t : 640 + 128 * t] = v
    stf[2:3, :] = jnp.broadcast_to(st1[2:3, 0:1], (1, DP))


def store_conv(clips, y, p, s, zp, zf, acc):
    main, small, tail = conv_gather(clips.frames, p, s)
    zf[y, :, 256:512] = main
    for t, v in enumerate(join_final(small, tail, zp[y])):
        zf[y, :, 512 + 128 * t : 640 + 128 * t] = v
    add_stats(clips, acc, pl.ds(0, 256), main)
    add_stats(clips, acc, pl.ds(256, 128), small)
    add_stats(clips, acc, pl.ds(384, 128), tail)


def conv_kernel(
    len_ref, zin, zone, zp, st1, beta, wf, ws, cat, scat, zf, stf, st2, acc, loc, buf, ssem, rsem
):
    greet()
    side, rows = zin.shape[0], zin.shape[1]
    clips = Clips(len_ref, 16, 1)
    acc[...] = jnp.zeros_like(acc)
    loc[...] = jnp.zeros_like(loc)
    for y in (0, side + 1):
        cat[y] = jnp.zeros(cat.shape[1:], BF16)
        scat[y] = jnp.zeros(scat.shape[1:], BF16)

    def build(y):
        a, b = inner_tiles(clips, zin[y], st1, beta)
        parts, small = tap_tiles(clips, a, b)
        for i, part in enumerate(parts):
            cat[y + 1, :, 128 * i : 128 * i + 128] = part.astype(BF16)
        scat[y + 1] = small.astype(BF16)

    loop(side, build)
    ny = 2

    def products(i):
        y0 = i * ny

        def taps(ref):
            return jnp.concatenate(
                [ref[pl.ds(y0 + dy, ny)].reshape(ny * rows, ref.shape[-1]) for dy in range(3)], axis=1
            )

        p = dot(taps(cat), wf[...])
        s = dot(taps(scat), ws[...])
        for q in range(ny):
            here = slice(q * rows, (q + 1) * rows)
            store_conv(clips, y0 + q, p[here], s[here], zp, zf, acc)

    loop(side // ny, products)
    pack_stats(clips, loc, acc)
    greeted()
    exchange_start(loc, buf, ssem, rsem)

    def move(y):
        zf[y, :, 0:256] = zone[y]

    loop(side, move)
    exchange_finish(loc, buf, ssem, rsem, st2)
    final_stats(st1, st2, stf)


def output_kernel(len_ref, zf, stf, beta, sig, hand, asum, bsum, scr):
    side = zf.shape[0]
    half = side // 2
    clips = Clips(len_ref, 16, 1)

    def body(k):
        for t in range(7):
            lanes = pl.ds(128 * t, 128)
            scale, mean = affine(stf, lanes)
            b = beta[0:1, lanes]
            pooled = None
            for q in range(2):
                u = (zf[2 * k + q, :, lanes] - mean) * scale
                sp, sg = soft(u + b)
                sp, sg = clips.times(sp, clips.valid), clips.times(sg, clips.valid)
                if t == 6:
                    lane = lax.broadcasted_iota(jnp.int32, sp.shape, 1)
                    one = clips.times(jnp.ones_like(sp), clips.valid)
                    sp = jnp.where(lane == 127, one, lane_below(sp, 64))
                    sg = lane_below(sg, 64)
                sig[2 * k + q, :, lanes] = sg.astype(BF16)
                three = [
                    jnp.sum(v.reshape(half, 2, 16, 128), axis=1) for v in (sp, sg, sg * u)
                ]
                pooled = three if pooled is None else [x + y for x, y in zip(pooled, three)]
            for v, dst in zip(pooled, (hand, asum, bsum)):
                scr[...] = v
                dst[k, :, :, lanes] = (
                    scr[:, pl.ds(0, 8, stride=2), :] + scr[:, pl.ds(1, 8, stride=2), :]
                ) * 0.125

    loop(half, body)


def second_kernel(
    len_ref, hand, asum, bsum, og, og_got, wp, wf, ws, beta, beta1,
    block_out, hg, packed, sums5, sums6, sums7,
    gown, grad, out, lsem, psem, qsem,
    hbuf, zin, zp, zf, stf, yp, tx, catf, cat, scat, pbuf, sbuf, dbuf, dzc, dzs, dz1, din,
    acc, st3, st4, acc7, accm, accs, accp,
    loc3, buf3, ss3, rs3, loc4, buf4, ss4, rs4, loc5, buf5, ss5, rs5,
    loc6, buf6, ss6, rs6, loc7, buf7, ss7, rs7,
):
    greet(partner=True)
    sec = lax.axis_index("section")
    own = pltpu.make_async_copy(og.at[sec], gown, lsem.at[0])
    own.start()
    side = hand.shape[0]
    rows = side * 8
    total = side * rows
    clips = Clips(len_ref, 8, 2)
    for ref in (acc, acc7, loc3, loc4, loc5, loc6, loc7):
        ref[...] = jnp.zeros_like(ref)

    hbuf[...] = hand[...].reshape(total, DP).astype(BF16)
    y = dot(hbuf[:, 0:D], wp[...])
    zf[:, :, 0:C0] = y[:, 0:C0].reshape(side, rows, C0)
    yp[...] = y[:, 256:384].reshape(side, rows, 128)
    zin[...] = y[:, 384:640].reshape(side, rows, 256)

    def first_sums(y):
        add_stats(clips, acc, pl.ds(0, 256), zf[y, :, 0:256])
        add_stats(clips, acc, pl.ds(384, 256), zin[y])

    loop(side, first_sums)
    pool_forward(clips, side, lambda y: yp[y], tx, zp, acc)
    pack_stats(clips, loc3, acc, side * side)
    greeted(partner=True)
    exchange_start(loc3, buf3, ss3, rs3)
    own.wait()
    mine, theirs = gown[...].astype(F32), og_got[...].astype(F32)
    low = jnp.where(sec == 0, mine, theirs)
    high = jnp.where(sec == 0, theirs, mine)
    grad[...] = jnp.concatenate([low, high], 2)
    exchange_finish(loc3, buf3, ss3, rs3, st3)

    catf[0] = jnp.zeros(catf.shape[1:], F32)
    catf[side + 1] = jnp.zeros(catf.shape[1:], F32)

    def build(y):
        a, b = inner_tiles(clips, zin[y], st3, beta)
        parts, small = tap_tiles(clips, a, b)
        for t, v in enumerate(parts + [small]):
            catf[y + 1, :, 128 * t : 128 * t + 128] = v

    loop(side, build)
    for dy in range(3):
        v = catf[dy : dy + side].reshape(total, 640).astype(BF16)
        cat[:, 512 * dy : 512 * dy + 512] = v[:, 0:512]
        scat[:, 128 * dy : 128 * dy + 128] = v[:, 512:640]
    pbuf[...] = dot(cat[...], wf[...]).reshape(side, rows, 1024)
    sbuf[...] = dot(scat[...], ws[...]).reshape(side, rows, 384)
    acc[...] = jnp.zeros_like(acc)
    loop(side, lambda y: store_conv(clips, y, pbuf[y], sbuf[y], zp, zf, acc))
    pack_stats(clips, loc4, acc)
    exchange(loc4, buf4, ss4, rs4, st4)
    final_stats(st3, st4, stf)

    def emit(y):
        for t in range(7):
            lanes = pl.ds(128 * t, 128)
            scale, mean = affine(stf, lanes)
            u = (zf[y, :, lanes] - mean) * scale
            sp, sg = soft(u + beta[0:1, lanes])
            width = 128 if t < 6 else 64
            gr = grad[y, :, :, 128 * t : 128 * t + width].reshape(rows, width)
            if t == 6:
                gr = jnp.concatenate([gr, jnp.zeros((rows, 64), F32)], 1)
            d = gr * clips.times(sg, clips.valid)
            dbuf[y, :, lanes] = d
            add_stats(clips, acc7, lanes, d, u)
            sp = clips.times(sp, clips.valid).reshape(side, 8, 128)[:, :, 0:width]
            for h in range(2):
                out[h, y, :, :, 128 * t : 128 * t + width] = sp[:, 4 * h : 4 * h + 4].astype(BF16)

    loop(side, emit)
    mine = pltpu.make_async_copy(out.at[sec], block_out.at[sec], lsem.at[1])
    mine.start()
    theirs = swap_copy(out.at[1 - sec], block_out.at[sec], psem, qsem)
    theirs.start()
    pack_stats(clips, loc5, acc7)
    exchange(loc5, buf5, ss5, rs5, sums5)
    count = st3[2:3, 0:128]

    def dz_of(y, t):
        lanes = pl.ds(128 * t, 128)
        scale, mean = affine(stf, lanes)
        u = (zf[y, :, lanes] - mean) * scale
        m1, m2 = sums5[0:1, lanes] / count, sums5[1:2, lanes] / count
        return clips.times((dbuf[y, :, lanes] - m1 - u * m2) * scale, clips.valid)

    def dz_final(y):
        for t in range(2):
            dz1[y, :, 128 * t : 128 * t + 128] = dz_of(y, t)
        main = jnp.concatenate([dz_of(y, 2), dz_of(y, 3)], 1)
        small, tail, pool = split_final(*(dz_of(y, t) for t in (4, 5, 6)))
        yp[y] = clips.times(pool * inv_edges(side, 8, y), clips.inv)

        def put(ref):
            def go(lane, v):
                ref[y, :, lane : lane + v.shape[-1]] = v

            return go

        put_spread(8, main, small, tail, put(dzc), put(dzs))

    loop(side, dz_final)

    def boxed(y, v):
        dz1[y, :, 256:384] = clips.times(v, clips.valid)

    box(clips, side, lambda y: yp[y], tx, boxed)
    dzc_b = dzc[...].reshape(total, 1024).astype(BF16)
    dzs_b = dzs[...].reshape(total, 384).astype(BF16)
    for dy in (-1, 0, 1):
        k = dy + 1
        q = dot_nt(dzc_b, wf[512 * k : 512 * k + 512]).reshape(side, rows, 512)
        r = dot_nt(dzs_b, ws[128 * k : 128 * k + 128]).reshape(side, rows, 128)
        if k == 0:
            catf[1 : side + 1] = jnp.zeros((side, rows, 640), F32)
        catf[1 + dy : 1 + dy + side, :, 0:512] += q
        catf[1 + dy : 1 + dy + side, :, 512:640] += r
    acc[...] = jnp.zeros_like(acc)

    def inner_back(y):
        parts = [catf[y + 1, :, 128 * t : 128 * t + 128] for t in range(5)]
        inner_up(clips, zin[y], untap(clips, parts[:4], parts[4]), st3, beta, acc, din, y)

    loop(side, inner_back)
    pack_stats(clips, loc6, acc)
    exchange_start(loc6, buf6, ss6, rs6)
    accm[...] = dot_tn(cat[...], dzc_b)
    exchange_finish(loc6, buf6, ss6, rs6, sums6)

    def dz_inner(y):
        for t in range(2):
            dz1[y, :, 384 + 128 * t : 512 + 128 * t] = inner_dz(
                clips, t, zin[y], din[y], st3, sums6, count
            )

    loop(side, dz_inner)
    dz1_b = dz1[...].reshape(total, 640).astype(BF16)
    hgv = dot_nt(dz1_b, wp[...]).astype(BF16).astype(F32)
    hg[:, :, :, 0:D] = hgv.reshape(side, side, 8, D)
    hg[:, :, :, D:DP] = jnp.zeros((side, side, 8, DP - D), F32)
    acc7[...] = jnp.zeros_like(acc7)

    def upstream(y):
        for t in range(7):
            lanes = pl.ds(128 * t, 128)
            gr = hg[y, :, :, lanes]
            acc7[0, :, lanes] += jnp.sum(gr * asum[y, :, :, lanes], axis=0)
            acc7[1, :, lanes] += jnp.sum(gr * bsum[y, :, :, lanes], axis=0)

    loop(side, upstream)
    pack_stats(clips, loc7, acc7)
    exchange_start(loc7, buf7, ss7, rs7)
    accs[...] = dot_tn(scat[...], dzs_b)
    accp[...] = dot_tn(hbuf[...], dz1_b)
    pool = dz1[:, :, 256:384].reshape(total, 128)
    rest = (pool - dz1_b[:, 256:384].astype(F32)).astype(BF16)
    accp[:, 256:384] += dot_tn(hbuf[...], rest)
    c = jnp.concatenate([typical(beta1[0:1, 0:D]), jnp.zeros((8, DP - D), F32)], 1)
    full = accp[...] - outer(c, accp[DP - 1 : DP, :])
    pack_grads(packed, accm, accs, beta, lambda t: full[0:D, 128 * t : 128 * t + 128])
    exchange_finish(loc7, buf7, ss7, rs7, sums7)
    mine.wait()
    theirs.wait()


def pack_grads(packed, accm, accs, beta, first):
    mid = centre_mid(accm, beta)
    small = centre_small(accs, beta)
    end = packed.shape[1]
    for t in range(8):
        lanes = slice(128 * t, 128 * t + 128)
        for k in range(3):
            packed[t, 480 * k : 480 * k + 480] = (
                accm[512 * k : 512 * k + 480, lanes] - mid[0:480, lanes]
            ).astype(BF16)
        if t < 5:
            if first is not None:
                packed[t, 1440 : 1440 + D] = first(t).astype(BF16)
        else:
            lanes = slice(128 * (t - 5), 128 * (t - 5) + 128)
            for k in range(3):
                packed[t, 1440 + 128 * k : 1568 + 128 * k] = (
                    accs[128 * k : 128 * k + 128, lanes] - small[:, lanes]
                ).astype(BF16)
            packed[t, 1824 : 1440 + D] = jnp.zeros((D - 384, 128), BF16)
        packed[t, 1440 + D : end] = jnp.zeros((end - 1440 - D, 128), BF16)


def inner_up(clips, z, backs, st, beta, acc, din, y):
    for t in range(2):
        lanes = pl.ds(384 + 128 * t, 128)
        scale, mean = affine(st, lanes)
        u = (z[:, 128 * t : 128 * t + 128] - mean) * scale
        d = backs[t] * clips.times(sigm(u + beta[0:1, pl.ds(896 + 128 * t, 128)]), clips.valid)
        din[y, :, 128 * t : 128 * t + 128] = d
        add_stats(clips, acc, lanes, d, u)


def inner_dz(clips, t, z, d, st, sums, count):
    lanes = pl.ds(384 + 128 * t, 128)
    here = slice(128 * t, 128 * t + 128)
    scale, mean = affine(st, lanes)
    u = (z[:, here] - mean) * scale
    m1, m2 = sums[0:1, lanes] / count, sums[1:2, lanes] / count
    dz = clips.times((d[:, here] - m1 - u * m2) * scale, clips.valid)
    return lane_below(dz, 64) if t == 1 else dz


def put_halves(ref, y, lane, v):
    side, lanes = v.shape[0] // 16, v.shape[1]
    v = v.reshape(side, 2, 8, lanes)
    for h in range(2):
        ref[h, y, :, lane : lane + lanes] = v[:, h].reshape(side * 8, lanes).astype(BF16)


def dz_kernel(len_ref, zf, sig, hg, stf, sums7, dzc, dzs, dz1, scr, yp, tx):
    side = zf.shape[0]
    half = side // 2
    rows = side * 16
    clips = Clips(len_ref, 16, 1)
    count = stf[2:3, 0:128]
    for y in (0, side + 1):
        dzc[y] = jnp.zeros(dzc.shape[1:], BF16)
        dzs[y] = jnp.zeros(dzs.shape[1:], BF16)

    def body(k):
        tiles = ([], [])
        for t in range(7):
            lanes = pl.ds(128 * t, 128)
            scale, mean = affine(stf, lanes)
            m1, m2 = sums7[0:1, lanes] / count, sums7[1:2, lanes] / count
            gr = hg[k, :, :, lanes] * 0.125
            scr[:, pl.ds(0, 8, stride=2), :] = gr
            scr[:, pl.ds(1, 8, stride=2), :] = gr
            gr = scr[...]
            gr = jnp.broadcast_to(gr[:, None], (half, 2, 16, 128)).reshape(rows, 128)
            for q in range(2):
                y = 2 * k + q
                u = (zf[y, :, lanes] - mean) * scale
                d = gr * sig[y, :, lanes].astype(F32)
                dz = clips.times((d - m1 - u * m2) * scale, clips.valid)
                if t < 2:
                    put_halves(dz1, y, 128 * t, dz)
                else:
                    tiles[q].append(dz)
        for q in range(2):
            y = 2 * k + q
            small, tail, pool = split_final(*tiles[q][2:])
            yp[y] = clips.times(pool * inv_edges(side, 16, y), clips.inv)

            def put(ref, y=y):
                def go(lane, v):
                    ref[y + 1, :, lane : lane + v.shape[-1]] = v.astype(BF16)

                return go

            put_spread(
                16, jnp.concatenate(tiles[q][:2], 1), small, tail, put(dzc), put(dzs)
            )

    loop(half, body)

    def boxed(y, v):
        put_halves(dz1, y, 256, clips.times(v, clips.valid))

    box(clips, side, lambda y: yp[y], tx, boxed)


def conv_grad_kernel(cat, scat, dzc, dzs, beta, packed, acc, accs):
    side = cat.shape[0] - 2
    rows = cat.shape[1]
    ny = 7
    acc[...] = jnp.zeros_like(acc)
    accs[...] = jnp.zeros_like(accs)

    def body(i):
        y0 = i * ny + 1

        def take(ref, y):
            return ref[pl.ds(y, ny)].reshape(ny * rows, ref.shape[-1])

        a, s = take(cat, y0), take(scat, y0)
        for dy in (-1, 0, 1):
            k = dy + 1
            acc[512 * k : 512 * k + 512] += dot_tn(a, take(dzc, y0 - dy))
            accs[128 * k : 128 * k + 128] += dot_tn(s, take(dzs, y0 - dy))

    loop(side // ny, body)
    pack_grads(packed, acc, accs, beta, None)


def conv_back_kernel(
    len_ref, dzc, dzs, wf, ws, zin, st1, beta, dzi, sums8, din, acc, loc, buf, ssem, rsem
):
    greet()
    side, rows = zin.shape[0], zin.shape[1]
    clips = Clips(len_ref, 16, 1)
    acc[...] = jnp.zeros_like(acc)
    loc[...] = jnp.zeros_like(loc)
    ny = 2

    def body(i):
        y0 = i * ny + 1
        q = s = None
        for dy in (-1, 0, 1):
            k = dy + 1
            here = pl.ds(y0 - dy, ny)
            t = dot_nt(dzc[here].reshape(ny * rows, 1024), wf[512 * k : 512 * k + 512])
            q = t if q is None else q + t
            t = dot_nt(dzs[here].reshape(ny * rows, 384), ws[128 * k : 128 * k + 128])
            s = t if s is None else s + t
        for j in range(ny):
            y = i * ny + j
            here = slice(j * rows, (j + 1) * rows)
            parts = [q[here, 128 * t : 128 * t + 128] for t in range(4)]
            inner_up(clips, zin[y], untap(clips, parts, s[here]), st1, beta, acc, din, y)

    loop(side // ny, body)
    pack_stats(clips, loc, acc)
    greeted()
    exchange(loc, buf, ssem, rsem, sums8)
    count = st1[2:3, 0:128]

    def dz(y):
        for t in range(2):
            put_halves(dzi, y, 128 * t, inner_dz(clips, t, zin[y], din[y], st1, sums8, count))

    loop(side, dz)


def input_kernel(
    x, x_got, dz1, dzi, wp, packed_in, gin, packed,
    x_own, near, far, acc, lsem, psem, qsem,
):
    greet_core()
    sec = lax.axis_index("section")
    own = pltpu.make_async_copy(x.at[sec], x_own, lsem.at[0])
    own.start()
    keep = pltpu.make_async_copy(packed_in, packed, lsem.at[1])
    keep.start()
    side = dz1.shape[1]
    rows = dz1.shape[2]
    ny = 7
    acc[...] = jnp.zeros_like(acc)
    for src, dst, half in ((x_got, far, 1 - sec), (x_own, near, sec)):

        def body(i, src=src, dst=dst, half=half):
            here = pl.ds(i * ny, ny)
            d = jnp.concatenate([dz1[half, here], dzi[half, here]], -1).reshape(ny * rows, 640)
            at = pl.ds(pl.multiple_of(i * ny * rows, 16), ny * rows)
            dst[at] = dot_nt(d, wp[...]).astype(BF16)
            acc[...] += dot_tn(src[at], d)

        if src is x_own:
            own.wait()
        loop(side // ny, body)
        if src is x_got:
            greeted_core()
            send = swap_copy(far, gin.at[sec], psem, qsem)
            send.start()
    mine = pltpu.make_async_copy(near, gin.at[sec], lsem.at[0])
    mine.start()
    keep.wait()
    for t in range(5):
        packed[t, 1440 : 1440 + D] = acc[:, 128 * t : 128 * t + 128].astype(BF16)
    mine.wait()
    send.wait()


def greet_core():
    pl.semaphore_signal(
        pltpu.get_barrier_semaphore(),
        inc=1,
        device_id={"section": 1 - lax.axis_index("section")},
        device_id_type=MESH,
    )


def greeted_core():
    pl.semaphore_wait(pltpu.get_barrier_semaphore(), 1)


def bit_of(me, k):
    return lax.rem(me // (1 << k), 2)


class Reducer:
    def __init__(self, q, land, ssem, rsem, ready, order, base):
        self.q, self.land, self.ssem, self.rsem, self.ready = q, land, ssem, rsem, ready
        self.order, self.base = order, base
        me = lax.axis_index("dp")
        self.steps = []
        tiles, rows = q.shape[0], q.shape[1]
        t0, r0 = 0, 0
        for i, k in enumerate(order):
            bit = bit_of(me, k)
            partner = me + (1 - 2 * bit) * (1 << k)
            if tiles > 1:
                tiles //= 2
                keep, send = (t0 + bit * tiles, r0), (t0 + (1 - bit) * tiles, r0)
            else:
                rows //= 2
                keep, send = (t0, r0 + bit * rows), (t0, r0 + (1 - bit) * rows)
            t0, r0 = keep
            self.steps.append((partner, keep, send, tiles, rows))

    def region(self, at, tiles, rows):
        t, r = at
        if not isinstance(r, int):
            r = pl.multiple_of(r, 16)
        return self.q.at[pl.ds(t, tiles), pl.ds(r, rows)]

    def copy(self, src, dst, sem, partner):
        return pltpu.make_async_remote_copy(
            src_ref=src,
            dst_ref=dst,
            send_sem=self.ssem.at[self.base + sem],
            recv_sem=self.rsem.at[self.base + sem],
            device_id={"dp": partner},
            device_id_type=MESH,
        )

    def halve(self, i):
        partner, keep, send, tiles, rows = self.steps[i]
        return self.copy(self.region(send, tiles, rows), self.land[i], i, partner)

    def add(self, i):
        partner, keep, send, tiles, rows = self.steps[i]
        q, land = self.region(keep, tiles, rows), self.land[i]
        chunk = 96 if rows % 96 == 0 else 16
        parts = rows // chunk

        def body(j):
            t, r = j // parts, pl.multiple_of(lax.rem(j, parts) * chunk, 16)
            at = pl.ds(r, chunk)
            q[t, at] = (q[t, at].astype(F32) + land[t, at].astype(F32)).astype(BF16)

        loop(tiles * parts, body)

    def free(self, i):
        pl.semaphore_signal(
            self.ready.at[self.base // 2 + i],
            inc=1,
            device_id={"dp": self.steps[i][0]},
            device_id_type=MESH,
        )

    def await_free(self, i):
        pl.semaphore_wait(self.ready.at[self.base // 2 + i], 1)

    def double(self, i):
        partner, keep, send, tiles, rows = self.steps[i]
        q = self.region(keep, tiles, rows)
        return self.copy(q, q, len(self.steps) + i, partner)


def land_shapes(tiles, rows, bits):
    out = []
    for _ in range(bits):
        if tiles > 1:
            tiles //= 2
        else:
            rows //= 2
        out.append((tiles, rows, 128))
    return out


def orders(bits):
    plain = list(range(bits))
    swapped = plain[:]
    if bits > 1:
        swapped[0], swapped[1] = 1, 0
    return plain, swapped


def reduce_kernel(bits, packed1, packed2, s5, s6, s7, s8, full, offs, *scratch):
    n = bits
    q = scratch[0:2]
    core_land = scratch[2:4]
    land = (scratch[4 : 4 + n], scratch[4 + n : 4 + 2 * n])
    sums, sums_got, csend, crecv, ssem, rsem, lsem, ready = scratch[4 + 2 * n :]
    sec = lax.axis_index("section")
    me = lax.axis_index("dp")
    barrier = pltpu.get_barrier_semaphore()
    greet_core()
    for k in range(n):
        partner = me + (1 - 2 * bit_of(me, k)) * (1 << k)
        pl.semaphore_signal(barrier, inc=1, device_id={"dp": partner}, device_id_type=MESH)
    half = q[0].shape[1]
    packed = (packed1, packed2)
    mine = []
    for b in range(2):
        src = packed[b].at[:, pl.ds(pl.multiple_of(sec * half, 16), half)]
        mine.append(pltpu.make_async_copy(src, q[b], lsem.at[b]))
        mine[b].start()
    sums[:, 0:DP] = jnp.where(sec == 0, s5[...], s7[...])
    sums[:, DP : DP + 640] = jnp.where(sec == 0, s6[...], s8[...])
    pl.semaphore_wait(barrier, n + 1)
    swaps = []
    for b in range(2):
        src = packed[b].at[:, pl.ds(pl.multiple_of((1 - sec) * half, 16), half)]
        swaps.append(swap_copy(src, core_land[b], csend.at[b], crecv.at[b]))
        swaps[b].start()
    small = swap_copy(sums, sums_got, csend.at[2], crecv.at[2])
    small.start()

    def core_sum(b):
        swaps[b].wait()
        mine[b].wait()
        chunk = 96 if half % 96 == 0 else 16
        parts = half // chunk

        def body(j):
            t, r = j // parts, pl.multiple_of(lax.rem(j, parts) * chunk, 16)
            at = pl.ds(r, chunk)
            q[b][t, at] = (q[b][t, at].astype(F32) + core_land[b][t, at].astype(F32)).astype(BF16)

        loop(8 * parts, body)

    plain, swapped = orders(n)

    def run(order1, order2):
        red = [
            Reducer(q[0], land[0], ssem, rsem, ready, order1, 0),
            Reducer(q[1], land[1], ssem, rsem, ready, order2, 2 * n),
        ]
        lag = 2
        flight = [None, None]
        for step in range(2 * n + lag + 1):
            for b in range(2):
                i = step - lag * b
                if i < 0 or i > 2 * n:
                    continue
                if i == 0:
                    core_sum(b)
                elif i <= n:
                    flight[b].wait()
                    red[b].free(i - 1)
                    red[b].add(i - 1)
                else:
                    flight[b].wait()
                if i < n:
                    flight[b] = red[b].halve(i)
                elif i < 2 * n:
                    red[b].await_free(2 * n - 1 - i)
                    flight[b] = red[b].double(2 * n - 1 - i)
                if i < 2 * n:
                    flight[b].start()

    pl.when(sec == 0)(lambda: run(plain, swapped))
    pl.when(sec == 1)(lambda: run(swapped, plain))

    def finish(b):
        keep = pltpu.make_async_copy(q[b], full.at[sec], lsem.at[2])
        keep.start()
        last = swap_copy(q[1 - b], full.at[sec], csend.at[3], crecv.at[3])
        last.start()
        keep.wait()
        last.wait()

    pl.when(sec == 0)(lambda: finish(0))
    pl.when(sec == 1)(lambda: finish(1))
    small.wait()
    for lanes, a, b in ((slice(0, DP), s7, s5), (slice(DP, DP + 640), s8, s6)):
        offs[:, lanes] = jnp.where(sec == 0, a[...], b[...]) + sums_got[:, lanes]


def unpack_kernel(full, offs, one, mid_in, mid, small_in, small, pool, offset, buf, nat, sem):
    half = full.shape[2]
    copies = [
        pltpu.make_async_copy(full.at[h], buf.at[:, h * half : (h + 1) * half], sem.at[h])
        for h in range(2)
    ]
    for c in copies:
        c.start()
    v = offs[...]
    lane = lax.broadcasted_iota(jnp.int32, v.shape, 1)
    out = jnp.where(lane < 256, v, 0.0)
    for lo, hi, by in ((256, 416, -1024), (416, 736, 160), (736, 768, -704), (768, 1024, 192)):
        out = jnp.where((lane >= lo) & (lane < hi), roll_lanes(v, by), out)
    offset[...] = out[0:1, 0:1024]
    for c in copies:
        c.wait()

    def take(t, r, rows):
        return buf[t, r : r + rows].astype(F32)

    for dt in range(3):
        for dy in range(3):
            for dx in range(3):
                to = 160 * (9 * dt + 3 * dy + dx)
                for rows, r in ((128, 480 * dy + 128 * dt), (32, 480 * dy + 384 + 32 * dt)):
                    nat[to : to + rows, 0:128] = take(2 * dx, r, rows)
                    nat[to : to + rows, 128:256] = take(2 * dx + 1, r, rows)
                    tail = take(6 + dx // 2, r, rows)
                    nat[to : to + rows, 256:384] = roll_lanes(tail, 64) if dx == 1 else tail
                    to = to + rows
                r = 1440 + 128 * dy + 32 * dt
                to = 32 * (9 * dt + 3 * dy + dx)
                small[to : to + 32, :] = take(5 + dx, r, 32)

    def turn(i):
        at = pl.ds(pl.multiple_of(i * 128, 128), 128)
        mid[0:256, at] = nat[at, 0:256].T
        mid[256:320, at] = nat[at, 256:384].T[0:64]

    total = mid.shape[1]
    loop(total // 128, turn)
    at = slice(total - total % 128, total)
    mid[0:256, at] = nat[at, 0:256].T
    mid[256:320, at] = nat[at, 256:384].T[0:64]
    for r in range(0, D, 128):
        rows = min(128, D - r)
        at = slice(r, r + rows)
        mid_in[0:128, at] = take(3, 1440 + r, rows).T
        last = take(4, 1440 + r, rows).T
        mid_in[128:160, at] = last[0:32]
        small_in[:, at] = last[32:64]
    one[:, 0:128] = take(0, 1440, D)
    one[:, 128:256] = take(1, 1440, D)
    pool[...] = take(2, 1440, D)


def vmem(*shape, dtype=F32):
    return pltpu.VMEM(shape, dtype)


def call(kernel, outs, args, scratch, collective=None, smem_first=True, any_in=(), any_out=()):
    def specs(count, anywhere):
        return [
            pl.BlockSpec(memory_space=pl.ANY if i in anywhere else pltpu.VMEM)
            for i in range(count)
        ]

    in_specs = specs(len(args), any_in)
    if smem_first:
        in_specs[0] = pl.BlockSpec(memory_space=pltpu.SMEM)
    params = {"vmem_limit_bytes": VMEM_LIMIT}
    if collective is not None:
        params.update(collective_id=collective, has_side_effects=True)
    return pl.pallas_call(
        kernel,
        out_shape=[jax.ShapeDtypeStruct(shape, dtype) for shape, dtype in outs],
        in_specs=in_specs,
        out_specs=specs(len(outs), any_out),
        scratch_shapes=scratch,
        compiler_params=pltpu.CompilerParams(**params),
    )(*args)


def on_device(
    clip_input, out_grad, clip_lengths, w_one, w_mid_in, w_mid, w_small_in, w_small, w_pool, bn_offset
):
    n = lax.axis_size("dp")
    bits = n.bit_length() - 1
    half, side = clip_input.shape[1], clip_input.shape[2]
    rows = side * 16
    side2 = side // 2
    rows2 = side2 * 8
    total2 = side2 * rows2
    unit = 32 << max(bits - 3, 0)
    packed_rows = -(-(1440 + D) // unit) * unit
    x = clip_input.transpose(0, 2, 3, 1, 4).reshape(2, side * side * half, D)
    og = out_grad.transpose(0, 2, 3, 1, 4)

    def like(a, dtype=BF16):
        return pltpu.VMEM(a.shape[1:], dtype)

    def turned(w):
        return w.transpose(0, 2, 1)

    weights = (w_one, turned(w_mid_in), turned(w_small_in), w_pool, turned(w_mid), w_small)
    dma = pltpu.SemaphoreType.DMA
    grid = (side, side, 2, 8)
    xgot, zone, zin, zp, st1, wp1, wp2, wf1, wf2, ws1, ws2, beta1, beta2, og_got = call(
        start_kernel,
        [
            (x.shape[1:], BF16),
            (grid + (256,), F32),
            (grid + (256,), F32),
            ((side, rows, 128), F32),
            ((8, 640), F32),
            ((D, 640), BF16),
            ((D, 640), BF16),
            ((1536, 1024), BF16),
            ((1536, 1024), BF16),
            ((384, 384), BF16),
            ((384, 384), BF16),
            ((1, 1152), F32),
            ((1, 1152), F32),
            (og.shape[1:], BF16),
        ],
        (clip_lengths, x, og) + weights + (bn_offset,),
        [
            like(x),
            like(x),
            vmem(*grid, 256),
            vmem(*grid, 256),
            vmem(side, rows, 128),
            vmem(*grid, 128),
            vmem(side + 2, rows, 128),
        ]
        + [like(w) for w in weights] * 2
        + [
            vmem(1, 1152),
            vmem(1, 1152),
            vmem(27 * C1A, 384, dtype=BF16),
            vmem(2, D, 640, dtype=BF16),
            vmem(2, 1536, 1024, dtype=BF16),
            vmem(2, 384, 384, dtype=BF16),
            vmem(2, 2, 8, 640),
            vmem(2, 16, 640),
        ]
        + exchange_scratch(n, 640)
        + [dma((7,)), dma((10,)), dma((9,)), dma((9,))],
        collective=1,
        any_in=range(1, 9),
        any_out=(0, 1, 2, 3, 5, 6, 7, 8, 9, 10, 13),
    )
    zone = zone.reshape(side, rows, 256)
    zin = zin.reshape(side, rows, 256)
    cat, scat, zf, stf = call(
        conv_kernel,
        [
            ((side + 2, rows, 512), BF16),
            ((side + 2, rows, 128), BF16),
            ((side, rows, DP), F32),
            ((8, DP), F32),
        ],
        (clip_lengths, zin, zone, zp, st1, beta1, wf1, ws1),
        [vmem(8, 512), vmem(2, 16, 512)] + exchange_scratch(n, 512),
        collective=2,
    )
    sig, hand, asum, bsum = call(
        output_kernel,
        [((side, rows, DP), BF16)] + [((side2, side2, 8, DP), F32)] * 3,
        (clip_lengths, zf, stf, beta1),
        [vmem(side2, 16, 128)],
    )
    block_output, hg, packed2, sums5, sums6, sums7 = call(
        second_kernel,
        [
            (og.shape, BF16),
            ((side2, side2, 8, DP), F32),
            ((8, packed_rows, 128), BF16),
            ((8, DP), F32),
            ((8, 640), F32),
            ((8, DP), F32),
        ],
        (clip_lengths, hand, asum, bsum, og, og_got, wp2, wf2, ws2, beta2, beta1),
        [
            like(og),
            vmem(side2, side2, 8, D),
            vmem(2, *og.shape[1:], dtype=BF16),
            dma((2,)),
            dma(()),
            dma(()),
            vmem(total2, DP, dtype=BF16),
            vmem(side2, rows2, 256),
            vmem(side2, rows2, 128),
            vmem(side2, rows2, DP),
            vmem(8, DP),
            vmem(side2, rows2, 128),
            vmem(side2 + 2, rows2, 128),
            vmem(side2 + 2, rows2, 640),
            vmem(total2, 1536, dtype=BF16),
            vmem(total2, 384, dtype=BF16),
            vmem(side2, rows2, 1024),
            vmem(side2, rows2, 384),
            vmem(side2, rows2, DP),
            vmem(side2, rows2, 1024),
            vmem(side2, rows2, 384),
            vmem(side2, rows2, 640),
            vmem(side2, rows2, 256),
            vmem(2, 8, 640),
            vmem(8, 640),
            vmem(8, 512),
            vmem(2, 8, DP),
            vmem(1536, 1024),
            vmem(384, 384),
            vmem(DP, 640),
        ]
        + exchange_scratch(n, 640)
        + exchange_scratch(n, 512)
        + exchange_scratch(n, DP)
        + exchange_scratch(n, 640)
        + exchange_scratch(n, DP),
        collective=3,
        any_in=(4,),
        any_out=(0,),
    )
    dzc, dzs, dz1 = call(
        dz_kernel,
        [
            ((side + 2, rows, 1024), BF16),
            ((side + 2, rows, 384), BF16),
            ((2, side, rows // 2, 384), BF16),
        ],
        (clip_lengths, zf, sig, hg, stf, sums7),
        [vmem(side2, 16, 128), vmem(side, rows, 128), vmem(side + 2, rows, 128)],
    )
    packed1 = call(
        conv_grad_kernel,
        [((8, packed_rows, 128), BF16)],
        (cat, scat, dzc, dzs, beta1),
        [vmem(1536, 1024), vmem(384, 384)],
        smem_first=False,
    )[0]
    dzi, sums8 = call(
        conv_back_kernel,
        [((2, side, rows // 2, 256), BF16), ((8, 640), F32)],
        (clip_lengths, dzc, dzs, wf1, ws1, zin, st1, beta1),
        [vmem(side, rows, 256), vmem(2, 16, 640)] + exchange_scratch(n, 640),
        collective=4,
    )
    gin, packed1 = call(
        input_kernel,
        [(x.shape, BF16), ((8, packed_rows, 128), BF16)],
        (x, xgot, dz1, dzi, wp1, packed1),
        [like(x), like(x), like(x), vmem(D, 640), dma((2,)), dma(()), dma(())],
        smem_first=False,
        collective=5,
        any_in=(0, 5),
        any_out=(0,),
    )
    half_rows = packed_rows // 2
    lands = [vmem(*shape, dtype=BF16) for shape in land_shapes(8, half_rows, bits)]
    full, offs = call(
        functools.partial(reduce_kernel, bits),
        [((2, 8, half_rows, 128), BF16), ((8, DP + 640), F32)],
        (packed1, packed2, sums5, sums6, sums7, sums8),
        [vmem(8, half_rows, 128, dtype=BF16)] * 4
        + lands * 2
        + [vmem(8, DP + 640)] * 2
        + [dma((4,)), dma((4,)), dma((4 * bits,)), dma((4 * bits,)), dma((3,))]
        + [pltpu.SemaphoreType.REGULAR((2 * bits,))],
        smem_first=False,
        collective=6,
        any_in=(0, 1),
        any_out=(0,),
    )
    one, mid_in, mid, small_in, small, pool, offset = call(
        unpack_kernel,
        [
            ((D, C0), F32),
            ((C1A, D), F32),
            ((C1B, 27 * C1A), F32),
            ((C2A, D), F32),
            ((27 * C2A, C2B), F32),
            ((D, C3), F32),
            ((1, 1024), F32),
        ],
        (full, offs),
        [vmem(8, packed_rows, 128, dtype=BF16), vmem(27 * C1A, 384), dma((2,))],
        smem_first=False,
        any_in=(0,),
    )
    input_grad = gin.reshape(2, side, side, half, D).transpose(0, 3, 1, 2, 4)
    return (
        block_output.transpose(0, 3, 1, 2, 4),
        input_grad,
        one[None],
        mid_in.T[None],
        mid.T[None],
        small_in.T[None],
        small[None],
        pool[None],
        offset,
    )


def solution(mesh):
    placed = (
        P("dp", "section", None, None, None),
        P("dp", "section", None, None, None),
        P("dp", None),
        P("section", None, None),
        P("section", None, None),
        P("section", None, None),
        P("section", None, None),
        P("section", None, None),
        P("section", None, None),
        P("section", None),
    )
    return jax.shard_map(
        on_device,
        mesh=mesh,
        in_specs=placed,
        out_specs=(
            P("dp", "section", None, None, None),
            P("dp", "section", None, None, None),
            P("section", None, None),
            P("section", None, None),
            P("section", None, None),
            P("section", None, None),
            P("section", None, None),
            P("section", None, None),
            P("section", None),
        ),
        check_vma=False,
    )
```

time: 591 us -> 399 us (0.68); the launches traced: 580 us -> 399 us
  waiting for transfers between devices: 154 us -> 0 us
  Pallas kernels: 259 us -> 392 us
  local copies, waits for them, and re-layouts: 107 us -> 6.38 us
  other arithmetic: 42 us -> 0 us
  between operations: 14.9 us -> 0.72 us
    psum x1 -> x0, waiting for transfers between devices: 151 us -> none  [on_device(): dwf = lax.psum(to_section(dwf1, dwf2), 'dp').astype(F32)]
    pallas_call x8 -> x10, Pallas kernels: 259 us -> 392 us  [call(): pl.pallas_call(kernel, out_shape=[jax.ShapeDtypeStruct(shape, dtype) for...]
    unnamed x65 -> x4, local copies, waits for them, and re-layouts: 33.3 us -> 6.38 us
    slice x27 -> x0, local copies, waits for them, and re-layouts: 23.1 us -> none  [the longest x1 7.24 us: restore_mid(): cols[:, :384].reshape(3, 3, 128, 3, C1B)]
    reshape x6 -> x0, local copies, waits for them, and re-layouts: 18.4 us -> none  [the longest x1 6.37 us: arrange_mid(): w[:, :, :128].reshape(3, 384, 3, C1B)]
    concatenate x7 -> x0, other arithmetic: 11.4 us -> none  [the longest x1 3.58 us: arrange_mid(): jnp.concatenate([w[:, :, :128].reshape(3, 384, 3, C1B), w[:, :, 128:].res...]
    select_n x7 -> x0, other arithmetic: 10.6 us -> none  [the longest x3 7.42 us: both(): return (jnp.where(first, v[0], got), jnp.where(first, got, v[0]))]
    concatenate x11 -> x0, local copies, waits for them, and re-layouts: 8.51 us -> none  [the longest x2 2.64 us: to_final(): jnp.concatenate([one, pool, mid[..., :256], small, mid[..., 256:], zero],...]
  transfers between devices with their start and end apart: 13 -> 0, of which waited for: 3 -> 0; matrix products, arithmetic and copies ran while one was open for 17% -> 0% of each run, Pallas kernels for 15% -> 0%
where the time goes in v2:
time: 399 us
  Pallas kernels  392 us (98%)
  local copies, waits for them, and re-layouts  6.38 us (2%)
    pallas_call x10, Pallas kernels, call(): pl.pallas_call(kernel, out_shape=[jax.ShapeDtypeStruct(shape, dtype) for...  392 us

profile of v2, /device:TPU:0, one launch (start us, length us, event | category | flops | bytes accessed | tf_op | source)
XLA Modules:
  0.0 398.9 jit_solution(8649232821042854781)
XLA Ops:
  0.6 30.8 %shard_map.169 = (bf16[1568,832]{1,0:T(8,128)(2,1)}, f32[14,14,2,8,256]{4,3,2,1,0:T(8,128)}, f32[14,14,2,8,256]{4,3,2,1,0:T(8,128)}, f32[14,224,128]{2,1,0:T(8,1...) custom-call(s32[2,2]{1,0:T(2,128)} %len_ref.11, ...), custom_call_target="tpu_custom_call" | custom-call | tf_op jit(solution)/shard_map/pallas_call | solution.py:1289
  31.5 35.1 %shard_map.170 = (bf16[16,224,512]{2,1,0:T(8,128)(2,1)}, bf16[16,224,128]{2,1,0:T(8,128)(2,1)}, f32[14,224,896]{2,1,0:T(8,128)}, f32[8,896]{1,0:T(8,128)}) custom-call(s32[2,2]{1,0:T(2,128)} %len_ref.11, f32[14,224,256]{2,1,0:T(8,128)} %bitcast.27, f32[14,224,256]{2,1,0:T(8,128)} %bitcast.30, f32[14,224,128]{2,1,0:T(8,128)} %get-tuple-element.55.zp, ...), custom_call_target="tpu_custom_call" | custom-call | tf_op jit(solution)/shard_map/pallas_call | solution.py:1289
  66.6 19.3 %shard_map.171 = (bf16[14,224,896]{2,1,0:T(8,128)(2,1)}, f32[7,7,8,896]{3,2,1,0:T(8,128)}, f32[7,7,8,896]{3,2,1,0:T(8,128)}, f32[7,7,8,896]{3,2,1,0:T(8,128)}) custom-call(s32[2,2]{1,0:T(2,128)} %len_ref.11, f32[14,224,896]{2,1,0:T(8,128)} %get-tuple-element.60.zf, f32[8,896]{1,0:T(8,128)} %get-tuple-element.61.stf, f32[1,1152]{1,0:T(1,128)} %get-tuple-element.57.beta.beta1), custom_call_target="tpu_custom_call" | custom-call | tf_op jit(solution)/shard_map/pallas_call | solution.py:1289
  85.9 64.0 %shard_map.172 = (bf16[2,7,7,4,832]{4,3,2,1,0:T(4,128)(2,1)}, f32[7,7,8,896]{3,2,1,0:T(8,128)}, bf16[8,2304,128]{2,1,0:T(8,128)(2,1)}, f32[8,896]{1,0:T(8,128)}, f32[8,640]{1,0:T(8,128)}, /*index=5*/f32[8,896]{1,0:T(8,128)}) custom-call(s32[2,2]{1,0:T(2,128)} %len_ref.11, f32[7,7,8,896]{3,2,1,0:T(8,128)} %get-tuple-element.62.hand, ...), custom_call_target="tpu_custom_call" | custom-call | tf_op jit(solution)/shard_map/pallas_call | solution.py:1289
  149.8 17.4 %shard_map.173 = (bf16[16,224,1024]{2,1,0:T(8,128)(2,1)}, bf16[16,224,384]{2,1,0:T(8,128)(2,1)}, bf16[2,14,112,384]{3,2,1,0:T(8,128)(2,1)}) custom-call(s32[2,2]{1,0:T(2,128)} %len_ref.11, f32[14,224,896]{2,1,0:T(8,128)} %get-tuple-element.60.zf, bf16[14,224,896]{2,1,0:T(8,128)(2,1)} %get-tuple-element.72.sig, f32[7,7,8,896]{3,2,1,0:T(8,128)} %get-tuple-element.73.hg, ...), custom_call_target="tpu_custom_call" | custom-call | tf_op jit(solution)/shard_map/pallas_call | solution.py:1289
  167.2 34.4 %shard_map.174 = (bf16[2,14,112,256]{3,2,1,0:T(8,128)(2,1)}, f32[8,640]{1,0:T(8,128)}) custom-call(s32[2,2]{1,0:T(2,128)} %len_ref.11, bf16[16,224,1024]{2,1,0:T(8,128)(2,1)} %get-tuple-element.76.dzc, bf16[16,224,384]{2,1,0:T(8,128)(2,1)} %get-tuple-element.77.dzs, bf16[1536,1024]{1,0:T(8,128)(2,1)} %get-tuple-element.58.wf, ...), custom_call_target="tpu_custom_call" | custom-call | tf_op jit(solution)/shard_map/pallas_call | solution.py:1289
  201.6 22.1 %shard_map.175.packed_in = bf16[8,2304,128]{2,1,0:T(8,128)(2,1)} custom-call(bf16[16,224,512]{2,1,0:T(8,128)(2,1)} %get-tuple-element.80.cat, bf16[16,224,128]{2,1,0:T(8,128)(2,1)} %get-tuple-element.81.scat, bf16[16,224,1024]{2,1,0:T(8,128)(2,1)} %get-tuple-element.76.dzc, bf16[16,224,384]{2,1,0:T(8,128)(2,1)} %get-tuple-element.77.dzs, ...), custom_call_target="tpu_custom_call" | custom-call | tf_op jit(solution)/shard_map/pallas_call | solution.py:1289
  223.7 16.8 %shard_map.176 = (bf16[2,1568,832]{2,1,0:T(8,128)(2,1)}, bf16[8,2304,128]{2,1,0:T(8,128)(2,1)}) custom-call(bf16[2,1568,832]{2,1,0:T(8,128)(2,1)} %bitcast.26, bf16[1568,832]{1,0:T(8,128)(2,1)} %get-tuple-element.71.x_got, bf16[2,14,112,384]{3,2,1,0:T(8,128)(2,1)} %get-tuple-element.75.dz1, bf16[2,14,112,256]{3,2,1,0:T(8,128)(2,1)} %get-tuple-element.78.dzi, ...), custom_call_target="tpu_custom_call" | custom-call | tf_op jit(solution)/shard_map/pallas_call | solution.py:1289
  240.4 140.9 %shard_map.177 = (bf16[2,8,1152,128]{3,2,1,0:T(8,128)(2,1)}, f32[8,1536]{1,0:T(8,128)}) custom-call(bf16[8,2304,128]{2,1,0:T(8,128)(2,1)} %get-tuple-element.83.packed1, bf16[8,2304,128]{2,1,0:T(8,128)(2,1)} %get-tuple-element.84.packed2, f32[8,896]{1,0:T(8,128)} %get-tuple-element.85.s5, f32[8,640]{1,0:T(8,128)} %get-tuple-element.86.s6, ...), custom_call_target="tpu_custom_call" | custom-call | tf_op jit(solution)/shard_map/pallas_call | solution.py:1289
  381.4 0.0 copy-start
  381.4 11.1 %shard_map.178 = (f32[832,256]{1,0:T(8,128)}, f32[160,832]{1,0:T(8,128)}, f32[320,4320]{1,0:T(8,128)}, f32[32,832]{1,0:T(8,128)}, f32[864,128]{1,0:T(8,128)}, /*index=5*/f32[832,128]{1,0:T(8,128)}, f32[1,1024]{1,0:T(1,128)}) custom-call(bf16[2,8,1152,128]{3,2,1,0:T(8,128)(2,1)} %get-tuple-element.88.full, f32[8,1536]{1,0:T(8,128)} %get-tuple-element.89.offs), custom_call_target="tpu_custom_call" | custom-call | tf_op jit(solution)/shard_map/pallas_call | solution.py:1289
  392.5 0.0 copy-done
  392.5 0.9 copy.21
  393.4 5.5 %copy.22 = bf16[2,8,14,14,832]{4,1,3,2,0:T(8,128)(2,1)} copy(bf16[2,8,14,14,832]{4,1,3,2,0:T(8,128)(2,1)} %bitcast.29) | data formatting | bytes 10436608
Async XLA Ops:
  381.4 11.1 %copy-start = (bf16[2,7,7,4,832]{4,3,2,1,0:T(4,128)(2,1)S(1)}, bf16[2,7,7,4,832]{4,3,2,1,0:T(4,128)(2,1)}, u32[]{:S(2)}) copy-start(bf16[2,7,7,4,832]{4,3,2,1,0:T(4,128)(2,1)} %get-tuple-element.70) | copy-start | bytes 1956868

commit v3 on v2

--- a/solution.py
+++ b/solution.py
@@ -156,7 +156,7 @@
     buf[me] = loc[...]
 
 
-def exchange_finish(loc, buf, ssem, rsem, out):
+def exchange_finish(loc, buf, ssem, rsem, out, tiles):
     n = lax.axis_size("dp")
     me = lax.axis_index("dp")
 
@@ -175,12 +175,19 @@
         return 0
 
     lax.fori_loop(1, n, wait, 0)
-    out[...] = jnp.sum(buf[...], axis=0)
-
-
-def exchange(loc, buf, ssem, rsem, out):
+    total = jnp.sum(buf[...], axis=0)
+    at = 2 * len(tiles)
+    for i, t in enumerate(tiles):
+        lanes = slice(128 * t, 128 * t + 128)
+        out[0:1, lanes] = total[2 * i : 2 * i + 1]
+        out[1:2, lanes] = total[2 * i + 1 : 2 * i + 2]
+        if at < loc.shape[0]:
+            out[2:3, lanes] = total[at : at + 1]
+
+
+def exchange(loc, buf, ssem, rsem, out, tiles):
     exchange_start(loc, buf, ssem, rsem)
-    exchange_finish(loc, buf, ssem, rsem, out)
+    exchange_finish(loc, buf, ssem, rsem, out, tiles)
 
 
 def swap_copy(src, dst, ssem, rsem):
@@ -194,24 +201,28 @@
     )
 
 
-def exchange_scratch(n, lanes):
+def exchange_scratch(n, rows):
     return [
-        pltpu.VMEM((8, lanes), F32),
-        pltpu.VMEM((n, 8, lanes), F32),
+        pltpu.VMEM((rows, 128), F32),
+        pltpu.VMEM((n, rows, 128), F32),
         pltpu.SemaphoreType.DMA((n,)),
         pltpu.SemaphoreType.DMA((n,)),
     ]
 
 
-def pack_stats(clips, loc, acc, count=None):
-    for t in range(loc.shape[1] // 128):
+FIRST, CONV, FINAL, INNER = range(5), range(4), range(7), (3, 4)
+
+
+def pack_stats(clips, loc, acc, tiles, count=None):
+    for i, t in enumerate(tiles):
         lanes = pl.ds(128 * t, 128)
-        loc[0:1, lanes] = jnp.sum(acc[0, :, lanes] * clips.valid, axis=0, keepdims=True)
-        loc[1:2, lanes] = jnp.sum(acc[1, :, lanes] * clips.valid, axis=0, keepdims=True)
+        for k in range(2):
+            loc[2 * i + k : 2 * i + k + 1, :] = jnp.sum(
+                acc[k, :, lanes] * clips.valid, axis=0, keepdims=True
+            )
     if count is not None:
-        total = jnp.sum(clips.valid, axis=0, keepdims=True) * float(count)
-        for t in range(loc.shape[1] // 128):
-            loc[2:3, 128 * t : 128 * t + 128] = total
+        at = 2 * len(tiles)
+        loc[at : at + 1, :] = jnp.sum(clips.valid, axis=0, keepdims=True) * float(count)
 
 
 def loop(n, body):
@@ -324,7 +335,7 @@
     xgot_out, zone_out, zin_out, zp_out, st, wp1, wp2, wf1, wf2, ws1, ws2, beta1, beta2, og_got,
     x_own, x_got, zone, zin, zp, yp, tx,
     own_one, own_mid_in, own_small_in, own_pool, own_mid, own_small,
-    got_one, got_mid_in, got_small_in, got_pool, got_mid, got_small, beta, got_beta, flip,
+    beta, got_beta, flip,
     wp, wf, ws, hacc, acc, loc, buf, ssem, rsem, lsem, osem, psem, qsem,
 ):
     greet(partner=True)
@@ -333,7 +344,6 @@
     clips = Clips(len_ref, 16, 1)
     raw = (w_one, w_mid_in, w_small_in, w_pool, w_mid, w_small)
     own = (own_one, own_mid_in, own_small_in, own_pool, own_mid, own_small)
-    got = (got_one, got_mid_in, got_small_in, got_pool, got_mid, got_small)
     local = [pltpu.make_async_copy(x.at[sec], x_own, lsem.at[0])]
     local += [
         pltpu.make_async_copy(a.at[0], b, lsem.at[i + 1]) for i, (a, b) in enumerate(zip(raw, own))
@@ -344,21 +354,22 @@
     acc[...] = jnp.zeros_like(acc)
     loc[...] = jnp.zeros_like(loc)
     arrange_beta(bn, beta)
-    greeted(partner=True)
-    pairs = [(a.at[0], b) for a, b in zip(raw[:4], got[:4])]
-    pairs += [(beta, got_beta), (x.at[1 - sec], x_got)]
-    pairs += [(a.at[0], b) for a, b in zip(raw[4:], got[4:])]
-    pairs += [(og.at[1 - sec], og_got)]
-    remote = [swap_copy(a, b, psem.at[i], qsem.at[i]) for i, (a, b) in enumerate(pairs)]
-    for c in remote:
-        c.start()
-    for c in local[1:]:
+    for c in local[1:5]:
         c.wait()
     arrange_first(own[:4], wp, sec, flip)
+    greeted(partner=True)
+    pairs = ((wp.at[sec], wp.at[sec]), (beta, got_beta), (x.at[1 - sec], x_got))
+    pairs += ((og.at[1 - sec], og_got), (wf.at[sec], wf.at[sec]), (ws.at[sec], ws.at[sec]))
+    remote = [swap_copy(a, b, psem.at[i], qsem.at[i]) for i, (a, b) in enumerate(pairs)]
+    for c in remote[:4]:
+        c.start()
+    for c in local[5:]:
+        c.wait()
     arrange_conv(own_mid, own_small, wf, ws, sec, flip)
-    for c in remote[:5]:
+    for c in remote[4:]:
+        c.start()
+    for c in remote[:2]:
         c.wait()
-    arrange_first(got[:4], wp, 1 - sec, flip)
     beta1[...] = jnp.where(sec == 0, beta[...], got_beta[...])
     beta2[...] = jnp.where(sec == 0, got_beta[...], beta[...])
     ny = side // 2
@@ -371,7 +382,7 @@
         outs.append(c)
 
     for part, src in enumerate((x_own, x_got)):
-        (local[0] if part == 0 else remote[5]).wait()
+        (local[0] if part == 0 else remote[2]).wait()
         half = sec if part == 0 else 1 - sec
 
         def body(i, src=src, half=half):
@@ -396,15 +407,14 @@
     acc[...] = hacc[...].reshape(acc.shape)
     pool_forward(clips, side, lambda y: yp[y].reshape(side * 16, 128), tx, zp, acc)
     put(zp, zp_out)
-    pack_stats(clips, loc, acc, side * side)
+    pack_stats(clips, loc, acc, FIRST, side * side)
     exchange_start(loc, buf, ssem, rsem)
-    for c in remote[6:]:
+    for c in remote[3:]:
         c.wait()
-    arrange_conv(got_mid, got_small, wf, ws, 1 - sec, flip)
     for a, b in ((wf, (wf1, wf2)), (ws, (ws1, ws2)), (wp, (wp1, wp2))):
         for i in range(2):
             put(a.at[i], b[i])
-    exchange_finish(loc, buf, ssem, rsem, st)
+    exchange_finish(loc, buf, ssem, rsem, st, FIRST)
     for c in outs:
         c.wait()
 
@@ -589,7 +599,7 @@
             store_conv(clips, y0 + q, p[here], s[here], zp, zf, acc)
 
     loop(side // ny, products)
-    pack_stats(clips, loc, acc)
+    pack_stats(clips, loc, acc, CONV)
     greeted()
     exchange_start(loc, buf, ssem, rsem)
 
@@ -597,7 +607,7 @@
         zf[y, :, 0:256] = zone[y]
 
     loop(side, move)
-    exchange_finish(loc, buf, ssem, rsem, st2)
+    exchange_finish(loc, buf, ssem, rsem, st2, CONV)
     final_stats(st1, st2, stf)
 
 
@@ -637,7 +647,7 @@
 
 def second_kernel(
     len_ref, hand, asum, bsum, og, og_got, wp, wf, ws, beta, beta1,
-    block_out, hg, packed, sums5, sums6, sums7,
+    block_out, hg, packed_a, packed_b, sums5, sums6, sums7,
     gown, grad, out, lsem, psem, qsem,
     hbuf, zin, zp, zf, stf, yp, tx, catf, cat, scat, pbuf, sbuf, dbuf, dzc, dzs, dz1, din,
     acc, st3, st4, acc7, accm, accs, accp,
@@ -667,7 +677,7 @@
 
     loop(side, first_sums)
     pool_forward(clips, side, lambda y: yp[y], tx, zp, acc)
-    pack_stats(clips, loc3, acc, side * side)
+    pack_stats(clips, loc3, acc, FIRST, side * side)
     greeted(partner=True)
     exchange_start(loc3, buf3, ss3, rs3)
     own.wait()
@@ -675,7 +685,7 @@
     low = jnp.where(sec == 0, mine, theirs)
     high = jnp.where(sec == 0, theirs, mine)
     grad[...] = jnp.concatenate([low, high], 2)
-    exchange_finish(loc3, buf3, ss3, rs3, st3)
+    exchange_finish(loc3, buf3, ss3, rs3, st3, FIRST)
 
     catf[0] = jnp.zeros(catf.shape[1:], F32)
     catf[side + 1] = jnp.zeros(catf.shape[1:], F32)
@@ -695,8 +705,8 @@
     sbuf[...] = dot(scat[...], ws[...]).reshape(side, rows, 384)
     acc[...] = jnp.zeros_like(acc)
     loop(side, lambda y: store_conv(clips, y, pbuf[y], sbuf[y], zp, zf, acc))
-    pack_stats(clips, loc4, acc)
-    exchange(loc4, buf4, ss4, rs4, st4)
+    pack_stats(clips, loc4, acc, CONV)
+    exchange(loc4, buf4, ss4, rs4, st4, CONV)
     final_stats(st3, st4, stf)
 
     def emit(y):
@@ -721,8 +731,8 @@
     mine.start()
     theirs = swap_copy(out.at[1 - sec], block_out.at[sec], psem, qsem)
     theirs.start()
-    pack_stats(clips, loc5, acc7)
-    exchange(loc5, buf5, ss5, rs5, sums5)
+    pack_stats(clips, loc5, acc7, FINAL)
+    exchange(loc5, buf5, ss5, rs5, sums5, FINAL)
     count = st3[2:3, 0:128]
 
     def dz_of(y, t):
@@ -770,10 +780,10 @@
         inner_up(clips, zin[y], untap(clips, parts[:4], parts[4]), st3, beta, acc, din, y)
 
     loop(side, inner_back)
-    pack_stats(clips, loc6, acc)
+    pack_stats(clips, loc6, acc, INNER)
     exchange_start(loc6, buf6, ss6, rs6)
     accm[...] = dot_tn(cat[...], dzc_b)
-    exchange_finish(loc6, buf6, ss6, rs6, sums6)
+    exchange_finish(loc6, buf6, ss6, rs6, sums6, INNER)
 
     def dz_inner(y):
         for t in range(2):
@@ -796,7 +806,7 @@
             acc7[1, :, lanes] += jnp.sum(gr * bsum[y, :, :, lanes], axis=0)
 
     loop(side, upstream)
-    pack_stats(clips, loc7, acc7)
+    pack_stats(clips, loc7, acc7, FINAL)
     exchange_start(loc7, buf7, ss7, rs7)
     accs[...] = dot_tn(scat[...], dzs_b)
     accp[...] = dot_tn(hbuf[...], dz1_b)
@@ -805,33 +815,41 @@
     accp[:, 256:384] += dot_tn(hbuf[...], rest)
     c = jnp.concatenate([typical(beta1[0:1, 0:D]), jnp.zeros((8, DP - D), F32)], 1)
     full = accp[...] - outer(c, accp[DP - 1 : DP, :])
-    pack_grads(packed, accm, accs, beta, lambda t: full[0:D, 128 * t : 128 * t + 128])
-    exchange_finish(loc7, buf7, ss7, rs7, sums7)
+    pack_mid(packed_a, accm, beta)
+    pack_first(packed_b, lambda t: full[0:D, 128 * t : 128 * t + 128], accs, beta)
+    exchange_finish(loc7, buf7, ss7, rs7, sums7, FINAL)
     mine.wait()
     theirs.wait()
 
 
-def pack_grads(packed, accm, accs, beta, first):
-    mid = centre_mid(accm, beta)
-    small = centre_small(accs, beta)
+def pack_mid(packed, acc, beta):
+    mid = centre_mid(acc, beta)
     end = packed.shape[1]
     for t in range(8):
         lanes = slice(128 * t, 128 * t + 128)
         for k in range(3):
             packed[t, 480 * k : 480 * k + 480] = (
-                accm[512 * k : 512 * k + 480, lanes] - mid[0:480, lanes]
+                acc[512 * k : 512 * k + 480, lanes] - mid[0:480, lanes]
             ).astype(BF16)
+        if end > 1440:
+            packed[t, 1440:end] = jnp.zeros((end - 1440, 128), BF16)
+
+
+def pack_first(packed, first, acc, beta):
+    small = centre_small(acc, beta)
+    end = packed.shape[1]
+    for t in range(8):
         if t < 5:
-            if first is not None:
-                packed[t, 1440 : 1440 + D] = first(t).astype(BF16)
+            packed[t, 0:D] = first(t).astype(BF16)
         else:
             lanes = slice(128 * (t - 5), 128 * (t - 5) + 128)
             for k in range(3):
-                packed[t, 1440 + 128 * k : 1568 + 128 * k] = (
-                    accs[128 * k : 128 * k + 128, lanes] - small[:, lanes]
+                packed[t, 128 * k : 128 * k + 128] = (
+                    acc[128 * k : 128 * k + 128, lanes] - small[:, lanes]
                 ).astype(BF16)
-            packed[t, 1824 : 1440 + D] = jnp.zeros((D - 384, 128), BF16)
-        packed[t, 1440 + D : end] = jnp.zeros((end - 1440 - D, 128), BF16)
+            packed[t, 384:D] = jnp.zeros((D - 384, 128), BF16)
+        if end > D:
+            packed[t, D:end] = jnp.zeros((end - D, 128), BF16)
 
 
 def inner_up(clips, z, backs, st, beta, acc, din, y):
@@ -861,188 +879,341 @@
         ref[h, y, :, lane : lane + lanes] = v[:, h].reshape(side * 8, lanes).astype(BF16)
 
 
-def dz_kernel(len_ref, zf, sig, hg, stf, sums7, dzc, dzs, dz1, scr, yp, tx):
-    side = zf.shape[0]
+def backward_kernel(
+    bits, len_ref, hg, stf, sums7, st1, beta, sums5, sums6,
+    zf, sig, zin_in, wf_in, ws_in, wp_in, cat_in, scat_in, x, x_got, packed2a, packed2b,
+    gin, full_a, full_b, offs,
+    zin, wf, ws, wp, dzc, dzs, dz1, dzi, sums8, snd, got,
+    p1a, p1b, q2a, q2b, core_a1, core_b1, core_a2, core_b2,
+    acc, loc, buf, ss8, rs8, lsem, csend, crecv, ssem, rsem, gsend, grecv, ready, *lands,
+):
+    greet(partner=True)
+    sec = lax.axis_index("section")
+    side = dz1.shape[1]
     half = side // 2
     rows = side * 16
     clips = Clips(len_ref, 16, 1)
     count = stf[2:3, 0:128]
+    loads = [
+        pltpu.make_async_copy(a, b, lsem.at[i])
+        for i, (a, b) in enumerate(((zin_in, zin), (wf_in, wf), (ws_in, ws), (wp_in, wp)))
+    ]
+    for i, (a, b) in enumerate(((packed2a, q2a), (packed2b, q2b))):
+        h = b.shape[1]
+        src = a.at[:, pl.ds(pl.multiple_of(sec * h, 16), h)]
+        loads.append(pltpu.make_async_copy(src, b, lsem.at[4 + i]))
+    for c in loads:
+        c.start()
+
+    def reducer(i, q, base_row, half_rows, swap_src, core_land, flip, load):
+        return Reducer(
+            bits, i, q, base_row, half_rows, swap_src, core_land, lands[bits * i : bits * i + bits],
+            csend, crecv, ssem, rsem, ready, flip, load,
+        )
+
+    def part(ref, half_rows, which):
+        return ref.at[:, pl.ds(pl.multiple_of(which * half_rows, 16), half_rows)]
+
+    ha, hb = q2a.shape[1], q2b.shape[1]
+    a2 = reducer(0, q2a, 0, ha, part(packed2a, ha, 1 - sec), core_a2, 1 - sec, loads[4])
+    b2 = reducer(1, q2b, 0, hb, part(packed2b, hb, 1 - sec), core_b2, 1 - sec, loads[5])
+    a1 = reducer(2, p1a, sec * ha, ha, part(p1a, ha, 1 - sec), core_a1, sec, None)
+    b1 = reducer(3, p1b, sec * hb, hb, part(p1b, hb, 1 - sec), core_b1, sec, None)
+
+    acc[...] = jnp.zeros_like(acc)
+    loc[...] = jnp.zeros_like(loc)
     for y in (0, side + 1):
         dzc[y] = jnp.zeros(dzc.shape[1:], BF16)
         dzs[y] = jnp.zeros(dzs.shape[1:], BF16)
 
-    def body(k):
-        tiles = ([], [])
-        for t in range(7):
-            lanes = pl.ds(128 * t, 128)
-            scale, mean = affine(stf, lanes)
-            m1, m2 = sums7[0:1, lanes] / count, sums7[1:2, lanes] / count
-            gr = hg[k, :, :, lanes] * 0.125
-            scr[:, pl.ds(0, 8, stride=2), :] = gr
-            scr[:, pl.ds(1, 8, stride=2), :] = gr
-            gr = scr[...]
-            gr = jnp.broadcast_to(gr[:, None], (half, 2, 16, 128)).reshape(rows, 128)
+    def dz_phase(zb, sb, scr, yp, tx, zsem):
+        def fetch(k, slot):
+            here = pl.ds(2 * k, 2)
+            return (
+                pltpu.make_async_copy(zf.at[here], zb.at[slot], zsem.at[0, slot]),
+                pltpu.make_async_copy(sig.at[here], sb.at[slot], zsem.at[1, slot]),
+            )
+
+        for c in fetch(0, 0):
+            c.start()
+
+        def body(k):
+            slot = lax.rem(k, 2)
+
+            @pl.when(k < half - 1)
+            def _():
+                for c in fetch(k + 1, 1 - slot):
+                    c.start()
+
+            @pl.when(k == 1)
+            def _():
+                greeted(partner=True)
+                a2.point(0)
+                b2.point(0)
+
+            pl.when(k == 4)(lambda: a2.point(1))
+            pl.when(k == 5)(lambda: b2.point(1))
+            for c in fetch(k, slot):
+                c.wait()
+            tiles = ([], [])
+            for t in range(7):
+                lanes = pl.ds(128 * t, 128)
+                scale, mean = affine(stf, lanes)
+                m1, m2 = sums7[0:1, lanes] / count, sums7[1:2, lanes] / count
+                gr = hg[k, :, :, lanes] * 0.125
+                scr[:, pl.ds(0, 8, stride=2), :] = gr
+                scr[:, pl.ds(1, 8, stride=2), :] = gr
+                gr = scr[...]
+                gr = jnp.broadcast_to(gr[:, None], (half, 2, 16, 128)).reshape(rows, 128)
+                for q in range(2):
+                    u = (zb[slot, q, :, lanes] - mean) * scale
+                    d = gr * sb[slot, q, :, lanes].astype(F32)
+                    dz = clips.times((d - m1 - u * m2) * scale, clips.valid)
+                    if t < 2:
+                        put_halves(dz1, 2 * k + q, 128 * t, dz)
+                    else:
+                        tiles[q].append(dz)
             for q in range(2):
                 y = 2 * k + q
-                u = (zf[y, :, lanes] - mean) * scale
-                d = gr * sig[y, :, lanes].astype(F32)
-                dz = clips.times((d - m1 - u * m2) * scale, clips.valid)
-                if t < 2:
-                    put_halves(dz1, y, 128 * t, dz)
-                else:
-                    tiles[q].append(dz)
-        for q in range(2):
-            y = 2 * k + q
-            small, tail, pool = split_final(*tiles[q][2:])
-            yp[y] = clips.times(pool * inv_edges(side, 16, y), clips.inv)
-
-            def put(ref, y=y):
-                def go(lane, v):
-                    ref[y + 1, :, lane : lane + v.shape[-1]] = v.astype(BF16)
-
-                return go
-
-            put_spread(
-                16, jnp.concatenate(tiles[q][:2], 1), small, tail, put(dzc), put(dzs)
-            )
-
-    loop(half, body)
-
-    def boxed(y, v):
-        put_halves(dz1, y, 256, clips.times(v, clips.valid))
-
-    box(clips, side, lambda y: yp[y], tx, boxed)
-
-
-def conv_grad_kernel(cat, scat, dzc, dzs, beta, packed, acc, accs):
-    side = cat.shape[0] - 2
-    rows = cat.shape[1]
-    ny = 7
-    acc[...] = jnp.zeros_like(acc)
-    accs[...] = jnp.zeros_like(accs)
-
-    def body(i):
-        y0 = i * ny + 1
-
-        def take(ref, y):
-            return ref[pl.ds(y, ny)].reshape(ny * rows, ref.shape[-1])
-
-        a, s = take(cat, y0), take(scat, y0)
-        for dy in (-1, 0, 1):
-            k = dy + 1
-            acc[512 * k : 512 * k + 512] += dot_tn(a, take(dzc, y0 - dy))
-            accs[128 * k : 128 * k + 128] += dot_tn(s, take(dzs, y0 - dy))
-
-    loop(side // ny, body)
-    pack_grads(packed, acc, accs, beta, None)
-
-
-def conv_back_kernel(
-    len_ref, dzc, dzs, wf, ws, zin, st1, beta, dzi, sums8, din, acc, loc, buf, ssem, rsem
-):
-    greet()
-    side, rows = zin.shape[0], zin.shape[1]
-    clips = Clips(len_ref, 16, 1)
-    acc[...] = jnp.zeros_like(acc)
-    loc[...] = jnp.zeros_like(loc)
-    ny = 2
-
-    def body(i):
-        y0 = i * ny + 1
-        q = s = None
-        for dy in (-1, 0, 1):
-            k = dy + 1
-            here = pl.ds(y0 - dy, ny)
-            t = dot_nt(dzc[here].reshape(ny * rows, 1024), wf[512 * k : 512 * k + 512])
-            q = t if q is None else q + t
-            t = dot_nt(dzs[here].reshape(ny * rows, 384), ws[128 * k : 128 * k + 128])
-            s = t if s is None else s + t
-        for j in range(ny):
-            y = i * ny + j
-            here = slice(j * rows, (j + 1) * rows)
-            parts = [q[here, 128 * t : 128 * t + 128] for t in range(4)]
-            inner_up(clips, zin[y], untap(clips, parts, s[here]), st1, beta, acc, din, y)
-
-    loop(side // ny, body)
-    pack_stats(clips, loc, acc)
-    greeted()
-    exchange(loc, buf, ssem, rsem, sums8)
-    count = st1[2:3, 0:128]
-
-    def dz(y):
-        for t in range(2):
-            put_halves(dzi, y, 128 * t, inner_dz(clips, t, zin[y], din[y], st1, sums8, count))
-
-    loop(side, dz)
-
-
-def input_kernel(
-    x, x_got, dz1, dzi, wp, packed_in, gin, packed,
-    x_own, near, far, acc, lsem, psem, qsem,
-):
-    greet_core()
-    sec = lax.axis_index("section")
-    own = pltpu.make_async_copy(x.at[sec], x_own, lsem.at[0])
-    own.start()
-    keep = pltpu.make_async_copy(packed_in, packed, lsem.at[1])
-    keep.start()
-    side = dz1.shape[1]
-    rows = dz1.shape[2]
-    ny = 7
-    acc[...] = jnp.zeros_like(acc)
-    for src, dst, half in ((x_got, far, 1 - sec), (x_own, near, sec)):
-
-        def body(i, src=src, dst=dst, half=half):
-            here = pl.ds(i * ny, ny)
-            d = jnp.concatenate([dz1[half, here], dzi[half, here]], -1).reshape(ny * rows, 640)
-            at = pl.ds(pl.multiple_of(i * ny * rows, 16), ny * rows)
-            dst[at] = dot_nt(d, wp[...]).astype(BF16)
-            acc[...] += dot_tn(src[at], d)
-
-        if src is x_own:
-            own.wait()
+                small, tail, pool = split_final(*tiles[q][2:])
+                yp[y] = clips.times(pool * inv_edges(side, 16, y), clips.inv)
+
+                def put(ref, y=y):
+                    def go(lane, v):
+                        ref[y + 1, :, lane : lane + v.shape[-1]] = v.astype(BF16)
+
+                    return go
+
+                put_spread(
+                    16, jnp.concatenate(tiles[q][:2], 1), small, tail, put(dzc), put(dzs)
+                )
+
+        loop(half, body)
+
+        def boxed(y, v):
+            put_halves(dz1, y, 256, clips.times(v, clips.valid))
+
+        box(clips, side, lambda y: yp[y], tx, boxed)
+
+    pl.run_scoped(
+        dz_phase,
+        vmem(2, 2, rows, DP),
+        vmem(2, 2, rows, DP, dtype=BF16),
+        vmem(half, 16, 128),
+        vmem(side, rows, 128),
+        vmem(side + 2, rows, 128),
+        pltpu.SemaphoreType.DMA((2, 2)),
+    )
+
+    def grad_phase(cat, scat, accm, accs, sems):
+        copies = [
+            pltpu.make_async_copy(cat_in, cat, sems.at[0]),
+            pltpu.make_async_copy(scat_in, scat, sems.at[1]),
+        ]
+        for c in copies:
+            c.start()
+        a2.point(2)
+        accm[...] = jnp.zeros_like(accm)
+        accs[...] = jnp.zeros_like(accs)
+        for c in copies:
+            c.wait()
+        ny = 2
+
+        def body(i):
+            y0 = i * ny + 1
+
+            def take(ref, y):
+                return ref[pl.ds(y, ny)].reshape(ny * rows, ref.shape[-1])
+
+            pl.when(i == 1)(lambda: b2.point(2))
+            pl.when(i == 2)(lambda: a2.point(3))
+            pl.when(i == 3)(lambda: b2.point(3))
+            pl.when(i == 5)(lambda: a2.point(4))
+            pl.when(i == 6)(lambda: b2.point(4))
+            a, s = take(cat, y0), take(scat, y0)
+            for dy in (-1, 0, 1):
+                k = dy + 1
+                accm[512 * k : 512 * k + 512] += dot_tn(a, take(dzc, y0 - dy))
+                accs[128 * k : 128 * k + 128] += dot_tn(s, take(dzs, y0 - dy))
+
         loop(side // ny, body)
-        if src is x_got:
-            greeted_core()
-            send = swap_copy(far, gin.at[sec], psem, qsem)
-            send.start()
-    mine = pltpu.make_async_copy(near, gin.at[sec], lsem.at[0])
-    mine.start()
-    keep.wait()
-    for t in range(5):
-        packed[t, 1440 : 1440 + D] = acc[:, 128 * t : 128 * t + 128].astype(BF16)
-    mine.wait()
-    send.wait()
-
-
-def greet_core():
-    pl.semaphore_signal(
-        pltpu.get_barrier_semaphore(),
-        inc=1,
-        device_id={"section": 1 - lax.axis_index("section")},
-        device_id_type=MESH,
+        pack_mid(p1a, accm, beta)
+        a1.point(0)
+        pack_first(p1b, lambda t: jnp.zeros((D, 128), F32), accs, beta)
+
+    pl.run_scoped(
+        grad_phase,
+        vmem(side + 2, rows, 512, dtype=BF16),
+        vmem(side + 2, rows, 128, dtype=BF16),
+        vmem(1536, 1024),
+        vmem(384, 384),
+        pltpu.SemaphoreType.DMA((2,)),
     )
 
-
-def greeted_core():
-    pl.semaphore_wait(pltpu.get_barrier_semaphore(), 1)
-
-
-def bit_of(me, k):
-    return lax.rem(me // (1 << k), 2)
+    def last_phase(din, x0, x1, ring, accp, sems):
+        own = pltpu.make_async_copy(x.at[sec], x0, sems.at[0])
+        other = pltpu.make_async_copy(x_got, x1, sems.at[1])
+        own.start()
+        other.start()
+        for c in loads[:4]:
+            c.wait()
+        a2.point(5)
+        ny = 2
+
+        def body(i):
+            y0 = i * ny + 1
+            pl.when(i == 1)(lambda: b2.point(5))
+            pl.when(i == 2)(lambda: a1.point(1))
+            pl.when(i == 3)(lambda: a2.point(6))
+            pl.when(i == 4)(lambda: b2.point(6))
+            pl.when(i == 6)(lambda: a2.point(7))
+            q = s = None
+            for dy in (-1, 0, 1):
+                k = dy + 1
+                here = pl.ds(y0 - dy, ny)
+                t = dot_nt(dzc[here].reshape(ny * rows, 1024), wf[512 * k : 512 * k + 512])
+                q = t if q is None else q + t
+                t = dot_nt(dzs[here].reshape(ny * rows, 384), ws[128 * k : 128 * k + 128])
+                s = t if s is None else s + t
+            for j in range(ny):
+                y = i * ny + j
+                here = slice(j * rows, (j + 1) * rows)
+                parts = [q[here, 128 * t : 128 * t + 128] for t in range(4)]
+                inner_up(clips, zin[y], untap(clips, parts, s[here]), st1, beta, acc, din, y)
+
+        loop(side // ny, body)
+        pack_stats(clips, loc, acc, INNER)
+        exchange_start(loc, buf, ss8, rs8)
+        a1.point(2)
+        b2.point(7)
+        other.wait()
+        own.wait()
+        sides = ((x1, 1 - sec), (x0, sec))
+        step = 7
+        size = step * side * 8
+
+        def outer_first(d_ref, lanes):
+            accp[:, lanes] = jnp.zeros((D, lanes.stop - lanes.start), F32)
+            for src, which in sides:
+
+                def body(i, src=src, which=which):
+                    at = pl.ds(pl.multiple_of(i * size, 16), size)
+                    d = d_ref[which, pl.ds(i * step, step)].reshape(size, d_ref.shape[-1])
+                    accp[:, lanes] += dot_tn(src[at], d)
+
+                loop(side // step, body)
+
+        outer_first(dz1, slice(0, 384))
+        a2.point(8)
+        exchange_finish(loc, buf, ss8, rs8, sums8, INNER)
+
+        def dz(y):
+            for t in range(2):
+                put_halves(dzi, y, 128 * t, inner_dz(clips, t, zin[y], din[y], st1, sums8, count))
+
+        loop(side, dz)
+        a1.point(3)
+        outer_first(dzi, slice(384, 640))
+        for t in range(5):
+            p1b[t, 0:D] = accp[:, 128 * t : 128 * t + 128].astype(BF16)
+        b1.point(0)
+        b2.point(8)
+        sent = []
+        ticks = (
+            lambda: (a1.point(4), b1.point(1)),
+            lambda: (a1.point(5), b1.point(2)),
+            lambda: (b1.point(3),),
+            lambda: (a1.point(6), b1.point(4)),
+        )
+        for p in range(4):
+            src, which = sides[p // 2]
+            i = p % 2
+            slot = p % 2
+            here = pl.ds(i * step, step)
+            if p >= 2:
+                sent[p - 2].wait()
+            d = jnp.concatenate([dz1[which, here], dzi[which, here]], -1).reshape(size, 640)
+            ring[slot] = dot_nt(d, wp[...]).astype(BF16)
+            to = gin.at[sec, i * size : (i + 1) * size]
+            if p < 2:
+                c = swap_copy(ring.at[slot], to, gsend.at[i], grecv.at[i])
+            else:
+                c = pltpu.make_async_copy(ring.at[slot], to, sems.at[2 + i])
+            c.start()
+            sent.append(c)
+            ticks[p]()
+        sent[2].wait()
+        sent[3].wait()
+
+    dma = pltpu.SemaphoreType.DMA
+    pl.run_scoped(
+        last_phase,
+        vmem(side, rows, 256),
+        vmem(side * side * 8, D, dtype=BF16),
+        vmem(side * side * 8, D, dtype=BF16),
+        vmem(2, 7 * side * 8, D, dtype=BF16),
+        vmem(D, 640),
+        dma((4,)),
+    )
+    snd[:, 0:DP] = jnp.where(sec == 0, sums5[...], sums7[...])
+    snd[:, DP : DP + 640] = jnp.where(sec == 0, sums6[...], sums8[...])
+    small = swap_copy(snd, got, csend.at[6], crecv.at[6])
+    small.start()
+    b1.point(5)
+    a1.point(7)
+    b1.point(6)
+    a2.flush()
+    b2.flush()
+    a1.point(8)
+    b1.point(7)
+    b1.point(8)
+    a1.flush()
+    b1.flush()
+
+    def finish(mine, theirs):
+        copies = []
+        for i, (full, m, t) in enumerate(((full_a, mine[0], theirs[0]), (full_b, mine[1], theirs[1]))):
+            copies.append(pltpu.make_async_copy(m, full.at[sec], lsem.at[6 + i]))
+            copies.append(swap_copy(t, full.at[sec], csend.at[4 + i], crecv.at[4 + i]))
+        for c in copies:
+            c.start()
+        for c in copies:
+            c.wait()
+
+    ones = (part(p1a, ha, sec), part(p1b, hb, sec))
+    twos = (q2a, q2b)
+    pl.when(sec == 0)(lambda: finish(ones, twos))
+    pl.when(sec == 1)(lambda: finish(twos, ones))
+    small.wait()
+    for lanes, a, b in ((slice(0, DP), sums7, sums5), (slice(DP, DP + 640), sums8, sums6)):
+        offs[:, lanes] = jnp.where(sec == 0, a[...], b[...]) + got[:, lanes]
+
+
+def put_halves(ref, y, lane, v):
+    side, lanes = v.shape[0] // 16, v.shape[1]
+    v = v.reshape(side, 2, 8, lanes)
+    for h in range(2):
+        ref[h, y, :, lane : lane + lanes] = v[:, h].reshape(side * 8, lanes).astype(BF16)
 
 
 class Reducer:
-    def __init__(self, q, land, ssem, rsem, ready, order, base):
-        self.q, self.land, self.ssem, self.rsem, self.ready = q, land, ssem, rsem, ready
-        self.order, self.base = order, base
+    POINTS = 9
+
+    def __init__(
+        self, bits, index, q, base, rows, swap_src, core_land, land, csend, crecv, ssem, rsem, ready, flip, load
+    ):
+        self.bits, self.index, self.q, self.base, self.rows = bits, index, q, base, rows
+        self.core_land, self.land, self.load = core_land, land, load
+        self.ssem, self.rsem, self.ready = ssem, rsem, ready
+        self.swap = swap_copy(swap_src, core_land, csend.at[index], crecv.at[index])
         me = lax.axis_index("dp")
+        plain, swapped = orders(bits)
         self.steps = []
-        tiles, rows = q.shape[0], q.shape[1]
-        t0, r0 = 0, 0
-        for i, k in enumerate(order):
-            bit = bit_of(me, k)
-            partner = me + (1 - 2 * bit) * (1 << k)
+        tiles, t0, r0 = 8, 0, base
+        for k, j in zip(plain, swapped):
+            power = (1 << k) + flip * ((1 << j) - (1 << k))
+            bit = lax.rem(me // power, 2)
+            partner = me + (1 - 2 * bit) * power
             if tiles > 1:
                 tiles //= 2
                 keep, send = (t0 + bit * tiles, r0), (t0 + (1 - bit) * tiles, r0)
@@ -1051,6 +1222,7 @@
                 keep, send = (t0, r0 + bit * rows), (t0, r0 + (1 - bit) * rows)
             t0, r0 = keep
             self.steps.append((partner, keep, send, tiles, rows))
+        self.last = 2 * bits
 
     def region(self, at, tiles, rows):
         t, r = at
@@ -1058,24 +1230,27 @@
             r = pl.multiple_of(r, 16)
         return self.q.at[pl.ds(t, tiles), pl.ds(r, rows)]
 
-    def copy(self, src, dst, sem, partner):
+    def copy(self, i):
+        if i == 0:
+            return self.swap
+        halving = i <= self.bits
+        partner, keep, send, tiles, rows = self.steps[i - 1 if halving else self.last - i]
+        src = self.region(send if halving else keep, tiles, rows)
+        sem = self.index * (self.last + 1) + i
         return pltpu.make_async_remote_copy(
             src_ref=src,
-            dst_ref=dst,
-            send_sem=self.ssem.at[self.base + sem],
-            recv_sem=self.rsem.at[self.base + sem],
+            dst_ref=self.land[i - 1] if halving else src,
+            send_sem=self.ssem.at[sem],
+            recv_sem=self.rsem.at[sem],
             device_id={"dp": partner},
             device_id_type=MESH,
         )
 
-    def halve(self, i):
-        partner, keep, send, tiles, rows = self.steps[i]
-        return self.copy(self.region(send, tiles, rows), self.land[i], i, partner)
-
-    def add(self, i):
-        partner, keep, send, tiles, rows = self.steps[i]
-        q, land = self.region(keep, tiles, rows), self.land[i]
-        chunk = 96 if rows % 96 == 0 else 16
+    def free(self, i):
+        return self.ready.at[self.index * self.bits + i]
+
+    def add(self, q, land, tiles, rows):
+        chunk = next(c for c in range(min(rows, 416), 0, -16) if rows % c == 0 and c % 16 == 0)
         parts = rows // chunk
 
         def body(j):
@@ -1085,21 +1260,33 @@
 
         loop(tiles * parts, body)
 
-    def free(self, i):
-        pl.semaphore_signal(
-            self.ready.at[self.base // 2 + i],
-            inc=1,
-            device_id={"dp": self.steps[i][0]},
-            device_id_type=MESH,
-        )
-
-    def await_free(self, i):
-        pl.semaphore_wait(self.ready.at[self.base // 2 + i], 1)
-
-    def double(self, i):
-        partner, keep, send, tiles, rows = self.steps[i]
-        q = self.region(keep, tiles, rows)
-        return self.copy(q, q, len(self.steps) + i, partner)
+    def start(self, i):
+        if i > self.bits:
+            pl.semaphore_wait(self.free(self.last - i), 1)
+        self.copy(i).start()
+
+    def finish(self, i):
+        self.copy(i).wait()
+        if i == 0:
+            if self.load is not None:
+                self.load.wait()
+            self.add(self.region((0, self.base), 8, self.rows), self.core_land, 8, self.rows)
+        elif i <= self.bits:
+            partner, keep, send, tiles, rows = self.steps[i - 1]
+            pl.semaphore_signal(
+                self.free(i - 1), inc=1, device_id={"dp": partner}, device_id_type=MESH
+            )
+            self.add(self.region(keep, tiles, rows), self.land[i - 1], tiles, rows)
+
+    def point(self, p):
+        count = self.last + 1
+        for i in range(p * count // self.POINTS, (p + 1) * count // self.POINTS):
+            if i > 0:
+                self.finish(i - 1)
+            self.start(i)
+
+    def flush(self):
+        self.finish(self.last)
 
 
 def land_shapes(tiles, rows, bits):
@@ -1121,104 +1308,16 @@
     return plain, swapped
 
 
-def reduce_kernel(bits, packed1, packed2, s5, s6, s7, s8, full, offs, *scratch):
-    n = bits
-    q = scratch[0:2]
-    core_land = scratch[2:4]
-    land = (scratch[4 : 4 + n], scratch[4 + n : 4 + 2 * n])
-    sums, sums_got, csend, crecv, ssem, rsem, lsem, ready = scratch[4 + 2 * n :]
-    sec = lax.axis_index("section")
-    me = lax.axis_index("dp")
-    barrier = pltpu.get_barrier_semaphore()
-    greet_core()
-    for k in range(n):
-        partner = me + (1 - 2 * bit_of(me, k)) * (1 << k)
-        pl.semaphore_signal(barrier, inc=1, device_id={"dp": partner}, device_id_type=MESH)
-    half = q[0].shape[1]
-    packed = (packed1, packed2)
-    mine = []
-    for b in range(2):
-        src = packed[b].at[:, pl.ds(pl.multiple_of(sec * half, 16), half)]
-        mine.append(pltpu.make_async_copy(src, q[b], lsem.at[b]))
-        mine[b].start()
-    sums[:, 0:DP] = jnp.where(sec == 0, s5[...], s7[...])
-    sums[:, DP : DP + 640] = jnp.where(sec == 0, s6[...], s8[...])
-    pl.semaphore_wait(barrier, n + 1)
-    swaps = []
-    for b in range(2):
-        src = packed[b].at[:, pl.ds(pl.multiple_of((1 - sec) * half, 16), half)]
-        swaps.append(swap_copy(src, core_land[b], csend.at[b], crecv.at[b]))
-        swaps[b].start()
-    small = swap_copy(sums, sums_got, csend.at[2], crecv.at[2])
-    small.start()
-
-    def core_sum(b):
-        swaps[b].wait()
-        mine[b].wait()
-        chunk = 96 if half % 96 == 0 else 16
-        parts = half // chunk
-
-        def body(j):
-            t, r = j // parts, pl.multiple_of(lax.rem(j, parts) * chunk, 16)
-            at = pl.ds(r, chunk)
-            q[b][t, at] = (q[b][t, at].astype(F32) + core_land[b][t, at].astype(F32)).astype(BF16)
-
-        loop(8 * parts, body)
-
-    plain, swapped = orders(n)
-
-    def run(order1, order2):
-        red = [
-            Reducer(q[0], land[0], ssem, rsem, ready, order1, 0),
-            Reducer(q[1], land[1], ssem, rsem, ready, order2, 2 * n),
-        ]
-        lag = 2
-        flight = [None, None]
-        for step in range(2 * n + lag + 1):
-            for b in range(2):
-                i = step - lag * b
-                if i < 0 or i > 2 * n:
-                    continue
-                if i == 0:
-                    core_sum(b)
-                elif i <= n:
-                    flight[b].wait()
-                    red[b].free(i - 1)
-                    red[b].add(i - 1)
-                else:
-                    flight[b].wait()
-                if i < n:
-                    flight[b] = red[b].halve(i)
-                elif i < 2 * n:
-                    red[b].await_free(2 * n - 1 - i)
-                    flight[b] = red[b].double(2 * n - 1 - i)
-                if i < 2 * n:
-                    flight[b].start()
-
-    pl.when(sec == 0)(lambda: run(plain, swapped))
-    pl.when(sec == 1)(lambda: run(swapped, plain))
-
-    def finish(b):
-        keep = pltpu.make_async_copy(q[b], full.at[sec], lsem.at[2])
-        keep.start()
-        last = swap_copy(q[1 - b], full.at[sec], csend.at[3], crecv.at[3])
-        last.start()
-        keep.wait()
-        last.wait()
-
-    pl.when(sec == 0)(lambda: finish(0))
-    pl.when(sec == 1)(lambda: finish(1))
-    small.wait()
-    for lanes, a, b in ((slice(0, DP), s7, s5), (slice(DP, DP + 640), s8, s6)):
-        offs[:, lanes] = jnp.where(sec == 0, a[...], b[...]) + sums_got[:, lanes]
-
-
-def unpack_kernel(full, offs, one, mid_in, mid, small_in, small, pool, offset, buf, nat, sem):
-    half = full.shape[2]
-    copies = [
-        pltpu.make_async_copy(full.at[h], buf.at[:, h * half : (h + 1) * half], sem.at[h])
-        for h in range(2)
-    ]
+def unpack_kernel(
+    full_a, full_b, offs, one, mid_in, mid, small_in, small, pool, offset, buf_a, buf_b, nat, sem
+):
+    copies = []
+    for i, (full, buf) in enumerate(((full_a, buf_a), (full_b, buf_b))):
+        half = full.shape[2]
+        for h in range(2):
+            copies.append(
+                pltpu.make_async_copy(full.at[h], buf.at[:, h * half : (h + 1) * half], sem.at[2 * i + h])
+            )
     for c in copies:
         c.start()
     v = offs[...]
@@ -1231,7 +1330,9 @@
         c.wait()
 
     def take(t, r, rows):
-        return buf[t, r : r + rows].astype(F32)
+        if r < 1440:
+            return buf_a[t, r : r + rows].astype(F32)
+        return buf_b[t, r - 1440 : r - 1440 + rows].astype(F32)
 
     for dt in range(3):
         for dy in range(3):
@@ -1307,7 +1408,7 @@
     rows2 = side2 * 8
     total2 = side2 * rows2
     unit = 32 << max(bits - 3, 0)
-    packed_rows = -(-(1440 + D) // unit) * unit
+    rows_a, rows_b = -(-1440 // unit) * unit, -(-D // unit) * unit
     x = clip_input.transpose(0, 2, 3, 1, 4).reshape(2, side * side * half, D)
     og = out_grad.transpose(0, 2, 3, 1, 4)
 
@@ -1348,7 +1449,7 @@
             vmem(*grid, 128),
             vmem(side + 2, rows, 128),
         ]
-        + [like(w) for w in weights] * 2
+        + [like(w) for w in weights]
         + [
             vmem(1, 1152),
             vmem(1, 1152),
@@ -1359,8 +1460,8 @@
             vmem(2, 2, 8, 640),
             vmem(2, 16, 640),
         ]
-        + exchange_scratch(n, 640)
-        + [dma((7,)), dma((10,)), dma((9,)), dma((9,))],
+        + exchange_scratch(n, 16)
+        + [dma((7,)), dma((10,)), dma((6,)), dma((6,))],
         collective=1,
         any_in=range(1, 9),
         any_out=(0, 1, 2, 3, 5, 6, 7, 8, 9, 10, 13),
@@ -1376,7 +1477,7 @@
             ((8, DP), F32),
         ],
         (clip_lengths, zin, zone, zp, st1, beta1, wf1, ws1),
-        [vmem(8, 512), vmem(2, 16, 512)] + exchange_scratch(n, 512),
+        [vmem(8, 512), vmem(2, 16, 512)] + exchange_scratch(n, 8),
         collective=2,
     )
     sig, hand, asum, bsum = call(
@@ -1385,12 +1486,13 @@
         (clip_lengths, zf, stf, beta1),
         [vmem(side2, 16, 128)],
     )
-    block_output, hg, packed2, sums5, sums6, sums7 = call(
+    block_output, hg, packed2a, packed2b, sums5, sums6, sums7 = call(
         second_kernel,
         [
             (og.shape, BF16),
             ((side2, side2, 8, DP), F32),
-            ((8, packed_rows, 128), BF16),
+            ((8, rows_a, 128), BF16),
+            ((8, rows_b, 128), BF16),
             ((8, DP), F32),
             ((8, 640), F32),
             ((8, DP), F32),
@@ -1428,64 +1530,58 @@
             vmem(384, 384),
             vmem(DP, 640),
         ]
-        + exchange_scratch(n, 640)
-        + exchange_scratch(n, 512)
-        + exchange_scratch(n, DP)
-        + exchange_scratch(n, 640)
-        + exchange_scratch(n, DP),
+        + exchange_scratch(n, 16)
+        + exchange_scratch(n, 8)
+        + exchange_scratch(n, 16)
+        + exchange_scratch(n, 8)
+        + exchange_scratch(n, 16),
         collective=3,
         any_in=(4,),
         any_out=(0,),
     )
-    dzc, dzs, dz1 = call(
-        dz_kernel,
+    ha, hb = rows_a // 2, rows_b // 2
+
+    def bf(*shape):
+        return vmem(*shape, dtype=BF16)
+
+    lands = []
+    for h in (ha, hb, ha, hb):
+        lands += [bf(*shape) for shape in land_shapes(8, h, bits)]
+    steps = 4 * (2 * bits + 1)
+    gin, full_a, full_b, offs = call(
+        functools.partial(backward_kernel, bits),
         [
-            ((side + 2, rows, 1024), BF16),
-            ((side + 2, rows, 384), BF16),
-            ((2, side, rows // 2, 384), BF16),
+            (x.shape, BF16),
+            ((2, 8, ha, 128), BF16),
+            ((2, 8, hb, 128), BF16),
+            ((8, DP + 640), F32),
         ],
-        (clip_lengths, zf, sig, hg, stf, sums7),
-        [vmem(side2, 16, 128), vmem(side, rows, 128), vmem(side + 2, rows, 128)],
-    )
-    packed1 = call(
-        conv_grad_kernel,
-        [((8, packed_rows, 128), BF16)],
-        (cat, scat, dzc, dzs, beta1),
-        [vmem(1536, 1024), vmem(384, 384)],
-        smem_first=False,
-    )[0]
-    dzi, sums8 = call(
-        conv_back_kernel,
-        [((2, side, rows // 2, 256), BF16), ((8, 640), F32)],
-        (clip_lengths, dzc, dzs, wf1, ws1, zin, st1, beta1),
-        [vmem(side, rows, 256), vmem(2, 16, 640)] + exchange_scratch(n, 640),
+        (clip_lengths, hg, stf, sums7, st1, beta1, sums5, sums6)
+        + (zf, sig, zin, wf1, ws1, wp1, cat, scat, x, xgot, packed2a, packed2b),
+        [
+            vmem(side, rows, 256),
+            bf(1536, 1024),
+            bf(384, 384),
+            bf(D, 640),
+            bf(side + 2, rows, 1024),
+            bf(side + 2, rows, 384),
+            bf(2, side, rows // 2, 384),
+            bf(2, side, rows // 2, 256),
+            vmem(8, 640),
+            vmem(8, DP + 640),
+            vmem(8, DP + 640),
+            bf(8, rows_a, 128),
+            bf(8, rows_b, 128),
+        ]
+        + [bf(8, h, 128) for h in (ha, hb) * 3]
+        + [vmem(2, 16, 640)]
+        + exchange_scratch(n, 8)
+        + [dma((8,)), dma((7,)), dma((7,)), dma((steps,)), dma((steps,)), dma((2,)), dma((2,))]
+        + [pltpu.SemaphoreType.REGULAR((4 * bits,))]
+        + lands,
         collective=4,
-    )
-    gin, packed1 = call(
-        input_kernel,
-        [(x.shape, BF16), ((8, packed_rows, 128), BF16)],
-        (x, xgot, dz1, dzi, wp1, packed1),
-        [like(x), like(x), like(x), vmem(D, 640), dma((2,)), dma(()), dma(())],
-        smem_first=False,
-        collective=5,
-        any_in=(0, 5),
-        any_out=(0,),
-    )
-    half_rows = packed_rows // 2
-    lands = [vmem(*shape, dtype=BF16) for shape in land_shapes(8, half_rows, bits)]
-    full, offs = call(
-        functools.partial(reduce_kernel, bits),
-        [((2, 8, half_rows, 128), BF16), ((8, DP + 640), F32)],
-        (packed1, packed2, sums5, sums6, sums7, sums8),
-        [vmem(8, half_rows, 128, dtype=BF16)] * 4
-        + lands * 2
-        + [vmem(8, DP + 640)] * 2
-        + [dma((4,)), dma((4,)), dma((4 * bits,)), dma((4 * bits,)), dma((3,))]
-        + [pltpu.SemaphoreType.REGULAR((2 * bits,))],
-        smem_first=False,
-        collective=6,
-        any_in=(0, 1),
-        any_out=(0,),
+        any_in=range(8, 20),
+        any_out=(0, 1, 2),
     )
     one, mid_in, mid, small_in, small, pool, offset = call(
         unpack_kernel,
@@ -1498,10 +1594,10 @@
             ((D, C3), F32),
             ((1, 1024), F32),
         ],
-        (full, offs),
-        [vmem(8, packed_rows, 128, dtype=BF16), vmem(27 * C1A, 384), dma((2,))],
+        (full_a, full_b, offs),
+        [bf(8, rows_a, 128), bf(8, rows_b, 128), vmem(27 * C1A, 384), dma((4,))],
         smem_first=False,
-        any_in=(0,),
+        any_in=(0, 1),
     )
     input_grad = gin.reshape(2, side, side, half, D).transpose(0, 3, 1, 2, 4)
     return (

time: 399 us -> 280 us (0.70)
  Pallas kernels: 392 us -> 273 us
    pallas_call x10 -> x6, Pallas kernels: 392 us -> 273 us  [call(): pl.pallas_call(kernel, out_shape=[jax.ShapeDtypeStruct(shape, dtype) for...]
where the time goes in v3:
time: 280 us
  Pallas kernels  273 us (98%)
  local copies, waits for them, and re-layouts  6.38 us (2%)
    pallas_call x6, Pallas kernels, call(): pl.pallas_call(kernel, out_shape=[jax.ShapeDtypeStruct(shape, dtype) for...  273 us
    unnamed x4, local copies, waits for them, and re-layouts  6.38 us

profile of v3, /device:TPU:0, one launch (start us, length us, event | category | flops | bytes accessed | tf_op | source)
XLA Modules:
  0.0 279.7 jit_solution(12178988665517711541)
XLA Ops:
  0.6 25.7 %shard_map.169 = (bf16[1568,832]{1,0:T(8,128)(2,1)}, f32[14,14,2,8,256]{4,3,2,1,0:T(8,128)}, f32[14,14,2,8,256]{4,3,2,1,0:T(8,128)}, f32[14,224,128]{2,1,0:T(8,1...) custom-call(s32[2,2]{1,0:T(2,128)} %len_ref.9, ...), custom_call_target="tpu_custom_call" | custom-call | tf_op jit(solution)/shard_map/pallas_call | solution.py:1390
  26.4 34.0 %shard_map.170 = (bf16[16,224,512]{2,1,0:T(8,128)(2,1)}, bf16[16,224,128]{2,1,0:T(8,128)(2,1)}, f32[14,224,896]{2,1,0:T(8,128)}, f32[8,896]{1,0:T(8,128)}) custom-call(s32[2,2]{1,0:T(2,128)} %len_ref.9, f32[14,224,256]{2,1,0:T(8,128)} %bitcast.27, f32[14,224,256]{2,1,0:T(8,128)} %bitcast.30, f32[14,224,128]{2,1,0:T(8,128)} %get-tuple-element.51.zp, ...), custom_call_target="tpu_custom_call" | custom-call | tf_op jit(solution)/shard_map/pallas_call | solution.py:1390
  60.4 19.3 %shard_map.171 = (bf16[14,224,896]{2,1,0:T(8,128)(2,1)}, f32[7,7,8,896]{3,2,1,0:T(8,128)}, f32[7,7,8,896]{3,2,1,0:T(8,128)}, f32[7,7,8,896]{3,2,1,0:T(8,128)}) custom-call(s32[2,2]{1,0:T(2,128)} %len_ref.9, f32[14,224,896]{2,1,0:T(8,128)} %get-tuple-element.56.zf, f32[8,896]{1,0:T(8,128)} %get-tuple-element.57.stf, f32[1,1152]{1,0:T(1,128)} %get-tuple-element.53.beta.beta1), custom_call_target="tpu_custom_call" | custom-call | tf_op jit(solution)/shard_map/pallas_call | solution.py:1390
  79.7 45.4 %shard_map.172 = (bf16[2,7,7,4,832]{4,3,2,1,0:T(4,128)(2,1)}, f32[7,7,8,896]{3,2,1,0:T(8,128)}, bf16[8,1472,128]{2,1,0:T(8,128)(2,1)}, bf16[8,832,128]{2,1,0:T(8...) custom-call(s32[2,2]{1,0:T(2,128)} %len_ref.9, f32[7,7,8,896]{3,2,1,0:T(8,128)} %get-tuple-element.58.hand, ...), custom_call_target="tpu_custom_call" | custom-call | tf_op jit(solution)/shard_map/pallas_call | solution.py:1390
  125.1 137.2 %shard_map.173 = (bf16[2,1568,832]{2,1,0:T(8,128)(2,1)}, bf16[2,8,736,128]{3,2,1,0:T(8,128)(2,1)}, bf16[2,8,416,128]{3,2,1,0:T(8,128)(2,1)}, f32[8,1536]{1,0:T(8,128)}) custom-call(s32[2,2]{1,0:T(2,128)} %len_ref.9, f32[7,7,8,896]{3,2,1,0:T(8,128)} %get-tuple-element.67.hg, f32[8,896]{1,0:T(8,128)} %get-tuple-element.57.stf, ...), custom_call_target="tpu_custom_call" | custom-call | tf_op jit(solution)/shard_map/pallas_call | solution.py:1390
  262.3 0.0 copy-start
  262.3 11.0 %shard_map.174 = (f32[832,256]{1,0:T(8,128)}, f32[160,832]{1,0:T(8,128)}, f32[320,4320]{1,0:T(8,128)}, f32[32,832]{1,0:T(8,128)}, f32[864,128]{1,0:T(8,128)}, /*index=5*/f32[832,128]{1,0:T(8,128)}, f32[1,1024]{1,0:T(1,128)}) custom-call(bf16[2,8,736,128]{3,2,1,0:T(8,128)(2,1)} %get-tuple-element.79.full_a, ...), custom_call_target="tpu_custom_call" | custom-call | tf_op jit(solution)/shard_map/pallas_call | solution.py:1390
  273.3 0.0 copy-done
  273.3 0.9 copy.21
  274.2 5.5 %copy.22 = bf16[2,8,14,14,832]{4,1,3,2,0:T(8,128)(2,1)} copy(bf16[2,8,14,14,832]{4,1,3,2,0:T(8,128)(2,1)} %bitcast.29) | data formatting | bytes 10436608
Async XLA Ops:
  262.3 11.1 %copy-start = (bf16[2,7,7,4,832]{4,3,2,1,0:T(4,128)(2,1)S(1)}, bf16[2,7,7,4,832]{4,3,2,1,0:T(4,128)(2,1)}, u32[]{:S(2)}) copy-start(bf16[2,7,7,4,832]{4,3,2,1,0:T(4,128)(2,1)} %get-tuple-element.66) | copy-start | bytes 1956868
